TPU v7x, 128 devices: a whole 4x4x4 slice. The times are simulated.
128 devices in a mesh: dp: 16 (over y, x), ctx: 8 (over z, core).
Axes of the slice: x: 4, y: 4, z: 4, core: 2. Of those that a mesh axis runs over, the one named last changes fastest.
Arguments:
- tokens: bfloat16 [16, 1024, 2048], P('dp', 'ctx'), may hold values from -6 to 6
- cotangent: bfloat16 [16, 1024, 2048], P('dp', 'ctx'), may hold values from -6 to 6
- w_query: float32 [2048, 2048], P('dp', 'ctx'), may hold values from -0.125 to 0.125
- query_first: float32 [2048, 2048], P('dp', 'ctx'), may hold values from -80 to 80
- query_second: float32 [2048, 2048], P('dp', 'ctx'), may hold values from 868.352 to 3440.64
- w_key: float32 [2048, 256], P(('dp', 'ctx')), may hold values from -0.125 to 0.125
- key_first: float32 [2048, 256], P(('dp', 'ctx')), may hold values from -256 to 256
- key_second: float32 [2048, 256], P(('dp', 'ctx')), may hold values from 6946.816 to 27525.12
- w_value: float32 [2048, 256], P(('dp', 'ctx')), may hold values from -0.125 to 0.125
- value_first: float32 [2048, 256], P(('dp', 'ctx')), may hold values from -256 to 256
- value_second: float32 [2048, 256], P(('dp', 'ctx')), may hold values from 6946.816 to 27525.12
- w_out: float32 [2048, 2048], P('ctx', 'dp'), may hold values from -1 to 1
- out_first: float32 [2048, 2048], P('ctx', 'dp'), may hold values from -4 to 4
- out_second: float32 [2048, 2048], P('ctx', 'dp'), may hold values from 1.696 to 6.72
- w_gate: float32 [2048, 5632], P('dp', 'ctx'), may hold values from -0.125 to 0.125
- gate_first: float32 [2048, 5632], P('dp', 'ctx'), may hold values from -40 to 40
- gate_second: float32 [2048, 5632], P('dp', 'ctx'), may hold values from 212.992 to 868.352
- w_up: float32 [2048, 5632], P('dp', 'ctx'), may hold values from -0.125 to 0.125
- up_first: float32 [2048, 5632], P('dp', 'ctx'), may hold values from -40 to 40
- up_second: float32 [2048, 5632], P('dp', 'ctx'), may hold values from 212.992 to 868.352
- w_down: float32 [5632, 2048], P('ctx', 'dp'), may hold values from -0.078125 to 0.078125
- down_first: float32 [5632, 2048], P('ctx', 'dp'), may hold values from -40 to 40
- down_second: float32 [5632, 2048], P('ctx', 'dp'), may hold values from 212.992 to 868.352
- norm_gains: float32 [2, 2048], P(None, ('dp', 'ctx')), may hold values from 0.5 to 1.5
- gains_first: float32 [2, 2048], P(None, ('dp', 'ctx')), may hold values from -80 to 80
- gains_second: float32 [2, 2048], P(None, ('dp', 'ctx')), may hold values from 868.352 to 3440.64
Outputs:
- output: bfloat16 [16, 1024, 2048], P('dp', 'ctx')
- input_grad: bfloat16 [16, 1024, 2048], P('dp', 'ctx')
- query_new: float32 [2048, 2048], P('dp', 'ctx')
- query_first_new: float32 [2048, 2048], P('dp', 'ctx')
- query_second_new: float32 [2048, 2048], P('dp', 'ctx')
- key_new: float32 [2048, 256], P(('dp', 'ctx'))
- key_first_new: float32 [2048, 256], P(('dp', 'ctx'))
- key_second_new: float32 [2048, 256], P(('dp', 'ctx'))
- value_new: float32 [2048, 256], P(('dp', 'ctx'))
- value_first_new: float32 [2048, 256], P(('dp', 'ctx'))
- value_second_new: float32 [2048, 256], P(('dp', 'ctx'))
- out_new: float32 [2048, 2048], P('ctx', 'dp')
- out_first_new: float32 [2048, 2048], P('ctx', 'dp')
- out_second_new: float32 [2048, 2048], P('ctx', 'dp')
- gate_new: float32 [2048, 5632], P('dp', 'ctx')
- gate_first_new: float32 [2048, 5632], P('dp', 'ctx')
- gate_second_new: float32 [2048, 5632], P('dp', 'ctx')
- up_new: float32 [2048, 5632], P('dp', 'ctx')
- up_first_new: float32 [2048, 5632], P('dp', 'ctx')
- up_second_new: float32 [2048, 5632], P('dp', 'ctx')
- down_new: float32 [5632, 2048], P('ctx', 'dp')
- down_first_new: float32 [5632, 2048], P('ctx', 'dp')
- down_second_new: float32 [5632, 2048], P('ctx', 'dp')
- gains_new: float32 [2, 2048], P(None, ('dp', 'ctx'))
- gains_first_new: float32 [2, 2048], P(None, ('dp', 'ctx'))
- gains_second_new: float32 [2, 2048], P(None, ('dp', 'ctx'))
All inputs are finite; a program needn't handle non-finite values.
Results may differ from a plain program's by a relative error of at most 0.025.
Values may be sent and summed in bfloat16 or wider, within the bound.
No kernel may reach another device: no remote copies, remote signals or barrier semaphores. Data moves between devices by JAX's collectives and lax.ppermute only.
A program may use at most 128 MiB of HBM per device.

v0:
```python
import jax
import jax.numpy as jnp
from jax import lax
from jax.sharding import PartitionSpec as P

D = 2048
HEADS = 32
KV_HEADS = 4
HD = 64
FF = 5632
SEQ_LEN = 1024
STEP = 10


EPS = 1e-05
BETA_ONE = 0.9
BETA_TWO = 0.95
ADAM_EPS = 1e-08
DECAY = 0.1


def tables(positions):
    half_width = HD // 2
    frequency = 10000.0 ** (-2.0 * jnp.arange(half_width).astype(jnp.float32) / HD)
    angles = positions.astype(jnp.float32)[:, None] * frequency[None, :]
    return (jnp.cos(angles)[:, None, :], jnp.sin(angles)[:, None, :])


def rotate(inputs, cos_table, sine_table):
    half_width = inputs.shape[-1] // 2
    first_half = inputs[..., :half_width]
    second_half = inputs[..., half_width:]
    return jnp.concatenate(
        [
            first_half * cos_table - second_half * sine_table,
            second_half * cos_table + first_half * sine_table,
        ],
        axis=-1,
    )


def rotate_back(inputs, cos_table, sine_table):
    half_width = inputs.shape[-1] // 2
    first_half = inputs[..., :half_width]
    second_half = inputs[..., half_width:]
    return jnp.concatenate(
        [
            first_half * cos_table + second_half * sine_table,
            second_half * cos_table - first_half * sine_table,
        ],
        axis=-1,
    )


def product(left, right):
    return jnp.dot(left, right, preferred_element_type=jnp.float32)


def contract_rows(left, right):
    return lax.dot_general(
        left, right, (((0,), (0,)), ((), ())), preferred_element_type=jnp.float32
    )


def contract_cols(left, right):
    return lax.dot_general(
        left, right, (((1,), (1,)), ((), ())), preferred_element_type=jnp.float32
    )


def adamw_step(weight, first, second, gradient, rate, decay):
    first_new = BETA_ONE * first + (1.0 - BETA_ONE) * gradient
    second_new = BETA_TWO * second + (1.0 - BETA_TWO) * gradient * gradient
    first_hat = first_new / (1.0 - BETA_ONE**STEP)
    second_hat = second_new / (1.0 - BETA_TWO**STEP)
    weight_new = weight - rate * (first_hat / (jnp.sqrt(second_hat) + ADAM_EPS) + decay * weight)
    return (weight_new, first_new, second_new)


def shards(
    tokens,
    cotangent,
    w_query,
    query_first,
    query_second,
    w_key,
    key_first,
    key_second,
    w_value,
    value_first,
    value_second,
    w_out,
    out_first,
    out_second,
    w_gate,
    gate_first,
    gate_second,
    w_up,
    up_first,
    up_second,
    w_down,
    down_first,
    down_second,
    norm_gains,
    gains_first,
    gains_second,
):
    inputs = tokens[0].astype(jnp.float32)
    row_count = inputs.shape[0]
    ctx_count = lax.axis_size("ctx")
    ctx_index = lax.axis_index("ctx")
    head_count = HEADS // ctx_count
    share = ctx_count // KV_HEADS
    kv_index = ctx_index // share
    scale_factor = HD ** (-0.5)
    wide_key, wide_value, full_gains = (
        lax.all_gather(w_key.astype(jnp.bfloat16), ("dp", "ctx"), axis=0, tiled=True),
        lax.all_gather(w_value.astype(jnp.bfloat16), ("dp", "ctx"), axis=0, tiled=True),
        lax.all_gather(norm_gains.astype(jnp.bfloat16), ("dp", "ctx"), axis=1, tiled=True),
    )
    gain_rows = full_gains.astype(jnp.float32)
    col_query, col_out, col_gate, col_up, col_down = (
        lax.all_gather(w_query.astype(jnp.bfloat16), "dp", axis=0, tiled=True),
        lax.all_gather(w_out.astype(jnp.bfloat16), "dp", axis=1, tiled=True),
        lax.all_gather(w_gate.astype(jnp.bfloat16), "dp", axis=0, tiled=True),
        lax.all_gather(w_up.astype(jnp.bfloat16), "dp", axis=0, tiled=True),
        lax.all_gather(w_down.astype(jnp.bfloat16), "dp", axis=1, tiled=True),
    )
    inv_first = lax.rsqrt(jnp.mean(inputs * inputs, axis=-1, keepdims=True) + EPS)
    unit_first = inputs * inv_first
    normed_in = (unit_first * gain_rows[0]).astype(jnp.bfloat16)
    normed_all, grad_all = (
        lax.all_gather(normed_in, "ctx", axis=0, tiled=True),
        lax.all_gather(cotangent[0], "ctx", axis=0, tiled=True),
    )
    total_len = normed_all.shape[0]
    cos_table, sine_table = tables(jnp.arange(total_len))
    local_cos, local_sine = tables(ctx_index * row_count + jnp.arange(row_count))
    key_cols = lax.dynamic_slice_in_dim(wide_key, kv_index * HD, HD, 1)
    value_cols = lax.dynamic_slice_in_dim(wide_value, kv_index * HD, HD, 1)
    query_proj = product(normed_all, col_query).reshape(total_len, head_count, HD)
    key_proj = product(normed_all, key_cols)
    value_head = product(normed_all, value_cols).astype(jnp.bfloat16)
    query_rot = rotate(query_proj, cos_table, sine_table).astype(jnp.bfloat16)
    key_rot = rotate(key_proj[:, None, :], cos_table, sine_table)[:, 0, :].astype(jnp.bfloat16)
    visible = jnp.arange(total_len)[:, None] >= jnp.arange(total_len)[None, :]
    query_stack = query_rot.transpose(1, 0, 2)

    def head_scores(query_head):
        scores = contract_cols(query_head, key_rot) * scale_factor
        return jnp.where(visible, scores, -1e30)

    def head_forward(query_head):
        scores = head_scores(query_head)
        row_max = jnp.max(scores, axis=-1, keepdims=True)
        exponent = jnp.exp(scores - row_max)
        total = jnp.sum(exponent, axis=-1, keepdims=True)
        probabilities = (exponent / total).astype(jnp.bfloat16)
        return (product(probabilities, value_head), row_max[:, 0] + jnp.log(total[:, 0]))

    attended, log_total = lax.map(head_forward, query_stack)
    mixed_rows = (
        attended.transpose(1, 0, 2).reshape(total_len, head_count * HD).astype(jnp.bfloat16)
    )
    middle = inputs + lax.psum_scatter(
        product(mixed_rows, col_out).astype(jnp.bfloat16), "ctx", scatter_dimension=0, tiled=True
    ).astype(jnp.float32)
    inv_second = lax.rsqrt(jnp.mean(middle * middle, axis=-1, keepdims=True) + EPS)
    unit_second = middle * inv_second
    normed_mid = (unit_second * gain_rows[1]).astype(jnp.bfloat16)
    mid_all = lax.all_gather(normed_mid, "ctx", axis=0, tiled=True)
    gate_proj = product(mid_all, col_gate)
    up_proj = product(mid_all, col_up)
    sigma = jax.nn.sigmoid(gate_proj)
    swish = gate_proj * sigma
    hidden = (swish * up_proj).astype(jnp.bfloat16)
    output = middle + lax.psum_scatter(
        product(hidden, col_down).astype(jnp.bfloat16), "ctx", scatter_dimension=0, tiled=True
    ).astype(jnp.float32)
    out_grad = cotangent[0].astype(jnp.float32)
    back_query, back_out, back_gate, back_up, back_down = (
        lax.all_gather(w_query.astype(jnp.bfloat16), "dp", axis=0, tiled=True),
        lax.all_gather(w_out.astype(jnp.bfloat16), "dp", axis=1, tiled=True),
        lax.all_gather(w_gate.astype(jnp.bfloat16), "dp", axis=0, tiled=True),
        lax.all_gather(w_up.astype(jnp.bfloat16), "dp", axis=0, tiled=True),
        lax.all_gather(w_down.astype(jnp.bfloat16), "dp", axis=1, tiled=True),
    )
    hidden_grad = contract_cols(grad_all, back_down)
    down_wgrad = contract_rows(hidden, grad_all)
    gate_grad = (hidden_grad * up_proj * sigma * (1.0 + gate_proj * (1.0 - sigma))).astype(
        jnp.bfloat16
    )
    up_grad = (hidden_grad * swish).astype(jnp.bfloat16)
    gate_wgrad = contract_rows(mid_all, gate_grad)
    up_wgrad = contract_rows(mid_all, up_grad)
    mid_ngrad = lax.psum_scatter(
        (contract_cols(gate_grad, back_gate) + contract_cols(up_grad, back_up)).astype(
            jnp.bfloat16
        ),
        "ctx",
        scatter_dimension=0,
        tiled=True,
    ).astype(jnp.float32)
    gain_two_grad = jnp.sum(mid_ngrad * unit_second, axis=0)
    unit_mid_grad = mid_ngrad * gain_rows[1]
    middle_grad = out_grad + inv_second * (
        unit_mid_grad - unit_second * jnp.mean(unit_mid_grad * unit_second, axis=-1, keepdims=True)
    )
    middle_low = middle_grad.astype(jnp.bfloat16)
    mid_grad_all = lax.all_gather(middle_low, "ctx", axis=0, tiled=True)
    out_wgrad = contract_rows(mixed_rows, mid_grad_all)
    mixed_grad = contract_cols(mid_grad_all, back_out).astype(jnp.bfloat16)
    grad_stack = mixed_grad.reshape(total_len, head_count, HD).transpose(1, 0, 2)

    def head_backward(operands):
        query_head, head_total, grad_head = operands
        scores = head_scores(query_head)
        probabilities = jnp.exp(scores - head_total[:, None])
        rounded = probabilities.astype(jnp.bfloat16)
        value_grad = contract_rows(rounded, grad_head)
        prob_grad = contract_cols(grad_head, value_head)
        score_grad = (
            probabilities * (prob_grad - jnp.sum(prob_grad * probabilities, axis=-1, keepdims=True))
        ).astype(jnp.bfloat16)
        query_grad = product(score_grad, key_rot) * scale_factor
        key_grad = contract_rows(score_grad, query_head) * scale_factor
        return (query_grad, key_grad, value_grad)

    query_grads, key_grads, value_grads = lax.map(
        head_backward, (query_stack, log_total, grad_stack)
    )
    key_pieces, value_pieces = (
        lax.all_to_all(
            jnp.sum(key_grads, axis=0)[None].astype(jnp.bfloat16),
            "ctx",
            split_axis=1,
            concat_axis=0,
            tiled=True,
        ).astype(jnp.float32),
        lax.all_to_all(
            jnp.sum(value_grads, axis=0)[None].astype(jnp.bfloat16),
            "ctx",
            split_axis=1,
            concat_axis=0,
            tiled=True,
        ).astype(jnp.float32),
    )
    key_mine = jnp.sum(key_pieces.reshape(KV_HEADS, share, row_count, HD), axis=1).transpose(
        1, 0, 2
    )
    value_mine = jnp.sum(value_pieces.reshape(KV_HEADS, share, row_count, HD), axis=1).transpose(
        1, 0, 2
    )
    key_low = (
        rotate_back(key_mine, local_cos, local_sine)
        .reshape(row_count, KV_HEADS * HD)
        .astype(jnp.bfloat16)
    )
    value_low = value_mine.reshape(row_count, KV_HEADS * HD).astype(jnp.bfloat16)
    query_low = (
        rotate_back(query_grads.transpose(1, 0, 2), cos_table, sine_table)
        .reshape(total_len, head_count * HD)
        .astype(jnp.bfloat16)
    )
    query_wgrad = contract_rows(normed_all, query_low)
    key_wgrad = contract_rows(normed_in, key_low)
    value_wgrad = contract_rows(normed_in, value_low)
    in_ngrad = lax.psum_scatter(
        contract_cols(query_low, back_query).astype(jnp.bfloat16),
        "ctx",
        scatter_dimension=0,
        tiled=True,
    ).astype(jnp.float32)
    in_ngrad = in_ngrad + contract_cols(key_low, wide_key) + contract_cols(value_low, wide_value)
    gain_one_grad = jnp.sum(in_ngrad * unit_first, axis=0)
    unit_in_grad = in_ngrad * gain_rows[0]
    input_grad = middle_grad + inv_first * (
        unit_in_grad - unit_first * jnp.mean(unit_in_grad * unit_first, axis=-1, keepdims=True)
    )
    gain_grads = jnp.stack([gain_one_grad, gain_two_grad])
    query_sum, out_sum, gate_sum, up_sum, down_sum = (
        lax.psum_scatter(
            query_wgrad.astype(jnp.bfloat16), "dp", scatter_dimension=0, tiled=True
        ).astype(jnp.float32),
        lax.psum_scatter(
            out_wgrad.astype(jnp.bfloat16), "dp", scatter_dimension=1, tiled=True
        ).astype(jnp.float32),
        lax.psum_scatter(
            gate_wgrad.astype(jnp.bfloat16), "dp", scatter_dimension=0, tiled=True
        ).astype(jnp.float32),
        lax.psum_scatter(
            up_wgrad.astype(jnp.bfloat16), "dp", scatter_dimension=0, tiled=True
        ).astype(jnp.float32),
        lax.psum_scatter(
            down_wgrad.astype(jnp.bfloat16), "dp", scatter_dimension=1, tiled=True
        ).astype(jnp.float32),
    )
    key_sum, value_sum, gains_sum = (
        lax.psum_scatter(key_wgrad, ("dp", "ctx"), scatter_dimension=0, tiled=True),
        lax.psum_scatter(value_wgrad, ("dp", "ctx"), scatter_dimension=0, tiled=True),
        lax.psum_scatter(gain_grads, ("dp", "ctx"), scatter_dimension=1, tiled=True),
    )
    wide_rate = 2.0 * D ** (-0.5)
    out_rate = 2.0 * max(1, 16 * D // SEQ_LEN) ** (-0.5)
    down_rate = 2.0 * FF ** (-0.5)
    query_new, query_first_new, query_second_new = adamw_step(
        w_query, query_first, query_second, query_sum, wide_rate, DECAY
    )
    key_new, key_first_new, key_second_new = adamw_step(
        w_key, key_first, key_second, key_sum, wide_rate, DECAY
    )
    value_new, value_first_new, value_second_new = adamw_step(
        w_value, value_first, value_second, value_sum, wide_rate, DECAY
    )
    out_new, out_first_new, out_second_new = adamw_step(
        w_out, out_first, out_second, out_sum, out_rate, DECAY
    )
    gate_new, gate_first_new, gate_second_new = adamw_step(
        w_gate, gate_first, gate_second, gate_sum, wide_rate, DECAY
    )
    up_new, up_first_new, up_second_new = adamw_step(
        w_up, up_first, up_second, up_sum, wide_rate, DECAY
    )
    down_new, down_first_new, down_second_new = adamw_step(
        w_down, down_first, down_second, down_sum, down_rate, DECAY
    )
    gains_new, gains_first_new, gains_second_new = adamw_step(
        norm_gains, gains_first, gains_second, gains_sum, 0.3, 0.0
    )
    return (
        output.astype(jnp.bfloat16)[None],
        input_grad.astype(jnp.bfloat16)[None],
        query_new,
        query_first_new,
        query_second_new,
        key_new,
        key_first_new,
        key_second_new,
        value_new,
        value_first_new,
        value_second_new,
        out_new,
        out_first_new,
        out_second_new,
        gate_new,
        gate_first_new,
        gate_second_new,
        up_new,
        up_first_new,
        up_second_new,
        down_new,
        down_first_new,
        down_second_new,
        gains_new,
        gains_first_new,
        gains_second_new,
    )


def solution(mesh):
    return jax.shard_map(
        shards,
        mesh=mesh,
        in_specs=(
            P("dp", "ctx", None),
            P("dp", "ctx", None),
            P("dp", "ctx"),
            P("dp", "ctx"),
            P("dp", "ctx"),
            P(("dp", "ctx"), None),
            P(("dp", "ctx"), None),
            P(("dp", "ctx"), None),
            P(("dp", "ctx"), None),
            P(("dp", "ctx"), None),
            P(("dp", "ctx"), None),
            P("ctx", "dp"),
            P("ctx", "dp"),
            P("ctx", "dp"),
            P("dp", "ctx"),
            P("dp", "ctx"),
            P("dp", "ctx"),
            P("dp", "ctx"),
            P("dp", "ctx"),
            P("dp", "ctx"),
            P("ctx", "dp"),
            P("ctx", "dp"),
            P("ctx", "dp"),
            P(None, ("dp", "ctx")),
            P(None, ("dp", "ctx")),
            P(None, ("dp", "ctx")),
        ),
        out_specs=(
            P("dp", "ctx", None),
            P("dp", "ctx", None),
            P("dp", "ctx"),
            P("dp", "ctx"),
            P("dp", "ctx"),
            P(("dp", "ctx"), None),
            P(("dp", "ctx"), None),
            P(("dp", "ctx"), None),
            P(("dp", "ctx"), None),
            P(("dp", "ctx"), None),
            P(("dp", "ctx"), None),
            P("ctx", "dp"),
            P("ctx", "dp"),
            P("ctx", "dp"),
            P("dp", "ctx"),
            P("dp", "ctx"),
            P("dp", "ctx"),
            P("dp", "ctx"),
            P("dp", "ctx"),
            P("dp", "ctx"),
            P("ctx", "dp"),
            P("ctx", "dp"),
            P("ctx", "dp"),
            P(None, ("dp", "ctx")),
            P(None, ("dp", "ctx")),
            P(None, ("dp", "ctx")),
        ),
        check_vma=False,
    )
```

profile of v0, /device:TPU:1, one launch (start us, length us, event | category | flops | bytes accessed | tf_op | source)
XLA Modules:
  0.0 3005.8 jit_solution(13833158269278973583)
XLA Ops:
  9.3 34.3 %all-gather.1 = bf16[128,16,2]{1,2,0:T(2,128)(2,1)S(1)} all-gather(bf16[1,16,2]{1,2,0:T(2,128)(2,1)S(1)} %convert_bitcast_fusion.3), channel_id=1, replica_groups=mesh['dp'=16,'ctx'=8] {'dp','ctx'}, dimensions={0}, use_global_device_ids=true | all-gather | bytes 8256 | tf_op jit(solution)/shard_map/all_gather | solution.py:119
  52.7 25.9 all-gather.20.cloned.1.call-done
  78.6 32.1 %all-gather.14.cloned.1.call-done = bf16[1024,2048]{1,0:T(8,128)(2,1)} async-done(((bf16[128,2048]{1,0:T(8,128)(2,1)}), bf16[1024,2048]{1,0:T(8,128)(2,1)}) %all-gather.14.cloned.1.call-update) | async-done | bytes 4194320 | tf_op jit(solution)/shard_map/all_gather | solution.py:133
  114.7 62.8 %all-gather.18.cloned.1.call-done = bf16[2048,256]{1,0:T(8,128)(2,1)} async-done(((bf16[16,256]{1,0:T(8,128)(2,1)}), bf16[2048,256]{1,0:T(8,128)(2,1)}) %all-gather.18.cloned.1.call-update) | async-done | bytes 1048592 | tf_op jit(solution)/shard_map/all_gather | solution.py:117
  182.0 36.3 %all-gather.16.cloned.1.call-done = bf16[2048,256]{1,0:T(8,128)(2,1)} async-done(((bf16[128,256]{1,0:T(8,128)(2,1)}), bf16[2048,256]{1,0:T(8,128)(2,1)}) %all-gather.16.cloned.1.call-update) | async-done | bytes 1048592 | tf_op jit(solution)/shard_map/all_gather | solution.py:123
  222.8 8.4 while.30
  231.3 32.2 %all-gather.22.cloned.1.call-done = bf16[256,2048]{1,0:T(8,128)(2,1)} async-done(((bf16[256,128]{1,0:T(8,128)(2,1)}), bf16[256,2048]{1,0:T(8,128)(2,1)}) %all-gather.22.cloned.1.call-update) | async-done | bytes 1048592 | tf_op jit(solution)/shard_map/all_gather | solution.py:124
  268.9 35.2 %reduce-scatter.23.cloned.1.call-done = bf16[128,2048]{1,0:T(8,128)(2,1)} async-done(((bf16[1024,2048]{1,0:T(8,128)(2,1)}), bf16[128,2048]{1,0:T(8,128)(2,1)}) %reduce-scatter.23.cloned.1.call-update) | async-done | bytes 524304 | tf_op jit(solution)/shard_map/reduce_scatter | solution.py:165
  310.3 48.7 %all-gather.28.cloned.1.call-done = bf16[2048,704]{0,1:T(8,128)(2,1)} async-done(((bf16[128,704]{0,1:T(8,128)(2,1)}), bf16[2048,704]{0,1:T(8,128)(2,1)}) %all-gather.28.cloned.1.call-update) | async-done | bytes 2883600 | tf_op jit(solution)/shard_map/all_gather | solution.py:126
  359.0 35.4 %all-gather.24.cloned.1.call-done = bf16[1024,2048]{1,0:T(8,128)(2,1)} async-done(((bf16[128,2048]{1,0:T(8,128)(2,1)}), bf16[1024,2048]{1,0:T(8,128)(2,1)}) %all-gather.24.cloned.1.call-update) | async-done | bytes 4194320 | tf_op jit(solution)/shard_map/all_gather | solution.py:171
  394.4 7.9 fusion.121
  402.3 44.5 %all-gather.26.cloned.1.call-done = bf16[2048,704]{0,1:T(8,128)(2,1)} async-done(((bf16[128,704]{0,1:T(8,128)(2,1)}), bf16[2048,704]{0,1:T(8,128)(2,1)}) %all-gather.26.cloned.1.call-update) | async-done | bytes 2883600 | tf_op jit(solution)/shard_map/all_gather | solution.py:125
  446.8 7.8 fusion.120
  454.6 45.4 %all-gather.30.cloned.1.call-done = bf16[704,2048]{1,0:T(8,128)(2,1)} async-done(((bf16[704,128]{1,0:T(8,128)(2,1)}), bf16[704,2048]{1,0:T(8,128)(2,1)}) %all-gather.30.cloned.1.call-update) | async-done | bytes 2883600 | tf_op jit(solution)/shard_map/all_gather | solution.py:127
  500.0 34.8 %all-gather.34.cloned.1.call-done = bf16[1,1024,2048]{2,1,0:T(8,128)(2,1)} async-done(((bf16[1,128,2048]{2,1,0:T(8,128)(2,1)}), bf16[1,1024,2048]{2,1,0:T(8,128)(2,1)}) %all-gather.34.cloned.1.call-update) | async-done | bytes 4194320 | tf_op jit(solution)/shard_map/all_gather | solution.py:134
  534.8 10.2 multiply_convert_fusion.1
  554.2 34.7 %reduce-scatter.27.cloned.1.call-done = bf16[128,2048]{1,0:T(8,128)(2,1)} async-done(((bf16[1024,2048]{1,0:T(8,128)(2,1)}), bf16[128,2048]{1,0:T(8,128)(2,1)}) %reduce-scatter.27.cloned.1.call-update) | async-done | bytes 524304 | tf_op jit(solution)/shard_map/reduce_scatter | solution.py:196
  593.4 7.3 fusion.44
  605.5 7.7 convolution_convert_fusion.4
  617.8 7.5 convolution_convert_fusion.3
  643.1 35.3 %while.31 = (s32[]{:T(128)}, f32[4,1024,64]{1,2,0:T(8,128)}, f32[4,1024,64]{1,2,0:T(8,128)}, f32[4,1024,64]{1,2,0:T(8,128)}, bf16[4,1024,64]{2,1,0:T(8,128)(2,1)...) while((s32[]{:T(128)}, f32[4,1024,64]{1,2,0:T(8,128)}, ...), condition=%wide.region_12.13_spmd.clone.clone, body=%wide.region_10.12_spmd.clone.sunk.clone | while | flops 681704448 | bytes 33839220 | solution.py:229
  689.6 11.3 all_to_all.8
  736.5 6.9 convolution_convert_fusion.1
  745.6 37.3 %reduce-scatter.39.cloned.1.call-done = bf16[128,704]{1,0:T(8,128)(2,1)} async-done(((bf16[2048,704]{1,0:T(8,128)(2,1)}), bf16[128,704]{1,0:T(8,128)(2,1)}) %reduce-scatter.39.cloned.1.call-update) | async-done | bytes 180240
  784.6 76.4 %reduce-scatter.41.cloned.1.call-done = bf16[128,704]{1,0:T(8,128)(2,1)} async-done(((bf16[2048,704]{1,0:T(8,128)(2,1)}), bf16[128,704]{1,0:T(8,128)(2,1)}) %reduce-scatter.41.cloned.1.call-update) | async-done | bytes 180240
  870.0 66.2 %reduce-scatter.37.cloned.1.call-done = bf16[128,256]{1,0:T(8,128)(2,1)} async-done(((bf16[2048,256]{1,0:T(8,128)(2,1)}), bf16[128,256]{1,0:T(8,128)(2,1)}) %reduce-scatter.37.cloned.1.call-update) | async-done | bytes 65552
  939.0 72.9 %reduce-scatter.31.cloned.1.call-done = bf16[128,256]{1,0:T(8,128)(2,1)} async-done(((bf16[2048,256]{1,0:T(8,128)(2,1)}), bf16[128,256]{1,0:T(8,128)(2,1)}) %reduce-scatter.31.cloned.1.call-update) | async-done | bytes 65552 | tf_op jit(solution)/shard_map/reduce_scatter | solution.py:282
  1013.7 634.4 %reduce-scatter.35.cloned.1.call-done = f32[16,256]{1,0:T(8,128)} async-done(((f32[2048,256]{1,0:T(8,128)}), f32[16,256]{1,0:T(8,128)}) %reduce-scatter.35.cloned.1.call-update) | async-done | bytes 16400 | tf_op jit(solution)/shard_map/reduce_scatter | solution.py:300
  1649.4 634.3 %reduce-scatter.33.cloned.1.call-done = f32[16,256]{1,0:T(8,128)} async-done(((f32[2048,256]{1,0:T(8,128)}), f32[16,256]{1,0:T(8,128)}) %reduce-scatter.33.cloned.1.call-update) | async-done | bytes 16400 | tf_op jit(solution)/shard_map/reduce_scatter | solution.py:299
  2285.1 36.7 %reduce-scatter.29.cloned.1.call-done = bf16[128,2048]{1,0:T(8,128)(2,1)} async-done(((bf16[1024,2048]{1,0:T(8,128)(2,1)}), bf16[128,2048]{1,0:T(8,128)(2,1)}) %reduce-scatter.29.cloned.1.call-update) | async-done | bytes 524304 | tf_op jit(solution)/shard_map/reduce_scatter | solution.py:268
  2326.7 34.5 %reduce-scatter.25.cloned.1.call-done = bf16[128,2048]{1,0:T(8,128)(2,1)} async-done(((bf16[1024,2048]{1,0:T(8,128)(2,1)}), bf16[128,2048]{1,0:T(8,128)(2,1)}) %reduce-scatter.25.cloned.1.call-update) | async-done | bytes 524304 | tf_op jit(solution)/shard_map/reduce_scatter | solution.py:177
  2364.0 633.4 %reduce-scatter.45.cloned.1.call-done = f32[16,2]{1,0:T(8,128)} async-done(((f32[2048,2]{1,0:T(8,128)}), f32[16,2]{1,0:T(8,128)}) %reduce-scatter.45.cloned.1.call-update) | async-done | bytes 144
  (286 shorter events, 195.2 us)
Async XLA Ops:
  7.2 71.4 %all-gather.20.cloned.1.call-start = ((), (), s32[]{:S(2)}) async-start(), calls=%async_computation.17 | async-start | bytes 1056768 | tf_op jit(solution)/shard_map/all_gather | solution.py:118
  8.6 102.2 %all-gather.14.cloned.1.call-start = ((), (), s32[]{:S(2)}) async-start(), calls=%async_computation.14 | async-start | bytes 4718592 | tf_op jit(solution)/shard_map/all_gather | solution.py:133
  47.3 130.2 %all-gather.18.cloned.1.call-start = ((), (), s32[]{:S(2)}) async-start(), calls=%async_computation.16 | async-start | bytes 1056768 | tf_op jit(solution)/shard_map/all_gather | solution.py:117
  48.7 169.6 %all-gather.16.cloned.1.call-start = ((), (), s32[]{:S(2)}) async-start(), calls=%async_computation.15 | async-start | bytes 1114112 | tf_op jit(solution)/shard_map/all_gather | solution.py:123
  50.3 213.1 %all-gather.22.cloned.1.call-start = ((), (), s32[]{:S(2)}) async-start(), calls=%async_computation.18 | async-start | bytes 1114112 | tf_op jit(solution)/shard_map/all_gather | solution.py:124
  52.0 252.1 %reduce-scatter.23.cloned.1.call-start = ((), (), s32[]{:S(2)}) async-start(), calls=%async_computation.19 | async-start | bytes 4718592 | tf_op jit(solution)/shard_map/reduce_scatter | solution.py:165
  268.0 91.0 %all-gather.28.cloned.1.call-start = ((), (), s32[]{:S(2)}) async-start(), calls=%async_computation.22 | async-start | bytes 3063808 | tf_op jit(solution)/shard_map/all_gather | solution.py:126
  268.8 125.6 %all-gather.24.cloned.1.call-start = ((), (), s32[]{:S(2)}) async-start(), calls=%async_computation.20 | async-start | bytes 4718592 | tf_op jit(solution)/shard_map/all_gather | solution.py:171
  307.4 139.4 %all-gather.26.cloned.1.call-start = ((), (), s32[]{:S(2)}) async-start(), calls=%async_computation.21 | async-start | bytes 3063808 | tf_op jit(solution)/shard_map/all_gather | solution.py:125
  308.2 191.8 %all-gather.30.cloned.1.call-start = ((), (), s32[]{:S(2)}) async-start(), calls=%async_computation.23 | async-start | bytes 3063808 | tf_op jit(solution)/shard_map/all_gather | solution.py:127
  309.0 225.8 %all-gather.34.cloned.1.call-start = ((), (), s32[]{:S(2)}) async-start(), calls=%async_computation.31 | async-start | bytes 4718592 | tf_op jit(solution)/shard_map/all_gather | solution.py:134
  309.7 279.2 %reduce-scatter.27.cloned.1.call-start = ((), (), s32[]{:S(2)}) async-start(), calls=%async_computation.25 | async-start | bytes 4718592 | tf_op jit(solution)/shard_map/reduce_scatter | solution.py:196
  554.2 75.9 %all-gather.32.cloned.1.call-start = ((), (), s32[]{:S(2)}) async-start(), calls=%async_computation.26 | async-start | bytes 4718592 | tf_op jit(solution)/shard_map/all_gather | solution.py:210
  593.4 150.4 %reduce-scatter.43.cloned.1.call-start = ((), (), s32[]{:S(2)}) async-start(), calls=%async_computation.35 | async-start | bytes 3342336
  605.4 177.4 %reduce-scatter.39.cloned.1.call-start = ((), (), s32[]{:S(2)}) async-start(), calls=%async_computation.33 | async-start | bytes 3342336
  617.8 243.2 %reduce-scatter.41.cloned.1.call-start = ((), (), s32[]{:S(2)}) async-start(), calls=%async_computation.34 | async-start | bytes 3342336
  629.9 306.3 %reduce-scatter.37.cloned.1.call-start = ((), (), s32[]{:S(2)}) async-start(), calls=%async_computation.32 | async-start | bytes 1114112
  643.1 368.7 %reduce-scatter.31.cloned.1.call-start = ((), (), s32[]{:S(2)}) async-start(), calls=%async_computation.28 | async-start | bytes 1114112 | tf_op jit(solution)/shard_map/reduce_scatter | solution.py:282
  684.5 963.5 %reduce-scatter.35.cloned.1.call-start = ((), (), s32[]{:S(2)}) async-start(), calls=%async_computation.30 | async-start | bytes 2113536 | tf_op jit(solution)/shard_map/reduce_scatter | solution.py:300
  714.8 9.4 all-to-all-start
  719.0 1564.8 %reduce-scatter.33.cloned.1.call-start = ((), (), s32[]{:S(2)}) async-start(), calls=%async_computation.29 | async-start | bytes 2113536 | tf_op jit(solution)/shard_map/reduce_scatter | solution.py:299
  731.8 1590.0 %reduce-scatter.29.cloned.1.call-start = ((), (), s32[]{:S(2)}) async-start(), calls=%async_computation.27 | async-start | bytes 4718592 | tf_op jit(solution)/shard_map/reduce_scatter | solution.py:268
  735.2 1626.1 %reduce-scatter.25.cloned.1.call-start = ((), (), s32[]{:S(2)}) async-start(), calls=%async_computation.24 | async-start | bytes 4718592 | tf_op jit(solution)/shard_map/reduce_scatter | solution.py:177
  743.5 2254.0 %reduce-scatter.45.cloned.1.call-start = ((), (), s32[]{:S(2)}) async-start(), calls=%async_computation.36 | async-start | bytes 1056768
  862.8 1421.0 %copy-start.24 = (f32[16,256]{1,0:T(8,128)S(1)}, f32[16,256]{1,0:T(8,128)}, u32[]{:S(2)}) copy-start(f32[16,256]{1,0:T(8,128)} %param.35) | copy-start | bytes 49156
  862.8 1459.0 %copy-start.5 = (bf16[2048,256]{1,0:T(8,128)(2,1)S(1)}, bf16[2048,256]{1,0:T(8,128)(2,1)}, u32[]{:S(2)}) copy-start(bf16[2048,256]{1,0:T(8,128)(2,1)} %all-gather.18.cloned.1.call-done) | copy-start | bytes 3145732
  865.2 1418.6 %copy-start.28 = (f32[16,256]{1,0:T(8,128)S(1)}, f32[16,256]{1,0:T(8,128)}, u32[]{:S(2)}) copy-start(f32[16,256]{1,0:T(8,128)} %param.36) | copy-start | bytes 49156
  865.2 1418.6 %copy-start.29 = (f32[16,256]{1,0:T(8,128)S(1)}, f32[16,256]{1,0:T(8,128)}, u32[]{:S(2)}) copy-start(f32[16,256]{1,0:T(8,128)} %param.37) | copy-start | bytes 49156
  865.2 1456.6 %copy-start.19 = (bf16[128,4,64]{0,2,1:T(8,128)(2,1)S(1)}, bf16[128,4,64]{0,2,1:T(8,128)(2,1)}, u32[]{:S(2)}) copy-start(bf16[128,4,64]{0,2,1:T(8,128)(2,1)} %copy-done.18) | copy-start | bytes 196612
  865.2 1458.1 %copy-start.17 = (bf16[128,4,64]{0,2,1:T(8,128)(2,1)S(1)}, bf16[128,4,64]{0,2,1:T(8,128)(2,1)}, u32[]{:S(2)}) copy-start(bf16[128,4,64]{0,2,1:T(8,128)(2,1)} %copy-done.16) | copy-start | bytes 196612
  865.2 1458.1 %copy-start.32 = (f32[128]{0:T(128)S(1)}, f32[128]{0:T(128)}, u32[]{:S(2)}) copy-start(f32[128]{0:T(128)} %copy-done.30) | copy-start | bytes 1540
  937.2 1388.0 %copy-start.25 = (f32[2048]{0:T(1024)S(1)}, f32[2048]{0:T(1024)}, u32[]{:S(2)}) copy-start(f32[2048]{0:T(1024)} %get-tuple-element.249) | copy-start | bytes 24580
  (38 other events, 6012.6 us)
Sparse Core Ops, SparseCore 0:
  11.4 67.1 all-gather.19
  80.9 29.8 all-gather.13
  114.1 63.3 all-gather.17
  180.1 38.2 all-gather.15
  220.9 42.5 all-gather.21
  268.1 35.8 reduce-scatter.22
  306.7 52.2 all-gather.27
  361.3 33.0 all-gather.23
  397.1 49.6 all-gather.25
  449.3 50.5 all-gather.29
  501.7 33.0 all-gather.33
  554.3 34.5 reduce-scatter.26
  593.5 34.5 all-gather.31
  631.2 73.3 reduce-scatter.42
  707.8 74.9 reduce-scatter.38
  786.0 74.9 reduce-scatter.40
  864.1 72.1 reduce-scatter.36
  939.6 72.1 reduce-scatter.30
  1014.2 633.8 reduce-scatter.34
  1650.4 633.3 reduce-scatter.32
  2286.2 35.5 reduce-scatter.28
  2324.2 36.9 reduce-scatter.24
  2363.6 633.8 reduce-scatter.44
where the time goes:
time: 3020 us; the launch traced here: 3010 us
  waiting for transfers between devices  2700 us (89%)
  matrix products  141 us (5%)
  other arithmetic  57.3 us (2%)
  blocking collectives  45.7 us (2%)
  local copies, waits for them, and re-layouts  40.4 us (1%)
    unnamed x28, waiting for transfers between devices  814 us
    reduce_scatter x1, waiting for transfers between devices, shards(): lax.psum_scatter(value_wgrad, ('dp', 'ctx'), scatter_dimension=0, tiled=T...  634 us
    reduce_scatter x1, waiting for transfers between devices, shards(): lax.psum_scatter(key_wgrad, ('dp', 'ctx'), scatter_dimension=0, tiled=True)  634 us
    reduce_scatter x1, waiting for transfers between devices, shards(): lax.psum_scatter(query_wgrad.astype(jnp.bfloat16), 'dp', scatter_dimensio...  72.9 us
    all_gather x1, waiting for transfers between devices, shards(): lax.all_gather(w_key.astype(jnp.bfloat16), ('dp', 'ctx'), axis=0, tiled=T...  62.8 us
  transfers between devices with their start and end apart: 24, of which 22 were waited for; matrix products, arithmetic and copies ran while one was open for 7% of the time, Pallas kernels for 0%

commit v1 on v0

v1 whole, which is shorter than its diff:
```python
import functools

import jax
import jax.numpy as jnp
from jax import lax
from jax.experimental import pallas as pl
from jax.experimental.pallas import tpu as pltpu
from jax.sharding import Mesh
from jax.sharding import PartitionSpec as P

D = 2048
HEADS = 32
KV_HEADS = 4
HD = 64
FF = 5632
SEQ_LEN = 1024
STEP = 10

EPS = 1e-05
BETA_ONE = 0.9
BETA_TWO = 0.95
ADAM_EPS = 1e-08
DECAY = 0.1

ROWS = 128
HID = FF // 8
TILES = 6
PAD = TILES * 128
QW = 256
AW = 384
BF = jnp.bfloat16
F32 = jnp.float32
MIB = 2**20


def params(limit=56, **more):
    return pltpu.CompilerParams(vmem_limit_bytes=limit * MIB, **more)


def cost(flops, nbytes, trans=0):
    return pl.CostEstimate(flops=int(flops), bytes_accessed=int(nbytes), transcendentals=int(trans))


def dot(left, right):
    return jnp.dot(left, right, preferred_element_type=F32)


def dot_cols(left, right):
    return lax.dot_general(left, right, (((1,), (1,)), ((), ())), preferred_element_type=F32)


def dot_rows(left, right):
    return lax.dot_general(left, right, (((0,), (0,)), ((), ())), preferred_element_type=F32)


def swap_halves(v):
    width = v.shape[-1]
    lane = lax.broadcasted_iota(jnp.int32, v.shape, v.ndim - 1)
    return jnp.where(
        lane % HD < HD // 2,
        pltpu.roll(v, width - HD // 2, v.ndim - 1),
        pltpu.roll(v, HD // 2, v.ndim - 1),
    )


def ring(axis, k):
    return functools.partial(
        lax.ppermute, axis_name=axis, perm=[(i, (i + k) % 4) for i in range(4)]
    )


def other_core(v):
    return lax.ppermute(v, "core", [(0, 1), (1, 0)])


def spread(v):
    own = [v, ring("z", 1)(v), ring("z", 2)(v), ring("z", 3)(v)]
    return own + [other_core(t) for t in own]


def gather_axis(v, axis):
    me = lax.axis_index(axis)
    out = lax.dynamic_update_index_in_dim(jnp.zeros((4,) + v.shape, v.dtype), v, me, 0)
    for k in (1, 3, 2):
        out = lax.dynamic_update_index_in_dim(out, ring(axis, k)(v), (me - k) % 4, 0)
    return out


def scatter_axis(v, axis):
    me = lax.axis_index(axis)
    part = lambda k: lax.dynamic_index_in_dim(v, (me + k) % 4, 0, False)
    total = part(0).astype(F32)
    for k in (1, 3, 2):
        total = total + ring(axis, k)(part(k)).astype(F32)
    return total


def natural(parts, axis):
    me = lax.axis_index(axis)
    turned = jnp.stack([parts[3], parts[2], parts[1], parts[0]])
    return lax.dynamic_slice_in_dim(jnp.concatenate([turned, turned]), 3 - me, 4, 0)


def load_blocks(where, blocks, held, sems):
    step = pl.program_id(0)

    def copy(i, k, half, source):
        return pltpu.make_async_copy(
            source, held.at[k, pl.ds(pl.multiple_of(half * ROWS, ROWS), ROWS)], sems.at[i]
        )

    @pl.when(step == 0)
    def _():
        for k in range(4):
            copy(k, k, where[4], blocks[k]).start()
            copy(4 + k, k, 1 - where[4], blocks[4 + k]).start()

    copy(step, step, where[4], blocks[0]).wait()
    copy(4 + step, step, 1 - where[4], blocks[4]).wait()
    return held[step]


HELD = [pltpu.VMEM((4, 2 * ROWS, D), BF), pltpu.SemaphoreType.DMA((8,))]
ANY8 = [pl.BlockSpec(memory_space=pl.ANY)] * 8


def by_block(width):
    return pl.BlockSpec((2 * ROWS, width), lambda i, where: (where[i], 0))


def whole(*shape):
    return pl.BlockSpec(shape, lambda i, *_: (0,) * len(shape))


def blocks_call(kernel, where, blocks, operands, in_specs, out_widths, flops):
    outs = [jax.ShapeDtypeStruct((SEQ_LEN, w), t) for w, t in out_widths]
    nbytes = 4 * 2**20 + sum(o.size * o.dtype.itemsize for o in outs)
    nbytes += sum(o.size * o.dtype.itemsize for o in operands)
    return pl.pallas_call(
        kernel,
        grid_spec=pltpu.PrefetchScalarGridSpec(
            num_scalar_prefetch=1,
            grid=(4,),
            in_specs=ANY8 + in_specs,
            out_specs=[by_block(w) for w, _ in out_widths],
            scratch_shapes=HELD,
        ),
        out_shape=outs,
        compiler_params=params(),
        cost_estimate=cost(flops, nbytes),
    )(where, *blocks, *operands)


def first_kernel(where, *refs):
    blocks, (w, tcos, tsin, unit_out, q_out, kv_out, held, sems) = refs[:8], refs[8:]
    x = load_blocks(where, blocks, held, sems).astype(F32)
    inv = lax.rsqrt(jnp.mean(x * x, axis=-1, keepdims=True) + EPS)
    unit = (x * inv).astype(BF)
    unit_out[...] = unit
    y = dot(unit, w[...])
    cos, sin = tcos[...], tsin[...]
    for j in range(2):
        part = y[:, j * 128 : (j + 1) * 128]
        q_out[:, j * 128 : (j + 1) * 128] = (part * cos + swap_halves(part) * sin).astype(BF)
    part = y[:, 256:384]
    is_key = lax.broadcasted_iota(jnp.int32, part.shape, 1) < HD
    kv_out[...] = jnp.where(is_key, part * cos + swap_halves(part) * sin, part).astype(BF)


def first_call(where, blocks, w, tcos, tsin):
    return blocks_call(
        first_kernel,
        where,
        blocks,
        (w, tcos, tsin),
        [whole(D, AW), by_block(128), by_block(128)],
        [(D, BF), (QW, BF), (128, BF)],
        2 * SEQ_LEN * D * AW,
    )


def hidden_grad_kernel(where, *refs):
    blocks, (w, all_out, grad_out, held, sems) = refs[:8], refs[8:]
    x = load_blocks(where, blocks, held, sems)
    all_out[...] = x
    grad_out[...] = dot(x, w[...])


def hidden_grad_call(where, blocks, w):
    return blocks_call(
        hidden_grad_kernel,
        where,
        blocks,
        (w,),
        [pl.BlockSpec((D, PAD), lambda i, *_: (0, 2))],
        [(D, BF), (PAD, F32)],
        2 * SEQ_LEN * D * PAD,
    )


def middle_kernel(where, *refs):
    blocks, (w, hg, all_out, hidden_out, grads_out, held, sems) = refs[:8], refs[8:]
    x = load_blocks(where, blocks, held, sems)
    all_out[...] = x
    for j in range(TILES):
        y = dot(x, w[:, 256 * j : 256 * (j + 1)])
        gate, up = y[:, :128], y[:, 128:]
        sigma = jax.nn.sigmoid(gate)
        swish = gate * sigma
        back = hg[:, 128 * j : 128 * (j + 1)]
        hidden_out[:, 128 * j : 128 * (j + 1)] = (swish * up).astype(BF)
        grads_out[:, 256 * j : 256 * j + 128] = (
            back * up * (sigma * (1.0 + gate * (1.0 - sigma)))
        ).astype(BF)
        grads_out[:, 256 * j + 128 : 256 * (j + 1)] = (back * swish).astype(BF)


def middle_call(where, blocks, w, hg):
    return blocks_call(
        middle_kernel,
        where,
        blocks,
        (w, hg),
        [whole(D, 2 * PAD), by_block(PAD)],
        [(D, BF), (PAD, BF), (2 * PAD, BF)],
        2 * SEQ_LEN * D * 2 * PAD,
    )


def mixed_grad_kernel(where, *refs):
    blocks, (w, all_out, grad_out, held, sems) = refs[:8], refs[8:]
    x = load_blocks(where, blocks, held, sems)
    all_out[...] = x
    grad_out[...] = dot(x, w[...]).astype(BF)


def mixed_grad_call(where, blocks, w):
    return blocks_call(
        mixed_grad_kernel,
        where,
        blocks,
        (w,),
        [whole(D, QW)],
        [(D, BF), (QW, BF)],
        2 * SEQ_LEN * D * QW,
    )


def partial_kernel(has_addend, has_unit, n_out, order, a, w, *refs):
    refs = list(refs)
    addend = refs.pop(0) if has_addend else None
    unit = refs.pop(0) if has_unit else None
    outs = [refs.pop(0) for _ in range(n_out)]
    gain_out = refs.pop(0) if has_unit else None
    picked = refs.pop(0)

    def block(k):
        return pl.ds(pl.multiple_of(order[k] * ROWS, ROWS), ROWS)

    @pl.when(pl.program_id(0) == 0)
    def _():
        for k in range(4):
            picked[k * ROWS : (k + 1) * ROWS] = a[block(k)]

    y = dot_cols(picked[...], w[...])
    if has_unit:
        total = jnp.zeros((1, y.shape[1]), F32)
        for k in range(4):
            total += jnp.sum(
                y[k * ROWS : (k + 1) * ROWS] * unit[block(k)].astype(F32), axis=0, keepdims=True
            )
        gain_out[...] = total
    if has_addend:
        y = y + addend[...].astype(F32)
    y = y.astype(BF)
    if n_out == 1:
        outs[0][...] = y
    else:
        for k in range(4):
            outs[k][...] = y[k * ROWS : (k + 1) * ROWS]


def partial_call(order, a, w, col, addend=None, unit=None):
    depth, tile = a.shape[1], 256
    in_specs = [
        whole(SEQ_LEN, depth),
        pl.BlockSpec((tile, depth), lambda i, *_: (i, col)),
    ]
    operands = [a, w]
    n_out, rows = 1, 4 * ROWS
    if addend is not None:
        n_out, rows = 4, ROWS
        in_specs.append(pl.BlockSpec((4 * ROWS, tile), lambda i, *_: (0, i)))
        operands.append(addend)
    out_specs = [pl.BlockSpec((rows, tile), lambda i, *_: (0, i))] * n_out
    out_shape = [jax.ShapeDtypeStruct((rows, D), BF)] * n_out
    if unit is not None:
        in_specs.append(pl.BlockSpec((SEQ_LEN, tile), lambda i, *_: (0, i)))
        operands.append(unit)
        out_specs = out_specs + [pl.BlockSpec((1, tile), lambda i, *_: (0, i))]
        out_shape = out_shape + [jax.ShapeDtypeStruct((1, D), F32)]
    return pl.pallas_call(
        functools.partial(partial_kernel, addend is not None, unit is not None, n_out),
        grid_spec=pltpu.PrefetchScalarGridSpec(
            num_scalar_prefetch=1,
            grid=(D // tile,),
            in_specs=in_specs,
            out_specs=out_specs,
            scratch_shapes=[pltpu.VMEM((4 * ROWS, depth), BF)],
        ),
        out_shape=out_shape,
        compiler_params=params(),
        cost_estimate=cost(
            2 * 4 * ROWS * D * depth, 2 * depth * (D + 512) + (2 + 2 * (n_out == 4)) * MIB
        ),
    )(order, *operands)


def scores_of(q, k, diagonal):
    s = dot_cols(q, k)
    if diagonal:
        row = lax.broadcasted_iota(jnp.int32, s.shape, 0) % ROWS
        s = jnp.where(row >= lax.broadcasted_iota(jnp.int32, s.shape, 1), s, -1e30)
    return s


def stack_heads(v):
    return jnp.concatenate([v[:, HD * h : HD * (h + 1)] for h in range(4)], axis=0)


def lay_heads(v):
    return jnp.concatenate([v[ROWS * h : ROWS * (h + 1)] for h in range(4)], axis=1)


def attend_kernel(q, kv, out, lse):
    key, value = kv[:, :HD], kv[:, HD:]
    lane = lax.broadcasted_iota(jnp.int32, (ROWS, 128), 1)
    for b in range(8):
        rows = slice(b * ROWS, (b + 1) * ROWS)
        mine = stack_heads(q[rows] * HD**-0.5)
        pieces = [(scores_of(mine, key[rows], True), value[rows])]
        if b:
            pieces.append((scores_of(mine, key[: b * ROWS], False), value[: b * ROWS]))
        top = functools.reduce(
            jnp.maximum, [jnp.max(s, axis=-1, keepdims=True) for s, _ in pieces]
        )
        total, mixed = 0.0, 0.0
        for s, v in pieces:
            p = jnp.exp(s - top)
            total = total + jnp.sum(p, axis=-1, keepdims=True)
            mixed = mixed + dot(p.astype(BF), v)
        out[rows] = lay_heads(mixed / total).astype(BF)
        log_total = top + jnp.log(total)
        spread_out = jnp.zeros((ROWS, 128), F32)
        for h in range(4):
            spread_out = jnp.where(lane == h, log_total[ROWS * h : ROWS * (h + 1)], spread_out)
        lse[rows] = spread_out


def attend_call(q, kv):
    return pl.pallas_call(
        attend_kernel,
        out_shape=[
            jax.ShapeDtypeStruct((SEQ_LEN, QW), BF),
            jax.ShapeDtypeStruct((SEQ_LEN, 128), F32),
        ],
        compiler_params=params(),
        cost_estimate=cost(4e9, 2 * MIB, 2 * MIB),
    )(q, kv)


def attend_back_kernel(q, kv, lse, mixed_grad, tcos, tsin, q_grad, kv_grad, held):
    key, value = kv[:, :HD], kv[:, HD:]
    held[...] = jnp.zeros_like(held)
    for b in range(8):
        rows = slice(b * ROWS, (b + 1) * ROWS)
        mine = stack_heads(q[rows] * HD**-0.5)
        grad = stack_heads(mixed_grad[rows])
        log_total = jnp.concatenate([lse[rows, h : h + 1] for h in range(4)], axis=0)
        pieces = [(rows, True)] + ([(slice(0, b * ROWS), False)] if b else [])
        probs, back = [], []
        inner = 0.0
        for cols, diagonal in pieces:
            p = jnp.exp(scores_of(mine, key[cols], diagonal) - log_total)
            g = dot_cols(grad, value[cols])
            inner = inner + jnp.sum(p * g, axis=-1, keepdims=True)
            probs.append(p)
            back.append(g)
        total = 0.0
        for (cols, _), p, g in zip(pieces, probs, back):
            s_grad = (p * (g - inner)).astype(BF)
            total = total + dot(s_grad, key[cols])
            held[:HD, cols] += dot_rows(mine, s_grad)
            held[HD:, cols] += dot_rows(grad, p.astype(BF))
        wide = lay_heads(total * HD**-0.5)
        cos, sin = tcos[rows], tsin[rows]
        for j in range(2):
            part = wide[:, 128 * j : 128 * (j + 1)]
            q_grad[rows, 128 * j : 128 * (j + 1)] = (part * cos - swap_halves(part) * sin).astype(
                BF
            )
    kv_grad[...] = held[...].T


def attend_back_call(q, kv, lse, mixed_grad, tcos, tsin):
    return pl.pallas_call(
        attend_back_kernel,
        out_shape=[
            jax.ShapeDtypeStruct((SEQ_LEN, QW), BF),
            jax.ShapeDtypeStruct((SEQ_LEN, 128), F32),
        ],
        scratch_shapes=[pltpu.VMEM((128, SEQ_LEN), F32)],
        compiler_params=params(),
        cost_estimate=cost(8e9, 4 * MIB, 2 * MIB),
    )(q, kv, lse, mixed_grad, tcos, tsin)


def wgrad_kernel(n, *refs):
    out = refs[-1]
    at = 0
    for j in range(n):
        x, g = refs[2 * j], refs[2 * j + 1]
        width = g.shape[1]
        out[:, at : at + width] = dot_rows(x[...], g[...]).astype(BF)
        at += width


def wgrad_call(*pairs):
    tile = 256
    in_specs, operands, width = [], [], 0
    for x, g in pairs:
        in_specs += [
            pl.BlockSpec((SEQ_LEN, tile), lambda i: (0, i)),
            pl.BlockSpec(g.shape, lambda i: (0, 0)),
        ]
        operands += [x, g]
        width += g.shape[1]
    return pl.pallas_call(
        functools.partial(wgrad_kernel, len(pairs)),
        grid=(D // tile,),
        in_specs=in_specs,
        out_specs=pl.BlockSpec((tile, width), lambda i: (i, 0)),
        out_shape=jax.ShapeDtypeStruct((D, width), BF),
        compiler_params=params(),
        cost_estimate=cost(
            2 * SEQ_LEN * D * width, 4 * MIB * len(pairs) + 2 * width * (SEQ_LEN + D)
        ),
    )(*operands)


def adamw_step(weight, first, second, gradient, rate, decay):
    first_new = BETA_ONE * first + (1.0 - BETA_ONE) * gradient
    second_new = BETA_TWO * second + (1.0 - BETA_TWO) * gradient * gradient
    first_hat = first_new / (1.0 - BETA_ONE**STEP)
    second_hat = second_new / (1.0 - BETA_TWO**STEP)
    weight_new = weight - rate * (first_hat / (jnp.sqrt(second_hat) + ADAM_EPS) + decay * weight)
    return (weight_new, first_new, second_new)


def rotary():
    positions = jnp.arange(SEQ_LEN).astype(F32)
    frequency = 10000.0 ** (-2.0 * jnp.arange(HD // 2).astype(F32) / HD)
    angles = positions[:, None] * frequency[None, :]
    cos, sin = jnp.cos(angles), jnp.sin(angles)
    return (
        jnp.concatenate([cos] * 4, axis=1),
        jnp.concatenate([-sin, sin, -sin, sin], axis=1),
    )


def pad_hidden(v):
    return jnp.pad(v, ((0, 0), (0, PAD - HID)))


def shards(
    tokens,
    cotangent,
    w_query,
    query_first,
    query_second,
    w_key,
    key_first,
    key_second,
    w_value,
    value_first,
    value_second,
    w_out,
    out_first,
    out_second,
    w_gate,
    gate_first,
    gate_second,
    w_up,
    up_first,
    up_second,
    w_down,
    down_first,
    down_second,
    norm_gains,
    gains_first,
    gains_second,
):
    z, core = lax.axis_index("z"), lax.axis_index("core")
    away = jnp.arange(4)
    where = jnp.concatenate([(z - away) % 4, core[None]]).astype(jnp.int32)
    mine_order = (2 * ((z + away) % 4) + core).astype(jnp.int32)
    other_order = (2 * ((z + away) % 4) + 1 - core).astype(jnp.int32)
    is_zero = core == 0

    small = jnp.concatenate(
        [
            w_key.astype(BF).reshape(16, 4, HD),
            w_value.astype(BF).reshape(16, 4, HD),
            jnp.broadcast_to(
                jnp.pad(norm_gains.astype(BF).T, ((0, 0), (0, 126)))[:, None, :], (16, 4, 128)
            ),
        ],
        axis=2,
    ).transpose(1, 0, 2)
    got = []
    for k in range(4):
        piece = lax.dynamic_index_in_dim(small, (z + k) % 4, 0, False)
        got.append(ring("z", k)(piece) if k else piece)
    got = natural(got, "z")
    across = other_core(got)
    kv_rows = jnp.stack(
        [jnp.where(is_zero, got, across), jnp.where(is_zero, across, got)], axis=1
    ).reshape(128, 256)
    gain_one = kv_rows[:, 128:129].astype(F32)
    gain_two = kv_rows[:, 129:130].astype(F32)

    w_attend = jnp.concatenate([w_query.astype(BF), kv_rows[:, :128]], axis=1)
    w_attend = (w_attend.astype(F32) * gain_one).astype(BF)
    w_mixed = w_out.astype(BF).T
    gate_tiles = pad_hidden(w_gate.astype(BF)).reshape(128, TILES, 1, 128)
    up_tiles = pad_hidden(w_up.astype(BF)).reshape(128, TILES, 1, 128)
    w_wide = jnp.concatenate([gate_tiles, up_tiles], axis=2).reshape(128, 2 * PAD)
    w_wide = (w_wide.astype(F32) * gain_two).astype(BF)
    w_ffn = jnp.concatenate([w_wide, pad_hidden(w_down.astype(BF).T)], axis=1)

    all_ffn = lax.all_gather(w_ffn, ("y", "x"), axis=0, tiled=True)
    all_attend = gather_axis(gather_axis(w_attend, "x"), "y").reshape(D, AW)
    all_mixed = (
        gather_axis(gather_axis(w_mixed, "y"), "x").transpose(1, 0, 2, 3).reshape(D, QW)
    )

    tcos, tsin = rotary()
    blocks = spread(tokens[0])
    unit_all, query, key_value = first_call(where, blocks, all_attend, tcos, tsin)
    attended, lse = attend_call(query, key_value)

    def reduce_rows(a, w, col, unit=None):
        other = partial_call(other_order, a, w, col, unit=unit)
        mine = partial_call(mine_order, a, w, col, addend=other_core(other[0]), unit=unit)
        total = mine[0].astype(F32)
        for k in (2, 1, 3):
            total = total + ring("z", k)(mine[k]).astype(F32)
        return total, (other[1] + mine[4] if unit is not None else None)

    x = tokens[0].astype(F32)
    inv_first = lax.rsqrt(jnp.mean(x * x, axis=-1, keepdims=True) + EPS)
    unit_first = x * inv_first

    mixed, _ = reduce_rows(attended, all_mixed, 0)
    middle = x + mixed
    inv_second = lax.rsqrt(jnp.mean(middle * middle, axis=-1, keepdims=True) + EPS)
    unit_second = middle * inv_second

    hidden_grad_blocks = spread(cotangent[0])
    grad_all, hidden_grad = hidden_grad_call(where, hidden_grad_blocks, all_ffn)

    mid_all, hidden, wide_grad = middle_call(
        where, spread(unit_second.astype(BF)), all_ffn, hidden_grad
    )
    mid_back, _ = reduce_rows(wide_grad, all_ffn, 0)
    ffn_wgrad = wgrad_call((mid_all, wide_grad), (grad_all, hidden))
    ffn_sum = lax.psum_scatter(ffn_wgrad, ("y", "x"), scatter_dimension=0, tiled=True)
    down_rows, _ = reduce_rows(hidden, all_ffn, 2)
    output = middle + down_rows

    slope = mid_back * unit_second
    gain_two_row = jnp.sum(slope, axis=0)
    middle_grad = cotangent[0].astype(F32) + inv_second * (
        mid_back - unit_second * jnp.mean(slope, axis=-1, keepdims=True)
    )
    mid_grad_all, mixed_grad = mixed_grad_call(where, spread(middle_grad.astype(BF)), all_mixed)
    out_wgrad = wgrad_call((mid_grad_all, attended)).reshape(4, 4, 128, QW)
    out_sum = scatter_axis(scatter_axis(out_wgrad, "y").astype(BF), "x")

    query_grad, kv_grad = attend_back_call(query, key_value, lse, mixed_grad, tcos, tsin)
    key_part, value_part = kv_grad[:, :HD], kv_grad[:, HD:]
    kept = jnp.where(is_zero, key_part, value_part)
    sent = jnp.where(is_zero, value_part, key_part).astype(BF)
    kept = kept + other_core(sent).astype(F32)
    half = HD // 2
    turned = jnp.concatenate([kept[:, half:], kept[:, :half]], axis=1)
    kept = jnp.where(is_zero, kept * tcos[:, :HD] - turned * tsin[:, :HD], kept).astype(BF)
    none = jnp.zeros_like(kept)
    attend_grad = jnp.concatenate(
        [query_grad, jnp.where(is_zero, kept, none), jnp.where(is_zero, none, kept)], axis=1
    )
    in_back, gain_one_row = reduce_rows(attend_grad, all_attend, 0, unit=unit_all)
    slope = in_back * unit_first
    input_grad = middle_grad + inv_first * (
        in_back - unit_first * jnp.mean(slope, axis=-1, keepdims=True)
    )

    attend_wgrad = wgrad_call((unit_all, attend_grad))
    gain_rows = jnp.stack([gain_one_row[0], gain_two_row])
    gain_high = gain_rows.astype(BF)
    gain_low = (gain_rows - gain_high.astype(F32)).astype(BF)
    gain_cols = jnp.pad(jnp.concatenate([gain_high, gain_low]).T, ((0, 0), (0, HD - 4)))
    tail = attend_wgrad[:, QW:]
    tail = jnp.where(
        is_zero,
        jnp.concatenate([tail[:, :HD], gain_cols], axis=1),
        jnp.concatenate([gain_cols, tail[:, HD:]], axis=1),
    )
    attend_wgrad = jnp.concatenate([attend_wgrad[:, :QW], tail], axis=1).reshape(4, 4, 128, AW)
    attend_sum = scatter_axis(
        scatter_axis(attend_wgrad.transpose(1, 0, 2, 3), "x").astype(BF), "y"
    )

    tail = attend_sum[:, QW:]
    tail_kv = jnp.where(is_zero, tail[:, :HD], tail[:, HD:]) * gain_one
    tail_gain = jnp.where(is_zero, tail[:, HD:], tail[:, :HD])
    tail = jnp.concatenate([tail_kv, tail_gain], axis=1).reshape(4, 32, 128)
    got = []
    for k in range(4):
        piece = lax.dynamic_index_in_dim(tail, (z + k) % 4, 0, False)
        got.append(ring("z", k)(piece) if k else piece)
    got = natural(got, "z")
    kv_mine = got[:, :, :HD].transpose(1, 0, 2).reshape(2, 16, 4 * HD)
    gain_mine = jnp.sum(got[:, :, HD:], axis=0).reshape(2, 16, HD)
    tail = jnp.concatenate([kv_mine, gain_mine], axis=2)
    own = lax.dynamic_index_in_dim(tail, core, 0, False)
    across = other_core(lax.dynamic_index_in_dim(tail, 1 - core, 0, False))
    key_sum = jnp.where(is_zero, own[:, : 4 * HD], across[:, : 4 * HD])
    value_sum = jnp.where(is_zero, across[:, : 4 * HD], own[:, : 4 * HD])
    gain_sum = own[:, 4 * HD : 4 * HD + 4] + across[:, 4 * HD : 4 * HD + 4]
    gains_sum = (gain_sum[:, :2] + gain_sum[:, 2:4]).T / norm_gains.astype(BF).astype(F32)

    query_sum = attend_sum[:, :QW] * gain_one
    wide_sum = ffn_sum[:, : 2 * PAD].astype(F32) * gain_two
    wide_sum = wide_sum.reshape(128, TILES, 2, 128)
    gate_sum = wide_sum[:, :, 0].reshape(128, PAD)[:, :HID]
    up_sum = wide_sum[:, :, 1].reshape(128, PAD)[:, :HID]
    down_sum = ffn_sum[:, 2 * PAD : 2 * PAD + HID].astype(F32).T

    wide_rate = 2.0 * D ** (-0.5)
    out_rate = 2.0 * max(1, 16 * D // SEQ_LEN) ** (-0.5)
    down_rate = 2.0 * FF ** (-0.5)
    return (
        output.astype(BF)[None],
        input_grad.astype(BF)[None],
        *adamw_step(w_query, query_first, query_second, query_sum, wide_rate, DECAY),
        *adamw_step(w_key, key_first, key_second, key_sum, wide_rate, DECAY),
        *adamw_step(w_value, value_first, value_second, value_sum, wide_rate, DECAY),
        *adamw_step(w_out, out_first, out_second, out_sum.T, out_rate, DECAY),
        *adamw_step(w_gate, gate_first, gate_second, gate_sum, wide_rate, DECAY),
        *adamw_step(w_up, up_first, up_second, up_sum, wide_rate, DECAY),
        *adamw_step(w_down, down_first, down_second, down_sum, down_rate, DECAY),
        *adamw_step(norm_gains, gains_first, gains_second, gains_sum, 0.3, 0.0),
    )


def solution(mesh):
    dp, ctx = ("y", "x"), ("z", "core")
    fine = Mesh(mesh.devices.reshape(4, 4, 4, 2), dp + ctx)
    act, col, row = P(dp, ctx, None), P(dp, ctx), P(ctx, dp)
    flat, gains = P(dp + ctx, None), P(None, dp + ctx)
    weights = (col,) * 3 + (flat,) * 6 + (row,) * 3 + (col,) * 6 + (row,) * 3 + (gains,) * 3
    return jax.shard_map(
        shards,
        mesh=fine,
        in_specs=(act, act) + weights,
        out_specs=(act, act) + weights,
        check_vma=False,
    )
```

time: 3020 us -> 556 us (0.18)
  waiting for transfers between devices: 2700 us -> 166 us
  Pallas kernels: 0 us -> 159 us
  matrix products: 141 us -> 0 us
  starting transfers between devices: 5.87 us -> 113 us
  blocking collectives: 45.7 us -> 0 us
    reduce_scatter x7 -> x1, waiting for transfers between devices: 1480 us -> 0.01 us  [shards(): lax.psum_scatter(ffn_wgrad, ('y', 'x'), scatter_dimension=0, tiled=True)]
    unnamed x28 -> x2, waiting for transfers between devices: 814 us -> 0.03 us
    all_gather x11 -> x1, waiting for transfers between devices: 398 us -> 0.02 us  [shards(): all_ffn = lax.all_gather(w_ffn, ('y', 'x'), axis=0, tiled=True)]
    ppermute x0 -> x77, waiting for transfers between devices: none -> 166 us  [the longest x12 65.8 us: spread(): own = [v, ring('z', 1)(v), ring('z', 2)(v), ring('z', 3)(v)]]
    pallas_call x0 -> x17, Pallas kernels: none -> 159 us  [the longest x8 72 us: partial_call(): pl.pallas_call(functools.partial(partial_kernel, addend is not None, unit...]
    dot_general x49 -> x0, matrix products: 141 us -> none  [the longest x15 51.6 us: contract_rows(): lax.dot_general(left, right, (((0,), (0,)), ((), ())), preferred_element_...]
    ppermute x0 -> x77, starting transfers between devices: none -> 113 us  [the longest x23 49.7 us: other_core(): return lax.ppermute(v, 'core', [(0, 1), (1, 0)])]
    all_gather x1 -> x0, blocking collectives: 34.3 us -> none  [shards(): lax.all_gather(norm_gains.astype(jnp.bfloat16), ('dp', 'ctx'), axis=1, ti...]
  transfers between devices with their start and end apart: 24 -> 79, of which waited for: 22 -> 25; matrix products, arithmetic and copies ran while one was open for 7% -> 12% of each run, Pallas kernels for 0% -> 23%
where the time goes in v1:
time: 556 us; the launch traced here: 549 us
  waiting for transfers between devices  166 us (30%)
  Pallas kernels  159 us (29%)
  starting transfers between devices  113 us (20%)
  local copies, waits for them, and re-layouts  53 us (10%)
  other arithmetic  42.1 us (8%)
  between operations  16.1 us (3%)
    pallas_call x8, Pallas kernels, partial_call(): pl.pallas_call(functools.partial(partial_kernel, addend is not None, unit...  72 us
    ppermute x12, waiting for transfers between devices, spread(): own = [v, ring('z', 1)(v), ring('z', 2)(v), ring('z', 3)(v)]  65.8 us
    ppermute x23, starting transfers between devices, other_core(): return lax.ppermute(v, 'core', [(0, 1), (1, 0)])  49.7 us
    ppermute x12, waiting for transfers between devices, reduce_rows(): total = total + ring('z', k)(mine[k]).astype(F32)  42.2 us
    pallas_call x4, Pallas kernels, blocks_call(): pl.pallas_call(kernel, grid_spec=pltpu.PrefetchScalarGridSpec(num_scalar_...  38.2 us
    pallas_call x3, Pallas kernels, wgrad_call(): pl.pallas_call(functools.partial(wgrad_kernel, len(pairs)), grid=(D // ti...  31.3 us
    unnamed x217, local copies, waits for them, and re-layouts  25.9 us
    ppermute x6, waiting for transfers between devices, shards(): got.append(ring('z', k)(piece) if k else piece)  21 us
  transfers between devices with their start and end apart: 79, of which 25 were waited for; matrix products, arithmetic and copies ran while one was open for 12% of the time, Pallas kernels for 23%

profile of v1, /device:TPU:1, one launch (start us, length us, event | category | flops | bytes accessed | tf_op | source)
XLA Modules:
  0.0 549.3 jit_solution(6793591330323060175)
XLA Ops:
  51.7 6.4 %collective-permute-done.20 = bf16[4,128,256]{2,1,0:T(8,128)(2,1)S(1)} collective-permute-done((bf16[4,128,256]{2,1,0:T(8,128)(2,1)}, bf16[4,128,256]{2,1,0:T(8,128)(2,1)S(1)}, u32[]{:S(2)}, u32[]{:S(2)}) %collective-permute-start.20) | collective-permute-done | bytes 262176 | tf_op jit(solution)/shard_map/ppermute | solution.py:85
  73.1 9.7 %collective-permute-start.5 = (bf16[128,2048]{1,0:T(8,128)(2,1)}, bf16[128,2048]{1,0:T(8,128)(2,1)S(1)}, u32[]{:S(2)}, u32[]{:S(2)}) collective-permute-start(bf16[128,2048]{1,0:T(8,128)(2,1)} %collective-permute-done.1.refs_2_), channel_id=1, source_target_pairs={{0,1},{1,0},{2,3},{3,2},{4,5},{5,4},{6,7},{7,6},{8,9},{9,8},{10,11... | collective-permute-start | bytes 1572872 | tf_op jit(solution)/shard_map/ppermute | solution.py:73
  94.2 9.1 %shard_map.449 = (bf16[1024,2048]{1,0:T(8,128)(2,1)}, bf16[1024,256]{1,0:T(8,128)(2,1)}, bf16[1024,128]{1,0:T(8,128)(2,1)}) custom-call(s32[5]{0:T(128)} %pad_add_fusion.where, bf16[128,2048]{1,0:T(8,128)(2,1)} %bitcast.179, bf16[128,2048]{1,0:T(8,128)(2,1)} %collective-permute-done.refs_1_, bf16[128,2048]{1,0:T(8,128)(2,1)} %collective-permute-done.1.refs_2_, ...), custom_call_target="tpu_custom_call" | custom-call | flops 1610612736 | bytes 11796480 | tf_op jit(solution)/shard_map/pallas_call | solution.py:139
  103.4 6.7 %shard_map.450 = (bf16[1024,256]{1,0:T(8,128)(2,1)}, f32[1024,128]{1,0:T(8,128)}) custom-call(bf16[1024,256]{1,0:T(8,128)(2,1)} %get-tuple-element.59.q, bf16[1024,128]{1,0:T(8,128)(2,1)} %get-tuple-element.60.kv), custom_call_target="tpu_custom_call" | custom-call | flops 4000000000 | bytes 2097152 | tf_op jit(solution)/shard_map/pallas_call | solution.py:361
  110.1 7.5 %shard_map.451 = bf16[512,2048]{1,0:T(8,128)(2,1)} custom-call(s32[4]{0:T(128)} %add_subtract_fusion.order, bf16[1024,256]{1,0:T(8,128)(2,1)} %get-tuple-element.61.a.refs_1_, bf16[2048,256]{1,0:T(8,128)(2,1)} %bitcast.176), custom_call_target="tpu_custom_call" | custom-call | flops 536870912 | bytes 3407872 | tf_op jit(solution)/shard_map/pallas_call | solution.py:302
  117.5 7.2 %collective-permute-start.23 = (bf16[512,2048]{1,0:T(8,128)(2,1)}, bf16[512,2048]{1,0:T(8,128)(2,1)S(1)}, u32[]{:S(2)}, u32[]{:S(2)}) collective-permute-start(bf16[512,2048]{1,0:T(8,128)(2,1)} %shard_map.451), channel_id=1, source_target_pairs={{0,1},{1,0},{2,3},{3,2},{4,5},{5,4},{6,7},{7,6},{8,9},{9,8},{10,11... | collective-permute-start | bytes 6291464 | tf_op jit(solution)/shard_map/ppermute | solution.py:73
  130.1 7.7 %shard_map.452 = (bf16[128,2048]{1,0:T(8,128)(2,1)}, bf16[128,2048]{1,0:T(8,128)(2,1)}, bf16[128,2048]{1,0:T(8,128)(2,1)}, bf16[128,2048]{1,0:T(8,128)(2,1)}) custom-call(s32[4]{0:T(128)} %broadcast_add_fusion.order, bf16[1024,256]{1,0:T(8,128)(2,1)} %get-tuple-element.61.a.refs_1_, bf16[2048,256]{1,0:T(8,128)(2,1)} %bitcast.177, bf16[512,2048]{1,0:T(8,128)(2,1)} %copy-done.13), custom_call_target="tpu_custom_call" | custom-call | flops 536870912 | bytes 5505024 | tf_op jit(solution)/shard_map/pallas_call | solution.py:302
  140.6 21.3 %collective-permute-done.34.refs_1_ = bf16[128,2048]{1,0:T(8,128)(2,1)S(1)} collective-permute-done((bf16[128,2048]{1,0:T(8,128)(2,1)S(1)}, bf16[128,2048]{1,0:T(8,128)(2,1)S(1)}, u32[]{:S(2)}, u32[]{:S(2)}) %collective-permute-start.34) | collective-permute-done | bytes 524320 | tf_op jit(solution)/shard_map/ppermute | solution.py:77
  163.4 9.7 %collective-permute-done.25 = bf16[128,2048]{1,0:T(8,128)(2,1)S(1)} collective-permute-done((bf16[128,2048]{1,0:T(8,128)(2,1)}, bf16[128,2048]{1,0:T(8,128)(2,1)S(1)}, u32[]{:S(2)}, u32[]{:S(2)}) %collective-permute-start.25) | collective-permute-done | bytes 524320 | tf_op jit(solution)/shard_map/ppermute | solution.py:557
  173.1 10.9 %collective-permute-start.39 = (bf16[128,2048]{1,0:T(8,128)(2,1)S(1)}, bf16[128,2048]{1,0:T(8,128)(2,1)S(1)}, u32[]{:S(2)}, u32[]{:S(2)}) collective-permute-start(bf16[128,2048]{1,0:T(8,128)(2,1)S(1)} %collective-permute-done.35.refs_2_), channel_id=1, source_target_pairs={{0,1},{1,0},{2,3},{3,2},{4,5},{5,4},{6,7},{7,6},{8,9},{9,8},{10,11... | collective-permute-start | bytes 1572872 | tf_op jit(solution)/shard_map/ppermute | solution.py:73
  189.8 22.6 %collective-permute-done.27.refs_1_ = bf16[128,2048]{1,0:T(8,128)(2,1)} collective-permute-done((bf16[128,2048]{1,0:T(8,128)(2,1)S(1)}, bf16[128,2048]{1,0:T(8,128)(2,1)}, u32[]{:S(2)}, u32[]{:S(2)}) %collective-permute-start.27) | collective-permute-done | bytes 524320 | tf_op jit(solution)/shard_map/ppermute | solution.py:77
  214.7 8.9 %shard_map.453 = (bf16[1024,2048]{1,0:T(8,128)(2,1)}, f32[1024,768]{1,0:T(8,128)}) custom-call(s32[5]{0:T(128)} %pad_add_fusion.where, bf16[128,2048]{1,0:T(8,128)(2,1)} %bitcast.188, bf16[128,2048]{1,0:T(8,128)(2,1)} %copy-done.56, bf16[128,2048]{1,0:T(8,128)(2,1)} %copy-done.57, bf16[128,2048]{1,0:T(8,128)(2,1)} %copy-done.58, ...), custom_call_target="tpu_custom_call" | custom-call | flops 3221225472 | bytes 20971520 | tf_op jit(solution)/shard_map/pallas_call | solution.py:139
  224.4 13.9 %shard_map.454 = (bf16[1024,2048]{1,0:T(8,128)(2,1)}, bf16[1024,768]{1,0:T(8,128)(2,1)}, bf16[1024,1536]{1,0:T(8,128)(2,1)}) custom-call(s32[5]{0:T(128)} %pad_add_fusion.where, bf16[128,2048]{1,0:T(8,128)(2,1)} %copy-done.41, bf16[128,2048]{1,0:T(8,128)(2,1)} %collective-permute-done.27.refs_1_, bf16[128,2048]{1,0:T(8,128)(2,1)} %collective-permute-done.28.refs_2_, ...), custom_call_target="tpu_custom_call" | custom-call | flops 6442450944 | bytes 25690112 | tf_op jit(solution)/shard_map/pallas_call | solution.py:139
  238.3 16.0 %shard_map.465 = bf16[2048,2304]{1,0:T(8,128)(2,1)} custom-call(bf16[1024,2048]{1,0:T(8,128)(2,1)} %get-tuple-element.90.refs_0_, bf16[1024,1536]{1,0:T(8,128)(2,1)} %get-tuple-element.72.a.refs_1_, bf16[1024,2048]{1,0:T(8,128)(2,1)} %get-tuple-element.91.refs_2_, bf16[1024,768]{1,0:T(8,128)(2,1)} %get-tuple-element.67.a.refs_3_), custom_call_target="tpu_custom_call" | custom-call | flops 9663676416 | bytes 22544384 | tf_op jit(solution)/shard_map/pallas_call | solution.py:438
  254.3 10.6 %shard_map.457 = bf16[512,2048]{1,0:T(8,128)(2,1)} custom-call(s32[4]{0:T(128)} %add_subtract_fusion.order, bf16[1024,1536]{1,0:T(8,128)(2,1)} %get-tuple-element.72.a.refs_1_, bf16[2048,2304]{1,0:T(8,128)(2,1)} %all-gather.2.cloned.1.call-done.refs_8_.w), custom_call_target="tpu_custom_call" | custom-call | flops 3221225472 | bytes 9961472 | tf_op jit(solution)/shard_map/pallas_call | solution.py:302
  265.0 8.7 %shard_map.455 = bf16[512,2048]{1,0:T(8,128)(2,1)} custom-call(s32[4]{0:T(128)} %add_subtract_fusion.order, bf16[1024,768]{1,0:T(8,128)(2,1)} %get-tuple-element.67.a.refs_3_, bf16[2048,2304]{1,0:T(8,128)(2,1)} %all-gather.2.cloned.1.call-done.refs_8_.w), custom_call_target="tpu_custom_call" | custom-call | flops 1610612736 | bytes 6029312 | tf_op jit(solution)/shard_map/pallas_call | solution.py:302
  275.6 11.0 %shard_map.458 = (bf16[128,2048]{1,0:T(8,128)(2,1)}, bf16[128,2048]{1,0:T(8,128)(2,1)}, bf16[128,2048]{1,0:T(8,128)(2,1)}, bf16[128,2048]{1,0:T(8,128)(2,1)}) custom-call(s32[4]{0:T(128)} %broadcast_add_fusion.order, bf16[1024,1536]{1,0:T(8,128)(2,1)} %get-tuple-element.72.a.refs_1_, bf16[2048,2304]{1,0:T(8,128)(2,1)} %all-gather.2.cloned.1.call-done.refs_8_.w, ...), custom_call_target="tpu_custom_call" | custom-call | flops 3221225472 | bytes 12058624 | tf_op jit(solution)/shard_map/pallas_call | solution.py:302
  291.3 8.9 %shard_map.456 = (bf16[128,2048]{1,0:T(8,128)(2,1)}, bf16[128,2048]{1,0:T(8,128)(2,1)}, bf16[128,2048]{1,0:T(8,128)(2,1)}, bf16[128,2048]{1,0:T(8,128)(2,1)}) custom-call(s32[4]{0:T(128)} %broadcast_add_fusion.order, bf16[1024,768]{1,0:T(8,128)(2,1)} %get-tuple-element.67.a.refs_3_, bf16[2048,2304]{1,0:T(8,128)(2,1)} %all-gather.2.cloned.1.call-done.refs_8_.w, ...), custom_call_target="tpu_custom_call" | custom-call | flops 1610612736 | bytes 8126464 | tf_op jit(solution)/shard_map/pallas_call | solution.py:302
  303.9 9.7 %collective-permute-done.47 = bf16[128,2048]{1,0:T(8,128)(2,1)S(1)} collective-permute-done((bf16[128,2048]{1,0:T(8,128)(2,1)}, bf16[128,2048]{1,0:T(8,128)(2,1)S(1)}, u32[]{:S(2)}, u32[]{:S(2)}) %collective-permute-start.47) | collective-permute-done | bytes 524320 | tf_op jit(solution)/shard_map/ppermute | solution.py:557
  314.1 10.5 %collective-permute-done.42 = bf16[128,2048]{1,0:T(8,128)(2,1)S(1)} collective-permute-done((bf16[128,2048]{1,0:T(8,128)(2,1)}, bf16[128,2048]{1,0:T(8,128)(2,1)S(1)}, u32[]{:S(2)}, u32[]{:S(2)}) %collective-permute-start.42) | collective-permute-done | bytes 524320 | tf_op jit(solution)/shard_map/ppermute | solution.py:557
  324.6 11.4 %collective-permute-done.43 = bf16[128,2048]{1,0:T(8,128)(2,1)S(1)} collective-permute-done((bf16[128,2048]{1,0:T(8,128)(2,1)}, bf16[128,2048]{1,0:T(8,128)(2,1)S(1)}, u32[]{:S(2)}, u32[]{:S(2)}) %collective-permute-start.43) | collective-permute-done | bytes 524320 | tf_op jit(solution)/shard_map/ppermute | solution.py:557
  342.0 10.1 %collective-permute-done.49.refs_1_ = bf16[128,2048]{1,0:T(8,128)(2,1)S(1)} collective-permute-done((bf16[128,2048]{1,0:T(8,128)(2,1)S(1)}, bf16[128,2048]{1,0:T(8,128)(2,1)S(1)}, u32[]{:S(2)}, u32[]{:S(2)}) %collective-permute-start.49) | collective-permute-done | bytes 524320 | tf_op jit(solution)/shard_map/ppermute | solution.py:77
  353.9 9.8 %collective-permute-done.50.refs_2_ = bf16[128,2048]{1,0:T(8,128)(2,1)S(1)} collective-permute-done((bf16[128,2048]{1,0:T(8,128)(2,1)S(1)}, bf16[128,2048]{1,0:T(8,128)(2,1)S(1)}, u32[]{:S(2)}, u32[]{:S(2)}) %collective-permute-start.50) | collective-permute-done | bytes 524320 | tf_op jit(solution)/shard_map/ppermute | solution.py:77
  368.2 6.3 %shard_map.459 = (bf16[1024,2048]{1,0:T(8,128)(2,1)}, bf16[1024,256]{1,0:T(8,128)(2,1)}) custom-call(s32[5]{0:T(128)} %pad_add_fusion.where, bf16[128,2048]{1,0:T(8,128)(2,1)} %copy-done.18, bf16[128,2048]{1,0:T(8,128)(2,1)} %copy-done.47, bf16[128,2048]{1,0:T(8,128)(2,1)} %copy-done.48, bf16[128,2048]{1,0:T(8,128)(2,1)} %copy-done.50, ...), custom_call_target="tpu_custom_call" | custom-call | flops 1073741824 | bytes 9961472 | tf_op jit(solution)/shard_map/pallas_call | solution.py:139
  374.4 10.6 %shard_map.460 = (bf16[1024,256]{1,0:T(8,128)(2,1)}, f32[1024,128]{1,0:T(8,128)}) custom-call(bf16[1024,256]{1,0:T(8,128)(2,1)} %get-tuple-element.59.q, bf16[1024,128]{1,0:T(8,128)(2,1)} %get-tuple-element.60.kv, f32[1024,128]{1,0:T(8,128)} %get-tuple-element.77.lse, bf16[1024,256]{1,0:T(8,128)(2,1)} %get-tuple-element.78.mixed_grad, ...), custom_call_target="tpu_custom_call" | custom-call | flops 8000000000 | bytes 4194304 | tf_op jit(solution)/shard_map/pallas_call | solution.py:406
  391.8 8.7 %shard_map.461 = (bf16[512,2048]{1,0:T(8,128)(2,1)}, f32[1,2048]{1,0:T(1,128)}) custom-call(s32[4]{0:T(128)} %add_subtract_fusion.order, bf16[1024,384]{1,0:T(8,128)(2,1)} %pad_maximum_fusion.1.a.refs_1_, bf16[2048,384]{1,0:T(8,128)(2,1)} %bitcast.174, bf16[1024,2048]{1,0:T(8,128)(2,1)} %get-tuple-element.81.refs_0_.refs_1_), custom_call_target="tpu_custom_call" | custom-call | flops 805306368 | bytes 4063232 | tf_op jit(solution)/shard_map/pallas_call | solution.py:302
  409.1 7.3 %shard_map.464 = bf16[2048,256]{1,0:T(8,128)(2,1)} custom-call(bf16[1024,2048]{1,0:T(8,128)(2,1)} %get-tuple-element.89.refs_0_, bf16[1024,256]{1,0:T(8,128)(2,1)} %get-tuple-element.61.a.refs_1_), custom_call_target="tpu_custom_call" | custom-call | flops 1073741824 | bytes 5767168 | tf_op jit(solution)/shard_map/pallas_call | solution.py:438
  419.2 5.5 %collective-permute-start.71 = (bf16[4,128,256]{1,2,0:T(8,128)(2,1)}, bf16[4,128,256]{1,2,0:T(8,128)(2,1)}, u32[]{:S(2)}, u32[]{:S(2)}) collective-permute-start(bf16[4,128,256]{1,2,0:T(8,128)(2,1)} %bitcast.69), channel_id=1, source_target_pairs={{0,32},{32,64},{64,96},{96,0},{1,33},{33,65},{65,97},{97,1},{2,34}... | collective-permute-start | bytes 786440 | tf_op jit(solution)/shard_map/ppermute | solution.py:94
  428.2 8.0 %shard_map.463 = bf16[2048,384]{1,0:T(8,128)(2,1)} custom-call(bf16[1024,2048]{1,0:T(8,128)(2,1)} %get-tuple-element.81.refs_0_.refs_1_, bf16[1024,384]{1,0:T(8,128)(2,1)} %pad_maximum_fusion.1.a.refs_1_), custom_call_target="tpu_custom_call" | custom-call | flops 1610612736 | bytes 6553600 | tf_op jit(solution)/shard_map/pallas_call | solution.py:438
  438.8 8.9 %shard_map.462 = (bf16[128,2048]{1,0:T(8,128)(2,1)}, bf16[128,2048]{1,0:T(8,128)(2,1)}, bf16[128,2048]{1,0:T(8,128)(2,1)}, bf16[128,2048]{1,0:T(8,128)(2,1)}, f32[1,2048]{1,0:T(1,128)}) custom-call(s32[4]{0:T(128)} %broadcast_add_fusion.order, bf16[1024,384]{1,0:T(8,128)(2,1)} %pad_maximum_fusion.1.a.refs_1_, bf16[2048,384]{1,0:T(8,128)(2,1)} %bitcast.175, ...), custom_call_target="tpu_custom_call" | custom-call | flops 805306368 | bytes 6160384 | tf_op jit(solution)/shard_map/pallas_call | solution.py:302
  457.9 13.5 %collective-permute-done.61 = bf16[4,128,384]{2,1,0:T(8,128)(2,1)} collective-permute-done((bf16[4,128,384]{2,1,0:T(8,128)(2,1)}, bf16[4,128,384]{2,1,0:T(8,128)(2,1)}, u32[]{:S(2)}, u32[]{:S(2)}) %collective-permute-start.61) | collective-permute-done | bytes 393248 | tf_op jit(solution)/shard_map/ppermute | solution.py:94
  485.9 18.0 %collective-permute-done.67 = f32[32,128]{1,0:T(8,128)S(1)} collective-permute-done((f32[32,128]{1,0:T(8,128)S(1)}, f32[32,128]{1,0:T(8,128)S(1)}, u32[]{:S(2)}, u32[]{:S(2)}) %collective-permute-start.67) | collective-permute-done | bytes 16416 | tf_op jit(solution)/shard_map/ppermute | solution.py:631
  (497 shorter events, 198.1 us)
Async XLA Ops:
  7.2 206.7 %all-gather.2.cloned.1.call-start = ((), (), s32[]{:S(2)}) async-start(), calls=%async_computation.1 | async-start | bytes 10027008 | tf_op jit(solution)/shard_map/all_gather | solution.py:541
  25.2 507.6 %reduce-scatter.2.cloned.1.call-start = ((), (), s32[]{:S(2)}) async-start(), calls=%async_computation.2 | async-start | bytes 10027008 | tf_op jit(solution)/shard_map/reduce_scatter | solution.py:577
  25.2 41.4 %collective-permute-start = (bf16[128,2048]{1,0:T(8,128)(2,1)S(1)}, bf16[128,2048]{1,0:T(8,128)(2,1)}, u32[]{:S(2)}, u32[]{:S(2)}) collective-permute-start(bf16[128,2048]{1,0:T(8,128)(2,1)S(1)} %bitcast.180), channel_id=1, source_target_pairs={{0,2},{2,4},{4,6},{6,0},{1,3},{3,5},{5,7},{7,1},{8,10},{10,12},{12... | collective-permute-start | bytes 1572872 | tf_op jit(solution)/shard_map/ppermute | solution.py:77
  25.4 42.5 %collective-permute-start.1 = (bf16[128,2048]{1,0:T(8,128)(2,1)S(1)}, bf16[128,2048]{1,0:T(8,128)(2,1)}, u32[]{:S(2)}, u32[]{:S(2)}) collective-permute-start(bf16[128,2048]{1,0:T(8,128)(2,1)S(1)} %bitcast.181), channel_id=1, source_target_pairs={{0,4},{2,6},{4,0},{6,2},{1,5},{3,7},{5,1},{7,3},{8,12},{10,14},{12... | collective-permute-start | bytes 1572872 | tf_op jit(solution)/shard_map/ppermute | solution.py:77
  66.6 25.8 %collective-permute-start.3 = (bf16[128,2048]{1,0:T(8,128)(2,1)S(1)}, bf16[128,2048]{1,0:T(8,128)(2,1)S(1)}, u32[]{:S(2)}, u32[]{:S(2)}) collective-permute-start(bf16[128,2048]{1,0:T(8,128)(2,1)S(1)} %bitcast.183), channel_id=1, source_target_pairs={{0,1},{1,0},{2,3},{3,2},{4,5},{5,4},{6,7},{7,6},{8,9},{9,8},{10,11... | collective-permute-start | bytes 1572872 | tf_op jit(solution)/shard_map/ppermute | solution.py:73
  67.9 24.4 %collective-permute-start.16 = (bf16[4,128,384]{2,1,0:T(8,128)(2,1)S(1)}, bf16[4,128,384]{2,1,0:T(8,128)(2,1)S(1)}, u32[]{:S(2)}, u32[]{:S(2)}) collective-permute-start(bf16[4,128,384]{2,1,0:T(8,128)(2,1)S(1)} %bitcast_dynamic-update-slice_fusion.8), channel_id=1, source_target_pairs={{0,64},{32,96},{64,0},{96,32},{1,65},{33,97},{65,1},{97,33},{2,66}... | collective-permute-start | bytes 1179656 | tf_op jit(solution)/shard_map/ppermute | solution.py:85
  124.7 37.2 %collective-permute-start.34 = (bf16[128,2048]{1,0:T(8,128)(2,1)S(1)}, bf16[128,2048]{1,0:T(8,128)(2,1)S(1)}, u32[]{:S(2)}, u32[]{:S(2)}) collective-permute-start(bf16[128,2048]{1,0:T(8,128)(2,1)S(1)} %bitcast.189), channel_id=1, source_target_pairs={{0,2},{2,4},{4,6},{6,0},{1,3},{3,5},{5,7},{7,1},{8,10},{10,12},{12... | collective-permute-start | bytes 1572872 | tf_op jit(solution)/shard_map/ppermute | solution.py:77
  124.7 37.2 %collective-permute-start.35 = (bf16[128,2048]{1,0:T(8,128)(2,1)S(1)}, bf16[128,2048]{1,0:T(8,128)(2,1)S(1)}, u32[]{:S(2)}, u32[]{:S(2)}) collective-permute-start(bf16[128,2048]{1,0:T(8,128)(2,1)S(1)} %bitcast.190), channel_id=1, source_target_pairs={{0,4},{2,6},{4,0},{6,2},{1,5},{3,7},{5,1},{7,3},{8,12},{10,14},{12... | collective-permute-start | bytes 1572872 | tf_op jit(solution)/shard_map/ppermute | solution.py:77
  137.8 25.6 %collective-permute-start.24 = (bf16[128,2048]{1,0:T(8,128)(2,1)}, bf16[128,2048]{1,0:T(8,128)(2,1)S(1)}, u32[]{:S(2)}, u32[]{:S(2)}) collective-permute-start(bf16[128,2048]{1,0:T(8,128)(2,1)} %get-tuple-element.63), channel_id=1, source_target_pairs={{0,4},{2,6},{4,0},{6,2},{1,5},{3,7},{5,1},{7,3},{8,12},{10,14},{12... | collective-permute-start | bytes 1572872 | tf_op jit(solution)/shard_map/ppermute | solution.py:557
  137.8 35.3 %collective-permute-start.25 = (bf16[128,2048]{1,0:T(8,128)(2,1)}, bf16[128,2048]{1,0:T(8,128)(2,1)S(1)}, u32[]{:S(2)}, u32[]{:S(2)}) collective-permute-start(bf16[128,2048]{1,0:T(8,128)(2,1)} %get-tuple-element.64), channel_id=1, source_target_pairs={{0,2},{2,4},{4,6},{6,0},{1,3},{3,5},{5,7},{7,1},{8,10},{10,12},{12... | collective-permute-start | bytes 1572872 | tf_op jit(solution)/shard_map/ppermute | solution.py:557
  137.9 46.1 %collective-permute-start.26 = (bf16[128,2048]{1,0:T(8,128)(2,1)}, bf16[128,2048]{1,0:T(8,128)(2,1)S(1)}, u32[]{:S(2)}, u32[]{:S(2)}) collective-permute-start(bf16[128,2048]{1,0:T(8,128)(2,1)} %get-tuple-element.65), channel_id=1, source_target_pairs={{0,6},{2,0},{4,2},{6,4},{1,7},{3,1},{5,3},{7,5},{8,14},{10,8},{12,... | collective-permute-start | bytes 1572872 | tf_op jit(solution)/shard_map/ppermute | solution.py:557
  161.9 24.5 %collective-permute-start.36 = (bf16[128,2048]{1,0:T(8,128)(2,1)S(1)}, bf16[128,2048]{1,0:T(8,128)(2,1)S(1)}, u32[]{:S(2)}, u32[]{:S(2)}) collective-permute-start(bf16[128,2048]{1,0:T(8,128)(2,1)S(1)} %bitcast.191), channel_id=1, source_target_pairs={{0,6},{2,0},{4,2},{6,4},{1,7},{3,1},{5,3},{7,5},{8,14},{10,8},{12,... | collective-permute-start | bytes 1572872 | tf_op jit(solution)/shard_map/ppermute | solution.py:77
  161.9 25.0 %collective-permute-start.37 = (bf16[128,2048]{1,0:T(8,128)(2,1)S(1)}, bf16[128,2048]{1,0:T(8,128)(2,1)S(1)}, u32[]{:S(2)}, u32[]{:S(2)}) collective-permute-start(bf16[128,2048]{1,0:T(8,128)(2,1)S(1)} %bitcast.192), channel_id=1, source_target_pairs={{0,1},{1,0},{2,3},{3,2},{4,5},{5,4},{6,7},{7,6},{8,9},{9,8},{10,11... | collective-permute-start | bytes 1572872 | tf_op jit(solution)/shard_map/ppermute | solution.py:73
  163.3 25.8 %collective-permute-start.38 = (bf16[128,2048]{1,0:T(8,128)(2,1)S(1)}, bf16[128,2048]{1,0:T(8,128)(2,1)S(1)}, u32[]{:S(2)}, u32[]{:S(2)}) collective-permute-start(bf16[128,2048]{1,0:T(8,128)(2,1)S(1)} %collective-permute-done.34.refs_1_), channel_id=1, source_target_pairs={{0,1},{1,0},{2,3},{3,2},{4,5},{5,4},{6,7},{7,6},{8,9},{9,8},{10,11... | collective-permute-start | bytes 1572872 | tf_op jit(solution)/shard_map/ppermute | solution.py:73
  186.3 26.1 %collective-permute-start.27 = (bf16[128,2048]{1,0:T(8,128)(2,1)S(1)}, bf16[128,2048]{1,0:T(8,128)(2,1)}, u32[]{:S(2)}, u32[]{:S(2)}) collective-permute-start(bf16[128,2048]{1,0:T(8,128)(2,1)S(1)} %multiply_convert_fusion.refs_0_), channel_id=1, source_target_pairs={{0,2},{2,4},{4,6},{6,0},{1,3},{3,5},{5,7},{7,1},{8,10},{10,12},{12... | collective-permute-start | bytes 1572872 | tf_op jit(solution)/shard_map/ppermute | solution.py:77
  186.4 26.9 %collective-permute-start.28 = (bf16[128,2048]{1,0:T(8,128)(2,1)S(1)}, bf16[128,2048]{1,0:T(8,128)(2,1)}, u32[]{:S(2)}, u32[]{:S(2)}) collective-permute-start(bf16[128,2048]{1,0:T(8,128)(2,1)S(1)} %multiply_convert_fusion.refs_0_), channel_id=1, source_target_pairs={{0,4},{2,6},{4,0},{6,2},{1,5},{3,7},{5,1},{7,3},{8,12},{10,14},{12... | collective-permute-start | bytes 1572872 | tf_op jit(solution)/shard_map/ppermute | solution.py:77
  186.9 26.3 %collective-permute-start.29 = (bf16[128,2048]{1,0:T(8,128)(2,1)S(1)}, bf16[128,2048]{1,0:T(8,128)(2,1)}, u32[]{:S(2)}, u32[]{:S(2)}) collective-permute-start(bf16[128,2048]{1,0:T(8,128)(2,1)S(1)} %multiply_convert_fusion.refs_0_), channel_id=1, source_target_pairs={{0,6},{2,0},{4,2},{6,4},{1,7},{3,1},{5,3},{7,5},{8,14},{10,8},{12,... | collective-permute-start | bytes 1572872 | tf_op jit(solution)/shard_map/ppermute | solution.py:77
  189.1 24.8 %collective-permute-start.40 = (bf16[128,2048]{1,0:T(8,128)(2,1)S(1)}, bf16[128,2048]{1,0:T(8,128)(2,1)S(1)}, u32[]{:S(2)}, u32[]{:S(2)}) collective-permute-start(bf16[128,2048]{1,0:T(8,128)(2,1)S(1)} %collective-permute-done.36.refs_3_), channel_id=1, source_target_pairs={{0,1},{1,0},{2,3},{3,2},{4,5},{5,4},{6,7},{7,6},{8,9},{9,8},{10,11... | collective-permute-start | bytes 1572872 | tf_op jit(solution)/shard_map/ppermute | solution.py:73
  189.7 33.9 %collective-permute-start.30 = (bf16[128,2048]{1,0:T(8,128)(2,1)S(1)}, bf16[128,2048]{1,0:T(8,128)(2,1)S(1)}, u32[]{:S(2)}, u32[]{:S(2)}) collective-permute-start(bf16[128,2048]{1,0:T(8,128)(2,1)S(1)} %multiply_convert_fusion.refs_0_), channel_id=1, source_target_pairs={{0,1},{1,0},{2,3},{3,2},{4,5},{5,4},{6,7},{7,6},{8,9},{9,8},{10,11... | collective-permute-start | bytes 1572872 | tf_op jit(solution)/shard_map/ppermute | solution.py:73
  287.4 26.3 %collective-permute-start.47 = (bf16[128,2048]{1,0:T(8,128)(2,1)}, bf16[128,2048]{1,0:T(8,128)(2,1)S(1)}, u32[]{:S(2)}, u32[]{:S(2)}) collective-permute-start(bf16[128,2048]{1,0:T(8,128)(2,1)} %get-tuple-element.75), channel_id=1, source_target_pairs={{0,2},{2,4},{4,6},{6,0},{1,3},{3,5},{5,7},{7,1},{8,10},{10,12},{12... | collective-permute-start | bytes 1572872 | tf_op jit(solution)/shard_map/ppermute | solution.py:557
  289.2 24.4 %collective-permute-start.48 = (bf16[128,2048]{1,0:T(8,128)(2,1)}, bf16[128,2048]{1,0:T(8,128)(2,1)S(1)}, u32[]{:S(2)}, u32[]{:S(2)}) collective-permute-start(bf16[128,2048]{1,0:T(8,128)(2,1)} %get-tuple-element.76), channel_id=1, source_target_pairs={{0,6},{2,0},{4,2},{6,4},{1,7},{3,1},{5,3},{7,5},{8,14},{10,8},{12,... | collective-permute-start | bytes 1572872 | tf_op jit(solution)/shard_map/ppermute | solution.py:557
  301.2 34.8 %collective-permute-start.43 = (bf16[128,2048]{1,0:T(8,128)(2,1)}, bf16[128,2048]{1,0:T(8,128)(2,1)S(1)}, u32[]{:S(2)}, u32[]{:S(2)}) collective-permute-start(bf16[128,2048]{1,0:T(8,128)(2,1)} %get-tuple-element.70), channel_id=1, source_target_pairs={{0,2},{2,4},{4,6},{6,0},{1,3},{3,5},{5,7},{7,1},{8,10},{10,12},{12... | collective-permute-start | bytes 1572872 | tf_op jit(solution)/shard_map/ppermute | solution.py:557
  302.1 33.9 %collective-permute-start.44 = (bf16[128,2048]{1,0:T(8,128)(2,1)}, bf16[128,2048]{1,0:T(8,128)(2,1)S(1)}, u32[]{:S(2)}, u32[]{:S(2)}) collective-permute-start(bf16[128,2048]{1,0:T(8,128)(2,1)} %get-tuple-element.71), channel_id=1, source_target_pairs={{0,6},{2,0},{4,2},{6,4},{1,7},{3,1},{5,3},{7,5},{8,14},{10,8},{12,... | collective-permute-start | bytes 1572872 | tf_op jit(solution)/shard_map/ppermute | solution.py:557
  337.8 25.9 %collective-permute-start.50 = (bf16[128,2048]{1,0:T(8,128)(2,1)S(1)}, bf16[128,2048]{1,0:T(8,128)(2,1)S(1)}, u32[]{:S(2)}, u32[]{:S(2)}) collective-permute-start(bf16[128,2048]{1,0:T(8,128)(2,1)S(1)} %get-tuple-element.252.refs_0_), channel_id=1, source_target_pairs={{0,4},{2,6},{4,0},{6,2},{1,5},{3,7},{5,1},{7,3},{8,12},{10,14},{12... | collective-permute-start | bytes 1572872 | tf_op jit(solution)/shard_map/ppermute | solution.py:77
  340.9 24.7 %collective-permute-start.52 = (bf16[128,2048]{1,0:T(8,128)(2,1)S(1)}, bf16[128,2048]{1,0:T(8,128)(2,1)S(1)}, u32[]{:S(2)}, u32[]{:S(2)}) collective-permute-start(bf16[128,2048]{1,0:T(8,128)(2,1)S(1)} %get-tuple-element.252.refs_0_), channel_id=1, source_target_pairs={{0,1},{1,0},{2,3},{3,2},{4,5},{5,4},{6,7},{7,6},{8,9},{9,8},{10,11... | collective-permute-start | bytes 1572872 | tf_op jit(solution)/shard_map/ppermute | solution.py:73
  400.6 38.2 %collective-permute-start.57 = (bf16[512,2048]{1,0:T(8,128)(2,1)}, bf16[512,2048]{1,0:T(8,128)(2,1)}, u32[]{:S(2)}, u32[]{:S(2)}) collective-permute-start(bf16[512,2048]{1,0:T(8,128)(2,1)} %get-tuple-element.82), channel_id=1, source_target_pairs={{0,1},{1,0},{2,3},{3,2},{4,5},{5,4},{6,7},{7,6},{8,9},{9,8},{10,11... | collective-permute-start | bytes 6291464 | tf_op jit(solution)/shard_map/ppermute | solution.py:73
  419.2 35.0 %collective-permute-start.71 = (bf16[4,128,256]{1,2,0:T(8,128)(2,1)}, bf16[4,128,256]{1,2,0:T(8,128)(2,1)}, u32[]{:S(2)}, u32[]{:S(2)}) collective-permute-start(bf16[4,128,256]{1,2,0:T(8,128)(2,1)} %bitcast.69), channel_id=1, source_target_pairs={{0,32},{32,64},{64,96},{96,0},{1,33},{33,65},{65,97},{97,1},{2,34}... | collective-permute-start | bytes 786440 | tf_op jit(solution)/shard_map/ppermute | solution.py:94
  425.6 30.9 %collective-permute-start.72 = (bf16[4,128,256]{1,2,0:T(8,128)(2,1)}, bf16[4,128,256]{1,2,0:T(8,128)(2,1)}, u32[]{:S(2)}, u32[]{:S(2)}) collective-permute-start(bf16[4,128,256]{1,2,0:T(8,128)(2,1)} %bitcast.70), channel_id=1, source_target_pairs={{0,96},{32,0},{64,32},{96,64},{1,97},{33,1},{65,33},{97,65},{2,98}... | collective-permute-start | bytes 786440 | tf_op jit(solution)/shard_map/ppermute | solution.py:94
  426.4 30.1 %collective-permute-start.73 = (bf16[4,128,256]{1,2,0:T(8,128)(2,1)}, bf16[4,128,256]{1,2,0:T(8,128)(2,1)}, u32[]{:S(2)}, u32[]{:S(2)}) collective-permute-start(bf16[4,128,256]{1,2,0:T(8,128)(2,1)} %bitcast.71), channel_id=1, source_target_pairs={{0,64},{32,96},{64,0},{96,32},{1,65},{33,97},{65,1},{97,33},{2,66}... | collective-permute-start | bytes 786440 | tf_op jit(solution)/shard_map/ppermute | solution.py:94
  478.5 43.6 %collective-permute-start.58 = (bf16[128,2048]{1,0:T(8,128)(2,1)}, bf16[128,2048]{1,0:T(8,128)(2,1)S(1)}, u32[]{:S(2)}, u32[]{:S(2)}) collective-permute-start(bf16[128,2048]{1,0:T(8,128)(2,1)} %get-tuple-element.84), channel_id=1, source_target_pairs={{0,4},{2,6},{4,0},{6,2},{1,5},{3,7},{5,1},{7,3},{8,12},{10,14},{12... | collective-permute-start | bytes 1572872 | tf_op jit(solution)/shard_map/ppermute | solution.py:557
  481.4 40.7 %collective-permute-start.59 = (bf16[128,2048]{1,0:T(8,128)(2,1)}, bf16[128,2048]{1,0:T(8,128)(2,1)S(1)}, u32[]{:S(2)}, u32[]{:S(2)}) collective-permute-start(bf16[128,2048]{1,0:T(8,128)(2,1)} %get-tuple-element.85), channel_id=1, source_target_pairs={{0,2},{2,4},{4,6},{6,0},{1,3},{3,5},{5,7},{7,1},{8,10},{10,12},{12... | collective-permute-start | bytes 1572872 | tf_op jit(solution)/shard_map/ppermute | solution.py:557
  481.7 40.4 %collective-permute-start.60 = (bf16[128,2048]{1,0:T(8,128)(2,1)}, bf16[128,2048]{1,0:T(8,128)(2,1)}, u32[]{:S(2)}, u32[]{:S(2)}) collective-permute-start(bf16[128,2048]{1,0:T(8,128)(2,1)} %get-tuple-element.86), channel_id=1, source_target_pairs={{0,6},{2,0},{4,2},{6,4},{1,7},{3,1},{5,3},{7,5},{8,14},{10,8},{12,... | collective-permute-start | bytes 1572872 | tf_op jit(solution)/shard_map/ppermute | solution.py:557
  (144 other events, 1428.7 us)
Sparse Core Ops, SparseCore 0:
  25.3 96.4 all-gather.1
  254.5 86.8 reduce-scatter.1

commit v2 on v1

v2 whole, which is shorter than its diff:
```python
import functools

import jax
import jax.numpy as jnp
from jax import lax
from jax.experimental import pallas as pl
from jax.experimental.pallas import tpu as pltpu
from jax.sharding import Mesh
from jax.sharding import PartitionSpec as P

D = 2048
HEADS = 32
KV_HEADS = 4
HD = 64
FF = 5632
SEQ_LEN = 1024
STEP = 10

EPS = 1e-05
BETA_ONE = 0.9
BETA_TWO = 0.95
ADAM_EPS = 1e-08
DECAY = 0.1

ROWS = 128
HID = FF // 8
TILES = 6
PAD = TILES * 128
QW = 256
AW = 384
BF = jnp.bfloat16
F32 = jnp.float32
MIB = 2**20


def params(limit=56, **more):
    return pltpu.CompilerParams(vmem_limit_bytes=limit * MIB, **more)


def cost(flops, nbytes, trans=0):
    return pl.CostEstimate(flops=int(flops), bytes_accessed=int(nbytes), transcendentals=int(trans))


def dot(left, right):
    return jnp.dot(left, right, preferred_element_type=F32)


def dot_cols(left, right):
    return lax.dot_general(left, right, (((1,), (1,)), ((), ())), preferred_element_type=F32)


def dot_rows(left, right):
    return lax.dot_general(left, right, (((0,), (0,)), ((), ())), preferred_element_type=F32)


def swap_halves(v):
    width = v.shape[-1]
    lane = lax.broadcasted_iota(jnp.int32, v.shape, v.ndim - 1)
    return jnp.where(
        lane % HD < HD // 2,
        pltpu.roll(v, width - HD // 2, v.ndim - 1),
        pltpu.roll(v, HD // 2, v.ndim - 1),
    )


def ring(axis, k):
    return functools.partial(
        lax.ppermute, axis_name=axis, perm=[(i, (i + k) % 4) for i in range(4)]
    )


def other_core(v):
    return lax.ppermute(v, "core", [(0, 1), (1, 0)])


def spread_z(v):
    return [v, ring("z", 1)(v), ring("z", 2)(v), ring("z", 3)(v)]


def spread(v):
    own = spread_z(v)
    return own + [other_core(t) for t in own]


def came(v, axis):
    return [v] + [ring(axis, k)(v) for k in (1, 2, 3)]


def swap_blocks(v, axes):
    return lax.all_to_all(v, axes, split_axis=0, concat_axis=0, tiled=True)


ANY = pl.BlockSpec(memory_space=pl.ANY)
HELD = [pltpu.VMEM((4, 2 * ROWS, D), BF), pltpu.SemaphoreType.DMA((8,))]


def load_blocks(halves, blocks, held, sems):
    step = pl.program_id(0)

    def copy(i, k, half, source):
        return pltpu.make_async_copy(
            source, held.at[k, pl.ds(pl.multiple_of(half * ROWS, ROWS), ROWS)], sems.at[i]
        )

    @pl.when(step == 0)
    def _():
        for k in range(4):
            copy(k, k, halves[0], blocks[k]).start()
            copy(4 + k, k, halves[1], blocks[4 + k]).start()

    copy(step, step, halves[0], blocks[0]).wait()
    copy(4 + step, step, halves[1], blocks[4]).wait()
    return held.at[step]


def by_block(width):
    return pl.BlockSpec((2 * ROWS, width), lambda i, where: (where[i], 0))


def by_step(width):
    return pl.BlockSpec((ROWS, width), lambda i, *_: (i, 0))


def whole(*shape):
    return pl.BlockSpec(shape, lambda i, *_: (0,) * len(shape))


def shape_of(shape, kind=BF):
    return jax.ShapeDtypeStruct(shape, kind)


def blocks_call(
    kernel, where, blocks, operands, in_specs, out_specs, outs, flops, behind=(), through=(), scratch=None
):
    n_in, n_out, n_more = 8 + len(operands), len(outs), len(behind) + len(through)

    def body(where, *refs):
        refs = list(refs)
        del refs[n_in + n_more + n_out : n_in + n_more + n_out + len(through)]
        del refs[n_in : n_in + n_more]
        kernel(where, *refs)

    nbytes = 4 * MIB + sum(o.size * o.dtype.itemsize for o in outs)
    nbytes += sum(o.size * o.dtype.itemsize for o in operands)
    first = 1 + n_in + len(behind)
    return pl.pallas_call(
        body,
        grid_spec=pltpu.PrefetchScalarGridSpec(
            num_scalar_prefetch=1,
            grid=(4,),
            in_specs=[ANY] * 8 + in_specs + [ANY] * n_more,
            out_specs=out_specs + [ANY] * len(through),
            scratch_shapes=scratch or HELD,
        ),
        out_shape=outs + [shape_of(v.shape, v.dtype) for v in through],
        input_output_aliases={first + i: n_out + i for i in range(len(through))},
        compiler_params=params(),
        cost_estimate=cost(flops, nbytes),
        name=kernel.__name__,
    )(where, *blocks, *operands, *behind, *through)


def assemble_call(axis, pieces, behind=()):
    order = ((lax.axis_index(axis) - jnp.arange(4)) % 4).astype(jnp.int32)

    def assemble_kernel(order, *refs):
        for k in range(4):
            refs[-1][order[k]] = refs[k][...]

    shape = pieces[0].shape
    return pl.pallas_call(
        assemble_kernel,
        grid_spec=pltpu.PrefetchScalarGridSpec(
            num_scalar_prefetch=1,
            grid=(1,),
            in_specs=[whole(*shape)] * 4 + [ANY] * len(behind),
            out_specs=whole(4, *shape),
        ),
        out_shape=shape_of((4,) + shape, pieces[0].dtype),
        compiler_params=params(),
        cost_estimate=cost(0, 16 * pieces[0].size),
        name="assemble_kernel",
    )(order, *pieces, *behind)


def weights_kernel(order, *refs):
    for k in range(4):
        rows = pl.ds(pl.multiple_of(order[k] * 512, 512), 512)
        piece = refs[k][...].reshape(512, AW + QW)
        refs[4][rows] = piece[:, :AW]
        refs[5][rows] = piece[:, AW:]


def weights_call(pieces):
    order = ((lax.axis_index("y") - jnp.arange(4)) % 4).astype(jnp.int32)
    return pl.pallas_call(
        weights_kernel,
        grid_spec=pltpu.PrefetchScalarGridSpec(
            num_scalar_prefetch=1,
            grid=(1,),
            in_specs=[whole(*pieces[0].shape)] * 4,
            out_specs=[whole(D, AW), whole(D, QW)],
        ),
        out_shape=[shape_of((D, AW)), shape_of((D, QW))],
        compiler_params=params(),
        cost_estimate=cost(0, 5 * MIB),
        name="weights_kernel",
    )(order, *pieces)


def attend_weights_kernel(kvg, query, mixed, out):
    gain = kvg[:, 128:129].astype(F32)
    out[:, :QW] = (query[...].astype(BF).astype(F32) * gain).astype(BF)
    out[:, QW:AW] = (kvg[:, :128].astype(F32) * gain).astype(BF)
    out[:, AW:] = mixed[...].T.astype(BF)


def attend_weights_call(kvg, query, mixed):
    return pl.pallas_call(
        attend_weights_kernel,
        out_shape=shape_of((ROWS, AW + QW)),
        compiler_params=params(),
        cost_estimate=cost(0, MIB),
        name="attend_weights_kernel",
    )(kvg, query, mixed)


def ffn_weights_kernel(kvg, gate, up, down, *refs):
    out = refs[-1]
    gain = kvg[:, 129:130].astype(F32)
    for j in range(TILES):
        n = min(128, HID - 128 * j)
        for s, ref in enumerate((gate, up, down)):
            part = ref[128 * j : 128 * j + n]
            if n < 128:
                part = jnp.concatenate([part, jnp.zeros((128 - n, 128), F32)], axis=0)
            part = part.T.astype(BF)
            if s < 2:
                part = (part.astype(F32) * gain).astype(BF)
            at = 2 * PAD + 128 * j if s == 2 else 256 * j + 128 * s
            out[:, at : at + 128] = part


def ffn_weights_call(kvg, gate, up, down, behind):
    vmem = pl.BlockSpec(memory_space=pltpu.VMEM)
    return pl.pallas_call(
        ffn_weights_kernel,
        in_specs=[vmem] * 4 + [ANY] * len(behind),
        out_specs=vmem,
        out_shape=shape_of((ROWS, 3 * PAD)),
        compiler_params=params(),
        cost_estimate=cost(0, 2 * MIB),
        name="ffn_weights_kernel",
    )(kvg, gate, up, down, *behind)


def norm_back_kernel(n_through, *refs):
    parts, (x, base), outs = refs[:4], refs[4:6], refs[6 + n_through : len(refs) - n_through]
    v = x[...].astype(F32)
    inv = lax.rsqrt(jnp.mean(v * v, axis=-1, keepdims=True) + EPS)
    unit = v * inv
    u = functools.reduce(jnp.add, [ref[...].astype(F32) for ref in parts])
    out = base[...].astype(F32) + inv * (u - unit * jnp.mean(u * unit, axis=-1, keepdims=True))
    for ref in outs:
        ref[...] = out.astype(ref.dtype)


def norm_back_call(parts, x, base, kinds, through=()):
    vmem = pl.BlockSpec(memory_space=pltpu.VMEM)
    return pl.pallas_call(
        functools.partial(norm_back_kernel, len(through)),
        in_specs=[vmem] * 6 + [ANY] * len(through),
        out_specs=[vmem] * len(kinds) + [ANY] * len(through),
        out_shape=[shape_of((ROWS, D), kind) for kind in kinds]
        + [shape_of(v.shape, v.dtype) for v in through],
        input_output_aliases={6 + i: len(kinds) + i for i in range(len(through))},
        compiler_params=params(),
        cost_estimate=cost(0, 5 * MIB),
        name="norm_back_kernel",
    )(*parts, x, base, *through)


def first_kernel(where, *refs):
    blocks, (w, tcos, tsin, all_out, q_out, kv_out, inv_out, held, sems) = refs[:8], refs[8:]
    x = load_blocks((where[4], 1 - where[4]), blocks, held, sems)[...]
    all_out[...] = x
    y = dot(x, w[...])
    x = x.astype(F32)
    inv = lax.rsqrt(jnp.mean(x * x, axis=-1, keepdims=True) + EPS)
    inv_out[...] = jnp.broadcast_to(inv, inv_out.shape)
    cos, sin = tcos[...] * inv, tsin[...] * inv
    for j in range(2):
        part = y[:, j * 128 : (j + 1) * 128]
        q_out[:, j * 128 : (j + 1) * 128] = (part * cos + swap_halves(part) * sin).astype(BF)
    part = y[:, 256:384]
    is_key = lax.broadcasted_iota(jnp.int32, part.shape, 1) < HD
    kv_out[...] = jnp.where(is_key, part * cos + swap_halves(part) * sin, part * inv).astype(BF)


def first_call(where, blocks, w, tcos, tsin, behind):
    return blocks_call(
        first_kernel,
        where,
        blocks,
        (w, tcos, tsin),
        [pl.BlockSpec((D, AW), lambda i, *_: (0, 0)), by_block(128), by_block(128)],
        [by_block(D), by_block(QW), by_block(128), by_block(128)],
        [
            shape_of((SEQ_LEN, D)),
            shape_of((SEQ_LEN, QW)),
            shape_of((SEQ_LEN, 128)),
            shape_of((SEQ_LEN, 128), F32),
        ],
        2 * SEQ_LEN * D * AW,
        behind,
    )


def put_halves(outs, value, cols=slice(None)):
    outs[0][:, cols] = value[:ROWS]
    outs[1][:, cols] = value[ROWS:]


def middle_kernel(where, *refs):
    blocks, grad_blocks, (w, *refs) = refs[:8], refs[8:16], refs[16:]
    hiddens, grads, (held, sems, grad_held, grad_sems) = refs[:2], refs[2:4], refs[4:]
    x = load_blocks((0, 1), blocks, held, sems)[...]
    c = load_blocks((0, 1), grad_blocks, grad_held, grad_sems)[...]
    for j in range(TILES // 2):
        backs = dot(c, w[:, 2 * PAD + 256 * j : 2 * PAD + 256 * (j + 1)])
        for i in range(2):
            t = 2 * j + i
            y = dot(x, w[:, 256 * t : 256 * (t + 1)])
            gate, up, back = y[:, :128], y[:, 128:], backs[:, 128 * i : 128 * (i + 1)]
            sigma = jax.nn.sigmoid(gate)
            swish = gate * sigma
            put_halves(hiddens, (swish * up).astype(BF), slice(128 * t, 128 * (t + 1)))
            g = (back * up * (sigma * (1.0 + gate * (1.0 - sigma)))).astype(BF)
            put_halves(grads, g, slice(256 * t, 256 * t + 128))
            put_halves(grads, (back * swish).astype(BF), slice(256 * t + 128, 256 * (t + 1)))


def middle_call(where, blocks, grad_blocks, w):
    return blocks_call(
        middle_kernel,
        where,
        blocks,
        (*grad_blocks, w),
        [ANY] * 8 + [whole(D, 3 * PAD)],
        [by_step(PAD)] * 2 + [by_step(2 * PAD)] * 2,
        [shape_of((4 * ROWS, PAD))] * 2 + [shape_of((4 * ROWS, 2 * PAD))] * 2,
        2 * SEQ_LEN * D * 3 * PAD,
        scratch=HELD * 2,
    )


def mixed_grad_kernel(where, *refs):
    blocks, (w, all_out, grad_out, held, sems) = refs[:8], refs[8:]
    x = load_blocks((where[4], 1 - where[4]), blocks, held, sems)[...]
    all_out[...] = x
    grad_out[...] = dot(x, w[...]).astype(BF)


def mixed_grad_call(where, blocks, w):
    return blocks_call(
        mixed_grad_kernel,
        where,
        blocks,
        (w,),
        [whole(D, QW)],
        [by_block(D), by_block(QW)],
        [shape_of((SEQ_LEN, D)), shape_of((SEQ_LEN, QW))],
        2 * SEQ_LEN * D * QW,
    )


def partial_kernel(n_in, n_behind, order, *refs):
    w, across, own = refs[n_in], refs[-2], refs[-1]
    if n_in == 1:
        a = refs[0]
        left = jnp.concatenate(
            [a[pl.ds(pl.multiple_of(order[k] * ROWS, ROWS), ROWS)] for k in range(8)], axis=0
        )
    else:
        left = jnp.concatenate([refs[0][...], refs[1][...]], axis=0)
    y = dot_cols(left, w[...]).astype(BF)
    across[...] = y[: 4 * ROWS]
    own[...] = y[4 * ROWS :]


def partial_call(order, a, w, col, tile, behind=()):
    depth = a[0].shape[1]
    return pl.pallas_call(
        functools.partial(partial_kernel, len(a), len(behind)),
        grid_spec=pltpu.PrefetchScalarGridSpec(
            num_scalar_prefetch=1,
            grid=(D // tile,),
            in_specs=[whole(*v.shape) for v in a]
            + [pl.BlockSpec((tile, depth), lambda i, *_: (i, col))]
            + [ANY] * len(behind),
            out_specs=[pl.BlockSpec((4 * ROWS, tile), lambda i, *_: (0, i))] * 2,
        ),
        out_shape=[shape_of((4 * ROWS, D))] * 2,
        compiler_params=params(),
        cost_estimate=cost(2 * 8 * ROWS * D * depth, 2 * depth * (D + 1024) + 4 * MIB),
        name="partial_kernel",
    )(order, *a, w, *behind)


def add_kernel(n_behind, across, own, *refs):
    for k, ref in enumerate(refs[n_behind:]):
        rows = slice(k * ROWS, (k + 1) * ROWS)
        ref[...] = (across[rows].astype(F32) + own[rows].astype(F32)).astype(BF)


def add_call(across, own, behind=()):
    vmem = pl.BlockSpec(memory_space=pltpu.VMEM)
    return pl.pallas_call(
        functools.partial(add_kernel, len(behind)),
        in_specs=[vmem] * 2 + [ANY] * len(behind),
        out_specs=[vmem] * 4,
        out_shape=[shape_of((ROWS, D))] * 4,
        compiler_params=params(),
        cost_estimate=cost(0, 6 * MIB),
        name="add_kernel",
    )(across, own, *behind)


def scores_of(q, k, diagonal):
    s = dot_cols(q, k)
    if diagonal:
        row = lax.broadcasted_iota(jnp.int32, s.shape, 0) % ROWS
        s = jnp.where(row >= lax.broadcasted_iota(jnp.int32, s.shape, 1), s, -1e30)
    return s


def stack_heads(v):
    return jnp.concatenate([v[:, HD * h : HD * (h + 1)] for h in range(4)], axis=0)


def lay_heads(v):
    return jnp.concatenate([v[ROWS * h : ROWS * (h + 1)] for h in range(4)], axis=1)


def attend_kernel(q, kv, out, lse):
    key, value = kv[:, :HD], kv[:, HD:]
    lane = lax.broadcasted_iota(jnp.int32, (ROWS, 128), 1)
    for b in range(8):
        rows = slice(b * ROWS, (b + 1) * ROWS)
        mine = stack_heads(q[rows] * HD**-0.5)
        pieces = [(scores_of(mine, key[rows], True), value[rows])]
        if b:
            pieces.append((scores_of(mine, key[: b * ROWS], False), value[: b * ROWS]))
        top = functools.reduce(
            jnp.maximum, [jnp.max(s, axis=-1, keepdims=True) for s, _ in pieces]
        )
        total, mixed = 0.0, 0.0
        for s, v in pieces:
            p = jnp.exp(s - top)
            total = total + jnp.sum(p, axis=-1, keepdims=True)
            mixed = mixed + dot(p.astype(BF), v)
        out[rows] = lay_heads(mixed / total).astype(BF)
        log_total = top + jnp.log(total)
        spread_out = jnp.zeros((ROWS, 128), F32)
        for h in range(4):
            spread_out = jnp.where(lane == h, log_total[ROWS * h : ROWS * (h + 1)], spread_out)
        lse[rows] = spread_out


def attend_call(q, kv):
    return pl.pallas_call(
        attend_kernel,
        out_shape=[shape_of((SEQ_LEN, QW)), shape_of((SEQ_LEN, 128), F32)],
        compiler_params=params(),
        cost_estimate=cost(4e9, 2 * MIB, 2 * MIB),
        name="attend_kernel",
    )(q, kv)


def attend_back_kernel(
    q, kv, lse, mixed_grad, tcos, tsin, inv, grad_out, scaled_out, held
):
    key, value = kv[:, :HD], kv[:, HD:]
    held[...] = jnp.zeros_like(held)

    def put(rows, cols, part, turn):
        part = jnp.where(turn, part * tcos[rows] - swap_halves(part) * tsin[rows], part)
        grad_out[rows, cols] = part.astype(BF)
        scaled_out[rows, cols] = (part * inv[rows]).astype(BF)

    for b in range(8):
        rows = slice(b * ROWS, (b + 1) * ROWS)
        mine = stack_heads(q[rows] * HD**-0.5)
        grad = stack_heads(mixed_grad[rows])
        log_total = jnp.concatenate([lse[rows, h : h + 1] for h in range(4)], axis=0)
        pieces = [(rows, True)] + ([(slice(0, b * ROWS), False)] if b else [])
        probs, back = [], []
        inner = 0.0
        for cols, diagonal in pieces:
            p = jnp.exp(scores_of(mine, key[cols], diagonal) - log_total)
            g = dot_cols(grad, value[cols])
            inner = inner + jnp.sum(p * g, axis=-1, keepdims=True)
            probs.append(p)
            back.append(g)
        total = 0.0
        for (cols, _), p, g in zip(pieces, probs, back):
            s_grad = (p * (g - inner)).astype(BF)
            total = total + dot(s_grad, key[cols])
            held[:HD, cols] += dot_rows(mine, s_grad)
            held[HD:, cols] += dot_rows(grad, p.astype(BF))
        wide = lay_heads(total * HD**-0.5)
        for j in range(2):
            put(rows, slice(128 * j, 128 * (j + 1)), wide[:, 128 * j : 128 * (j + 1)], True)
    is_key = lax.broadcasted_iota(jnp.int32, (ROWS, 128), 1) < HD
    for b in range(8):
        rows = slice(b * ROWS, (b + 1) * ROWS)
        put(rows, slice(QW, AW), held[:, rows].T, is_key)


def attend_back_call(q, kv, lse, mixed_grad, tcos, tsin, inv):
    return pl.pallas_call(
        attend_back_kernel,
        out_shape=[shape_of((SEQ_LEN, AW))] * 2,
        scratch_shapes=[pltpu.VMEM((128, SEQ_LEN), F32)],
        compiler_params=params(),
        cost_estimate=cost(8e9, 4 * MIB, 2 * MIB),
        name="attend_back_kernel",
    )(q, kv, lse, mixed_grad, tcos, tsin, inv)


def wgrad_kernel(counts, *refs):
    out = refs[-1]
    at, ref = 0, 0
    for group in counts:
        total = 0.0
        for n in group:
            x = refs[ref : ref + n]
            x = x[0][...] if n == 1 else jnp.concatenate([v[...] for v in x], axis=0)
            total = total + dot_rows(x, refs[ref + n][...])
            ref += n + 1
        out[:, at : at + total.shape[1]] = total.astype(BF)
        at += total.shape[1]


def wgrad_call(tile, *groups, behind=()):
    in_specs, operands, width = [], [], 0
    for group in groups:
        for x, g in group:
            in_specs += [pl.BlockSpec((v.shape[0], tile), lambda i: (0, i)) for v in x]
            in_specs.append(pl.BlockSpec(g.shape, lambda i: (0, 0)))
            operands += [*x, g]
        width += group[0][1].shape[1]
    counts = tuple(tuple(len(x) for x, _ in group) for group in groups)
    return pl.pallas_call(
        functools.partial(wgrad_kernel, counts),
        grid=(D // tile,),
        in_specs=in_specs + [ANY] * len(behind),
        out_specs=pl.BlockSpec((tile, width), lambda i: (i, 0)),
        out_shape=shape_of((D, width)),
        compiler_params=params(),
        cost_estimate=cost(
            2 * SEQ_LEN * D * width, 4 * MIB * len(groups) + 2 * width * (SEQ_LEN + D)
        ),
        name="wgrad_kernel",
    )(*operands, *behind)


WIDE_RATE = 2.0 * D ** (-0.5)
OUT_RATE = 2.0 * max(1, 16 * D // SEQ_LEN) ** (-0.5)
DOWN_RATE = 2.0 * FF ** (-0.5)


def adamw(ins, outs, gradient, rate, decay=DECAY, at=slice(None)):
    weight, first, second = (ref[at] for ref in ins)
    first_new = BETA_ONE * first + (1.0 - BETA_ONE) * gradient
    second_new = BETA_TWO * second + (1.0 - BETA_TWO) * gradient * gradient
    first_hat = first_new / (1.0 - BETA_ONE**STEP)
    second_hat = second_new / (1.0 - BETA_TWO**STEP)
    outs[0][at] = weight - rate * (first_hat / (jnp.sqrt(second_hat) + ADAM_EPS) + decay * weight)
    outs[1][at] = first_new
    outs[2][at] = second_new


def step_call(kernel, operands, states, extra):
    flat = [v for group in states for v in group]
    return pl.pallas_call(
        kernel,
        out_shape=[shape_of(v.shape, F32) for v in flat] + list(extra),
        compiler_params=params(),
        cost_estimate=cost(0, 8 * sum(v.size for v in flat)),
        name=kernel.__name__,
    )(*operands, *flat)


def wide_step_kernel(sums, w, kvg, *refs):
    ins, outs = refs[:9], refs[9:]
    total, gain = 0.0, kvg[:, 129:130].astype(F32)
    for j in range(TILES):
        at = slice(128 * j, min(128 * (j + 1), HID))
        for s in range(3):
            start = 2 * PAD + 128 * j if s == 2 else 256 * j + 128 * s
            cols = slice(start, start + 128)
            g = sums[:, cols].astype(F32)
            if s < 2:
                total = total + g * w[:, cols].astype(F32)
                g = g * gain
            adamw(
                ins[3 * s : 3 * s + 3],
                outs[3 * s : 3 * s + 3],
                g.T[: at.stop - at.start],
                DOWN_RATE if s == 2 else WIDE_RATE,
                at=at,
            )
    outs[9][...] = jnp.sum(total, axis=-1, keepdims=True)


def sum_blocks(parts):
    total = parts[:ROWS].astype(F32)
    for i in range(1, 16):
        total = total + parts[ROWS * i : ROWS * (i + 1)].astype(F32)
    return total


def query_step_kernel(parts, w, gain, gain_two_sum, *refs):
    ins, outs, tail = refs[:6], refs[6:12], refs[12]
    g = sum_blocks(parts)
    adamw(ins[3:], outs[3:], g[:, AW:].T, OUT_RATE)
    g = g[:, :AW]
    gain_one_sum = jnp.sum(g * w[:, :AW].astype(F32), axis=-1, keepdims=True)
    g = g * gain[...]
    adamw(ins[:3], outs[:3], g[:, :QW], WIDE_RATE)
    tail[:, :128] = g[:, QW:]
    lane = lax.broadcasted_iota(jnp.int32, (ROWS, 128), 1)
    tail[:, 128:] = jnp.where(lane == 0, gain_one_sum, gain_two_sum[...])


def last_step_kernel(parts, *refs):
    heads = [parts[2 * h] + parts[2 * h + 1] for h in range(KV_HEADS)]
    key = jnp.concatenate([v[:, :HD] for v in heads], axis=1)
    value = jnp.concatenate([v[:, HD : 2 * HD] for v in heads], axis=1)
    adamw(refs[0:3], refs[6:9], key, WIDE_RATE)
    adamw(refs[3:6], refs[9:12], value, WIDE_RATE)
    refs[12][...] = functools.reduce(jnp.add, [v[:, 128:] for v in heads])


def adamw_step(weight, first, second, gradient, rate, decay):
    first_new = BETA_ONE * first + (1.0 - BETA_ONE) * gradient
    second_new = BETA_TWO * second + (1.0 - BETA_TWO) * gradient * gradient
    first_hat = first_new / (1.0 - BETA_ONE**STEP)
    second_hat = second_new / (1.0 - BETA_TWO**STEP)
    weight_new = weight - rate * (first_hat / (jnp.sqrt(second_hat) + ADAM_EPS) + decay * weight)
    return (weight_new, first_new, second_new)


def rotary():
    positions = jnp.arange(SEQ_LEN).astype(F32)
    frequency = 10000.0 ** (-2.0 * jnp.arange(HD // 2).astype(F32) / HD)
    angles = positions[:, None] * frequency[None, :]
    cos, sin = jnp.cos(angles), jnp.sin(angles)
    return (
        jnp.concatenate([cos] * 4, axis=1),
        jnp.concatenate([-sin, sin, -sin, sin], axis=1),
    )


def shards(
    tokens,
    cotangent,
    w_query,
    query_first,
    query_second,
    w_key,
    key_first,
    key_second,
    w_value,
    value_first,
    value_second,
    w_out,
    out_first,
    out_second,
    w_gate,
    gate_first,
    gate_second,
    w_up,
    up_first,
    up_second,
    w_down,
    down_first,
    down_second,
    norm_gains,
    gains_first,
    gains_second,
):
    z, core = lax.axis_index("z"), lax.axis_index("core")
    dp, ctx = ("y", "x"), ("z", "core")
    back = (z - jnp.arange(4)) % 4
    where = jnp.concatenate([back, core[None]]).astype(jnp.int32)
    order = jnp.concatenate([2 * back + 1 - core, 2 * back + core]).astype(jnp.int32)

    small = jnp.concatenate(
        [
            w_key.astype(BF).reshape(16, 4, HD),
            w_value.astype(BF).reshape(16, 4, HD),
            jnp.broadcast_to(
                jnp.pad(norm_gains.astype(BF).T, ((0, 0), (0, 126)))[:, None, :], (16, 4, 128)
            ),
        ],
        axis=2,
    ).transpose(1, 0, 2)
    small = jnp.broadcast_to(small[:, None], (4, 2, 16, 256)).reshape(ROWS, 256)
    kvg = swap_blocks(small, ctx)
    gain_one = kvg[:, 128:129].astype(F32)

    token_blocks = spread_z(tokens[0])
    grad_blocks = spread_z(cotangent[0])
    w_attend = attend_weights_call(kvg, w_query, w_out)
    near_attend = assemble_call("x", came(w_attend, "x"), token_blocks[1:])
    far_attend = came(near_attend, "y")
    w_ffn = ffn_weights_call(
        kvg, w_gate.T, w_up.T, w_down, far_attend[1:] + grad_blocks[1:]
    )
    all_ffn = lax.all_gather(w_ffn, dp, axis=0, tiled=True)
    all_attend, all_mixed = weights_call(far_attend)
    token_blocks = token_blocks + [other_core(t) for t in token_blocks]

    tcos, tsin = rotary()
    tokens_all, query, key_value, inv_all = first_call(
        where, token_blocks, all_attend, tcos, tsin, ()
    )
    grad_blocks = grad_blocks + [other_core(t) for t in grad_blocks]
    attended, lse = attend_call(query, key_value)

    def reduce_core(a, w, col, tile, behind=()):
        across, own = partial_call(order, a, w, col, tile)
        return add_call(other_core(across), own, behind)

    def reduce_z(parts):
        return [parts[0]] + [ring("z", 4 - k)(parts[k]) for k in (1, 2, 3)]

    def total(parts):
        return functools.reduce(jnp.add, [t.astype(F32) for t in parts])

    mixed_parts = reduce_core((attended,), all_mixed, 0, 1024, grad_blocks[5:])
    middle = tokens[0].astype(F32) + total(reduce_z(mixed_parts))
    inv_second = lax.rsqrt(jnp.mean(middle * middle, axis=-1, keepdims=True) + EPS)
    unit_second = middle * inv_second

    mid_blocks = spread(unit_second.astype(BF))
    hidden0, hidden1, wide0, wide1 = middle_call(where, mid_blocks, grad_blocks, all_ffn)
    wide_parts = reduce_core((wide1, wide0), all_ffn, 0, 512)
    mid_parts = reduce_z(wide_parts)
    ffn_wgrad = wgrad_call(
        256,
        ((mid_blocks[:4], wide0), (mid_blocks[4:], wide1)),
        ((grad_blocks[:4], hidden0), (grad_blocks[4:], hidden1)),
        behind=wide_parts[:1],
    )
    down_sums = partial_call(order, (hidden1, hidden0), all_ffn, 2, 512, wide_parts[:1])
    middle_grad, middle_low, ffn_wgrad, *down_sums = norm_back_call(
        mid_parts, middle, cotangent[0], (F32, BF), (ffn_wgrad, *down_sums)
    )
    ffn_sum = lax.psum_scatter(ffn_wgrad, dp, scatter_dimension=0, tiled=True)
    mid_grad_all, mixed_grad = mixed_grad_call(where, spread(middle_low), all_mixed)
    attend_grad, scaled_grad = attend_back_call(
        query, key_value, lse, mixed_grad, tcos, tsin, inv_all
    )
    attend_wgrad = wgrad_call(
        512, (([tokens_all], scaled_grad),), (([mid_grad_all], attended),)
    )
    attend_parts = swap_blocks(attend_wgrad, dp)
    in_parts = reduce_core((attend_grad,), all_attend, 0, 1024)
    in_parts = reduce_z(in_parts)
    (input_grad,) = norm_back_call(in_parts, tokens[0], middle_grad, (BF,))
    down_parts = add_call(other_core(down_sums[0]), down_sums[1], in_parts[1::2])
    output = middle + total(reduce_z(down_parts))

    *wide_new, gain_two_sum = step_call(
        wide_step_kernel,
        (ffn_sum, w_ffn, kvg),
        (
            (w_gate.T, gate_first.T, gate_second.T),
            (w_up.T, up_first.T, up_second.T),
            (w_down, down_first, down_second),
        ),
        [shape_of((ROWS, 1), F32)],
    )
    wide_new = [v.T for v in wide_new[:6]] + wide_new[6:]
    *query_new, tail = step_call(
        query_step_kernel,
        (attend_parts, w_attend, gain_one, gain_two_sum),
        ((w_query, query_first, query_second), (w_out, out_first, out_second)),
        [shape_of((ROWS, 256), F32)],
    )
    tail = swap_blocks(tail, ctx).reshape(8, 16, 256)
    *kv_new, gains_sum = step_call(
        last_step_kernel,
        (tail,),
        ((w_key, key_first, key_second), (w_value, value_first, value_second)),
        [shape_of((16, 128), F32)],
    )
    gains_sum = gains_sum[:, :2].T / norm_gains.astype(BF).astype(F32)
    gains_new = adamw_step(norm_gains, gains_first, gains_second, gains_sum, 0.3, 0.0)
    return (
        output.astype(BF)[None],
        input_grad[None],
        *query_new[:3],
        *kv_new,
        *query_new[3:],
        *wide_new,
        *gains_new,
    )


def solution(mesh):
    dp, ctx = ("y", "x"), ("z", "core")
    fine = Mesh(mesh.devices.reshape(4, 4, 4, 2), dp + ctx)
    act, col, row = P(dp, ctx, None), P(dp, ctx), P(ctx, dp)
    flat, gains = P(dp + ctx, None), P(None, dp + ctx)
    weights = (col,) * 3 + (flat,) * 6 + (row,) * 3 + (col,) * 6 + (row,) * 3 + (gains,) * 3
    return jax.shard_map(
        shards,
        mesh=fine,
        in_specs=(act, act) + weights,
        out_specs=(act, act) + weights,
        check_vma=False,
    )
```

time: 556 us -> 422 us (0.76)
  starting transfers between devices: 113 us -> 67.9 us
  local copies, waits for them, and re-layouts: 53 us -> 15.4 us
  other arithmetic: 42.1 us -> 12.4 us
  waiting for transfers between devices: 166 us -> 154 us
  Pallas kernels: 159 us -> 151 us
    ppermute x23 -> x20, starting transfers between devices: 49.7 us -> 12.7 us  [other_core(): return lax.ppermute(v, 'core', [(0, 1), (1, 0)])]
    ppermute x54 -> x30, waiting for transfers between devices: 160 us -> 125 us  [the longest x12 67 us: spread_z(): return [v, ring('z', 1)(v), ring('z', 2)(v), ring('z', 3)(v)]]
    ppermute x54 -> x30, starting transfers between devices: 63.6 us -> 30.3 us  [the longest x12 13.8 us: spread_z(): return [v, ring('z', 1)(v), ring('z', 2)(v), ring('z', 3)(v)]]
    all_to_all x0 -> x3, starting transfers between devices: none -> 24.8 us  [swap_blocks(): return lax.all_to_all(v, axes, split_axis=0, concat_axis=0, tiled=True)]
    unnamed x217 -> x127, local copies, waits for them, and re-layouts: 25.9 us -> 14.2 us
    reduce_scatter x1, waiting for transfers between devices: 0.01 us -> 9.46 us  [shards(): ffn_sum = lax.psum_scatter(ffn_wgrad, dp, scatter_dimension=0, tiled=True)]
    pallas_call x17 -> x24, Pallas kernels: 159 us -> 151 us  [the longest x3 34 us: blocks_call(): pl.pallas_call(body, grid_spec=pltpu.PrefetchScalarGridSpec(num_scalar_pr...]
    ppermute x23 -> x20, waiting for transfers between devices: 6.38 us -> 14.2 us  [other_core(): return lax.ppermute(v, 'core', [(0, 1), (1, 0)])]
  transfers between devices with their start and end apart: 79 -> 55, of which waited for: 25 -> 30; matrix products, arithmetic and copies ran while one was open for 12% -> 2% of each run, Pallas kernels for 23% -> 26%
where the time goes in v2:
time: 422 us; the launch traced here: 416 us
  waiting for transfers between devices  154 us (36%)
  Pallas kernels  151 us (36%)
  starting transfers between devices  67.9 us (16%)
  local copies, waits for them, and re-layouts  15.4 us (4%)
  between operations  15 us (4%)
  other arithmetic  12.4 us (3%)
    ppermute x12, waiting for transfers between devices, spread_z(): return [v, ring('z', 1)(v), ring('z', 2)(v), ring('z', 3)(v)]  67 us
    ppermute x12, waiting for transfers between devices, reduce_z(): return [parts[0]] + [ring('z', 4 - k)(parts[k]) for k in (1, 2, 3)]  43.7 us
    pallas_call x3, Pallas kernels, blocks_call(): pl.pallas_call(body, grid_spec=pltpu.PrefetchScalarGridSpec(num_scalar_pr...  34 us
    pallas_call x4, Pallas kernels, partial_call(): pl.pallas_call(functools.partial(partial_kernel, len(a), len(behind)), gr...  29.8 us
    all_to_all x3, starting transfers between devices, swap_blocks(): return lax.all_to_all(v, axes, split_axis=0, concat_axis=0, tiled=True)  24.8 us
    pallas_call x2, Pallas kernels, wgrad_call(): pl.pallas_call(functools.partial(wgrad_kernel, counts), grid=(D // tile,)...  24 us
    pallas_call x4, Pallas kernels, add_call(): pl.pallas_call(functools.partial(add_kernel, len(behind)), in_specs=[vmem...  15.5 us
    ppermute x20, waiting for transfers between devices, other_core(): return lax.ppermute(v, 'core', [(0, 1), (1, 0)])  14.2 us
  transfers between devices with their start and end apart: 55, of which 30 were waited for; matrix products, arithmetic and copies ran while one was open for 2% of the time, Pallas kernels for 26%

profile of v2, /device:TPU:1, one launch (start us, length us, event | category | flops | bytes accessed | tf_op | source)
XLA Modules:
  0.0 415.7 jit_solution(9068522244829015222)
XLA Ops:
  10.5 6.8 %all-to-all-start = ((bf16[8,16,256]{2,1,0:T(8,128)(2,1)}), bf16[8,16,256]{2,1,0:T(8,128)(2,1)S(1)}, u32[]{:S(2)}, u32[]{:S(2)}) async-start(bf16[8,16,256]{2,1,0:T(8,128)(2,1)} %bitcast.4), calls=%async_computation | async-start | bytes 131072 | tf_op jit(solution)/shard_map/all_to_all | solution.py:90
  26.2 4.4 %collective-permute-done.7.refs_1_ = bf16[128,640]{1,0:T(8,128)(2,1)S(1)} collective-permute-done((bf16[128,640]{1,0:T(8,128)(2,1)}, bf16[128,640]{1,0:T(8,128)(2,1)S(1)}, u32[]{:S(2)}, u32[]{:S(2)}) %collective-permute-start.7) | collective-permute-done | bytes 163872 | tf_op jit(solution)/shard_map/ppermute | solution.py:86
  32.1 4.6 %collective-permute-done.8.refs_2_ = bf16[128,640]{1,0:T(8,128)(2,1)S(1)} collective-permute-done((bf16[128,640]{1,0:T(8,128)(2,1)}, bf16[128,640]{1,0:T(8,128)(2,1)S(1)}, u32[]{:S(2)}, u32[]{:S(2)}) %collective-permute-start.8) | collective-permute-done | bytes 163872 | tf_op jit(solution)/shard_map/ppermute | solution.py:86
  56.0 9.6 %collective-permute-done.16.refs_4_.refs_10_.refs_12_ = bf16[128,2048]{1,0:T(8,128)(2,1)S(1)} collective-permute-done((bf16[128,2048]{1,0:T(8,128)(2,1)S(1)}, bf16[128,2048]{1,0:T(8,128)(2,1)S(1)}, u32[]{:S(2)}, u32[]{:S(2)}) %collective-permute-start.16) | collective-permute-done | bytes 524320 | tf_op jit(solution)/shard_map/ppermute | solution.py:77
  65.6 12.9 %collective-permute-done.18.refs_5_.refs_11_.refs_13_ = bf16[128,2048]{1,0:T(8,128)(2,1)S(1)} collective-permute-done((bf16[128,2048]{1,0:T(8,128)(2,1)S(1)}, bf16[128,2048]{1,0:T(8,128)(2,1)S(1)}, u32[]{:S(2)}, u32[]{:S(2)}) %collective-permute-start.18) | collective-permute-done | bytes 524320 | tf_op jit(solution)/shard_map/ppermute | solution.py:77
  92.8 4.4 %weights_kernel.1 = (bf16[2048,384]{1,0:T(8,128)(2,1)}, bf16[2048,256]{1,0:T(8,128)(2,1)}) custom-call(s32[4]{0:T(128)} %and_select_fusion.1.order, bf16[4,128,640]{2,1,0:T(8,128)(2,1)} %assemble_kernel.1.refs_0_, bf16[4,128,640]{2,1,0:T(8,128)(2,1)} %copy-done.4, bf16[4,128,640]{2,1,0:T(8,128)(2,1)} %copy-done.5, bf16[4,128,640]{2,1,0:T(8,128)(2,1)} %copy-done.6), custom_call_target="tpu_custom_call" | custom-call | bytes 5242880 | tf_op jit(solution)/shard_map/weights_kernel/pallas_call | solution.py:196
  98.5 8.3 %first_kernel.1 = (bf16[1024,2048]{1,0:T(8,128)(2,1)}, bf16[1024,256]{1,0:T(8,128)(2,1)}, bf16[1024,128]{1,0:T(8,128)(2,1)}, f32[1024,128]{1,0:T(8,128)}) custom-call(s32[5]{0:T(128)} %pad_add_fusion.1.where, bf16[128,2048]{1,0:T(8,128)(2,1)} %bitcast.41, bf16[128,2048]{1,0:T(8,128)(2,1)} %copy-done.12, bf16[128,2048]{1,0:T(8,128)(2,1)} %copy-done.14, ...), custom_call_target="tpu_custom_call" | custom-call | flops 1610612736 | bytes 12320768 | tf_op jit(solution)/shard_map/first_kernel/pallas_call | solution.py:146
  106.7 6.6 %attend_kernel.1 = (bf16[1024,256]{1,0:T(8,128)(2,1)}, f32[1024,128]{1,0:T(8,128)}) custom-call(bf16[1024,256]{1,0:T(8,128)(2,1)} %get-tuple-element.96.q, bf16[1024,128]{1,0:T(8,128)(2,1)} %get-tuple-element.97.kv), custom_call_target="tpu_custom_call" | custom-call | flops 4000000000 | bytes 2097152 | tf_op jit(solution)/shard_map/attend_kernel/pallas_call | solution.py:471
  113.4 4.7 %partial_kernel.4 = (bf16[512,2048]{1,0:T(8,128)(2,1)}, bf16[512,2048]{1,0:T(8,128)(2,1)}) custom-call(s32[8]{0:T(128)} %pad_add_fusion.order, bf16[1024,256]{1,0:T(8,128)(2,1)} %get-tuple-element.98.refs_0_.refs_3_, bf16[2048,256]{1,0:T(8,128)(2,1)} %get-tuple-element.99.refs_1_.refs_8_), custom_call_target="tpu_custom_call" | custom-call | flops 1073741824 | bytes 5767168 | tf_op jit(solution)/shard_map/partial_kernel/pallas_call | solution.py:393
  119.1 3.9 collective-permute-done.15.refs_0_.refs_13_.refs_16_
  126.0 3.9 add_kernel.4
  132.1 11.2 %collective-permute-done.20 = bf16[128,2048]{1,0:T(8,128)(2,1)S(1)} collective-permute-done((bf16[128,2048]{1,0:T(8,128)(2,1)}, bf16[128,2048]{1,0:T(8,128)(2,1)S(1)}, u32[]{:S(2)}, u32[]{:S(2)}) %collective-permute-start.20) | collective-permute-done | bytes 524320 | tf_op jit(solution)/shard_map/ppermute | solution.py:738
  146.1 11.9 %collective-permute-done.22 = bf16[128,2048]{1,0:T(8,128)(2,1)S(1)} collective-permute-done((bf16[128,2048]{1,0:T(8,128)(2,1)}, bf16[128,2048]{1,0:T(8,128)(2,1)S(1)}, u32[]{:S(2)}, u32[]{:S(2)}) %collective-permute-start.22) | collective-permute-done | bytes 524320 | tf_op jit(solution)/shard_map/ppermute | solution.py:738
  163.6 21.6 %collective-permute-done.23.refs_1_ = bf16[128,2048]{1,0:T(8,128)(2,1)S(1)} collective-permute-done((bf16[128,2048]{1,0:T(8,128)(2,1)S(1)}, bf16[128,2048]{1,0:T(8,128)(2,1)S(1)}, u32[]{:S(2)}, u32[]{:S(2)}) %collective-permute-start.23) | collective-permute-done | bytes 524320 | tf_op jit(solution)/shard_map/ppermute | solution.py:77
  190.5 19.3 %middle_kernel.1 = (bf16[512,768]{1,0:T(8,128)(2,1)}, bf16[512,768]{1,0:T(8,128)(2,1)}, bf16[512,1536]{1,0:T(8,128)(2,1)}, bf16[512,1536]{1,0:T(8,128)(2,1)}) custom-call(s32[5]{0:T(128)} %pad_add_fusion.1.where, bf16[128,2048]{1,0:T(8,128)(2,1)} %copy-done.32, bf16[128,2048]{1,0:T(8,128)(2,1)} %copy-done.54, bf16[128,2048]{1,0:T(8,128)(2,1)} %copy-done.55, ...), custom_call_target="tpu_custom_call" | custom-call | flops 9663676416 | bytes 22544384 | tf_op jit(solution)/shard_map/middle_kernel/pallas_call | solution.py:146
  209.8 11.3 %partial_kernel.5 = (bf16[512,2048]{1,0:T(8,128)(2,1)}, bf16[512,2048]{1,0:T(8,128)(2,1)}) custom-call(s32[8]{0:T(128)} %pad_add_fusion.order, bf16[512,1536]{1,0:T(8,128)(2,1)} %get-tuple-element.106.refs_0_.refs_9_, bf16[512,1536]{1,0:T(8,128)(2,1)} %get-tuple-element.107.refs_1_.refs_4_, bf16[2048,2304]{1,0:T(8,128)(2,1)} %all-gather.2.cloned.1.call-done.refs_16_.refs_2_), custom_call_target="tpu_custom_call" | custom-call | flops 6442450944 | bytes 13631488 | tf_op jit(solution)/shard_map/partial_kernel/pallas_call | solution.py:393
  221.5 4.0 collective-permute-done.31.across
  232.0 16.0 %wgrad_kernel.2.refs_6_ = bf16[2048,2304]{1,0:T(8,128)(2,1)} custom-call(bf16[128,2048]{1,0:T(8,128)(2,1)} %copy-done.32, bf16[128,2048]{1,0:T(8,128)(2,1)} %copy-done.54, bf16[128,2048]{1,0:T(8,128)(2,1)} %copy-done.55, bf16[128,2048]{1,0:T(8,128)(2,1)} %copy-done.56, bf16[512,1536]{1,0:T(8,128)(2,1)} %get-tuple-element.107.refs_1_.refs_4_, ...), custom_call_target="tpu_custom_call" | custom-call | flops 9663676416 | bytes 22544384 | tf_op jit(solution)/shard_map/wgrad_kernel/pallas_call | solution.py:554
  248.0 7.7 %partial_kernel.6 = (bf16[512,2048]{1,0:T(8,128)(2,1)}, bf16[512,2048]{1,0:T(8,128)(2,1)}) custom-call(s32[8]{0:T(128)} %pad_add_fusion.order, bf16[512,768]{1,0:T(8,128)(2,1)} %get-tuple-element.115.refs_19_.refs_0_, bf16[512,768]{1,0:T(8,128)(2,1)} %get-tuple-element.114.refs_14_.refs_1_, bf16[2048,2304]{1,0:T(8,128)(2,1)} %all-gather.2.cloned.1.call-done.refs_16_.refs_2_, ...), custom_call_target="tpu_custom_call" | custom-call | flops 3221225472 | bytes 8912896 | tf_op jit(solution)/shard_map/partial_kernel/pallas_call | solution.py:393
  259.0 4.1 norm_back_kernel.2
  269.9 19.6 %collective-permute-done.36.refs_1_ = bf16[128,2048]{1,0:T(8,128)(2,1)S(1)} collective-permute-done((bf16[128,2048]{1,0:T(8,128)(2,1)S(1)}, bf16[128,2048]{1,0:T(8,128)(2,1)S(1)}, u32[]{:S(2)}, u32[]{:S(2)}) %collective-permute-start.36) | collective-permute-done | bytes 524320 | tf_op jit(solution)/shard_map/ppermute | solution.py:77
  294.8 6.4 %mixed_grad_kernel.1 = (bf16[1024,2048]{1,0:T(8,128)(2,1)}, bf16[1024,256]{1,0:T(8,128)(2,1)}) custom-call(s32[5]{0:T(128)} %pad_add_fusion.1.where, bf16[128,2048]{1,0:T(8,128)(2,1)} %get-tuple-element.121.refs_0_, bf16[128,2048]{1,0:T(8,128)(2,1)} %copy-done.40, bf16[128,2048]{1,0:T(8,128)(2,1)} %copy-done.42, bf16[128,2048]{1,0:T(8,128)(2,1)} %copy-done.43, ...), custom_call_target="tpu_custom_call" | custom-call | flops 1073741824 | bytes 9961472 | tf_op jit(solution)/shard_map/mixed_grad_kernel/pallas_call | solution.py:146
  301.2 11.7 %attend_back_kernel.1 = (bf16[1024,384]{1,0:T(8,128)(2,1)}, bf16[1024,384]{1,0:T(8,128)(2,1)}) custom-call(bf16[1024,256]{1,0:T(8,128)(2,1)} %get-tuple-element.96.q, bf16[1024,128]{1,0:T(8,128)(2,1)} %get-tuple-element.97.kv, f32[1024,128]{1,0:T(8,128)} %get-tuple-element.120.lse, bf16[1024,256]{1,0:T(8,128)(2,1)} %get-tuple-element.122.mixed_grad, ...), custom_call_target="tpu_custom_call" | custom-call | flops 8000000000 | bytes 4194304 | tf_op jit(solution)/shard_map/attend_back_kernel/pallas_call | solution.py:521
  312.9 6.0 %partial_kernel.7 = (bf16[512,2048]{1,0:T(8,128)(2,1)}, bf16[512,2048]{1,0:T(8,128)(2,1)}) custom-call(s32[8]{0:T(128)} %pad_add_fusion.order, bf16[1024,384]{1,0:T(8,128)(2,1)} %get-tuple-element.124.refs_0_, bf16[2048,384]{1,0:T(8,128)(2,1)} %get-tuple-element.95.refs_8_.refs_1_), custom_call_target="tpu_custom_call" | custom-call | flops 1610612736 | bytes 6553600 | tf_op jit(solution)/shard_map/partial_kernel/pallas_call | solution.py:393
  319.7 8.0 %wgrad_kernel.3 = bf16[2048,640]{1,0:T(8,128)(2,1)} custom-call(bf16[1024,2048]{1,0:T(8,128)(2,1)} %get-tuple-element.136.refs_0_, bf16[1024,384]{1,0:T(8,128)(2,1)} %get-tuple-element.137.refs_1_, bf16[1024,2048]{1,0:T(8,128)(2,1)} %get-tuple-element.138.refs_2_, bf16[1024,256]{1,0:T(8,128)(2,1)} %get-tuple-element.98.refs_0_.refs_3_), custom_call_target="tpu_custom_call" | custom-call | flops 2684354560 | bytes 12320768 | tf_op jit(solution)/shard_map/wgrad_kernel/pallas_call | solution.py:554
  327.7 5.8 %all-to-all-start.1 = ((bf16[16,128,640]{2,1,0:T(8,128)(2,1)}), bf16[16,128,640]{2,1,0:T(8,128)(2,1)}, u32[]{:S(2)}, u32[]{:S(2)}) async-start(bf16[16,128,640]{2,1,0:T(8,128)(2,1)} %bitcast.37), calls=%async_computation.1 | async-start | bytes 5242880 | tf_op jit(solution)/shard_map/all_to_all | solution.py:90
  333.5 4.1 add_kernel.6
  340.0 10.7 %collective-permute-done.44.refs_0_.refs_1_ = bf16[128,2048]{1,0:T(8,128)(2,1)S(1)} collective-permute-done((bf16[128,2048]{1,0:T(8,128)(2,1)}, bf16[128,2048]{1,0:T(8,128)(2,1)S(1)}, u32[]{:S(2)}, u32[]{:S(2)}) %collective-permute-start.44) | collective-permute-done | bytes 524320 | tf_op jit(solution)/shard_map/ppermute | solution.py:738
  366.2 9.5 %reduce-scatter.2.cloned.1.call-done.sums = bf16[128,2304]{1,0:T(8,128)(2,1)} async-done(((bf16[2048,2304]{1,0:T(8,128)(2,1)}), bf16[128,2304]{1,0:T(8,128)(2,1)}) %reduce-scatter.2.cloned.1.call-update) | async-done | bytes 589840 | tf_op jit(solution)/shard_map/reduce_scatter | solution.py:762
  375.7 5.0 %wide_step_kernel.1 = (f32[704,128]{1,0:T(8,128)}, f32[704,128]{1,0:T(8,128)}, f32[704,128]{1,0:T(8,128)}, f32[704,128]{1,0:T(8,128)}, f32[704,128]{1,0:T(8,128)...) custom-call(bf16[128,2304]{1,0:T(8,128)(2,1)} %reduce-scatter.2.clon, ...), custom_call_target="tpu_custom_call" | custom-call | bytes 6488064 | tf_op jit(solution)/shard_map/wide_step_kernel/pallas_call | solution.py:586
  386.0 12.2 %all-to-all-start.2 = ((f32[8,16,256]{2,1,0:T(8,128)}), f32[8,16,256]{2,1,0:T(8,128)S(1)}, u32[]{:S(2)}, u32[]{:S(2)}) async-start(f32[8,16,256]{2,1,0:T(8,128)} %bitcast.64), calls=%async_computation.3 | async-start | bytes 262144 | tf_op jit(solution)/shard_map/all_to_all | solution.py:90
  399.4 4.1 all-to-all-done.2.parts
  (264 shorter events, 120.4 us)
Async XLA Ops:
  17.3 173.2 %all-gather.2.cloned.1.call-start = ((), (), s32[]{:S(2)}) async-start(), calls=%async_computation.4 | async-start | bytes 10027008 | tf_op jit(solution)/shard_map/all_gather | solution.py:722
  17.3 24.2 %collective-permute-start = (bf16[128,2048]{1,0:T(8,128)(2,1)}, bf16[128,2048]{1,0:T(8,128)(2,1)S(1)}, u32[]{:S(2)}, u32[]{:S(2)}) collective-permute-start(bf16[128,2048]{1,0:T(8,128)(2,1)} %bitcast.38), channel_id=1, source_target_pairs={{0,2},{2,4},{4,6},{6,0},{1,3},{3,5},{5,7},{7,1},{8,10},{10,12},{12... | collective-permute-start | bytes 1572872 | tf_op jit(solution)/shard_map/ppermute | solution.py:77
  18.7 25.6 %collective-permute-start.1 = (bf16[128,2048]{1,0:T(8,128)(2,1)}, bf16[128,2048]{1,0:T(8,128)(2,1)S(1)}, u32[]{:S(2)}, u32[]{:S(2)}) collective-permute-start(bf16[128,2048]{1,0:T(8,128)(2,1)} %bitcast.39), channel_id=1, source_target_pairs={{0,4},{2,6},{4,0},{6,2},{1,5},{3,7},{5,1},{7,3},{8,12},{10,14},{12... | collective-permute-start | bytes 1572872 | tf_op jit(solution)/shard_map/ppermute | solution.py:77
  21.1 23.2 %collective-permute-start.2 = (bf16[128,2048]{1,0:T(8,128)(2,1)}, bf16[128,2048]{1,0:T(8,128)(2,1)S(1)}, u32[]{:S(2)}, u32[]{:S(2)}) collective-permute-start(bf16[128,2048]{1,0:T(8,128)(2,1)} %bitcast.40), channel_id=1, source_target_pairs={{0,6},{2,0},{4,2},{6,4},{1,7},{3,1},{5,3},{7,5},{8,14},{10,8},{12,... | collective-permute-start | bytes 1572872 | tf_op jit(solution)/shard_map/ppermute | solution.py:77
  25.9 29.5 %collective-permute-start.14 = (bf16[128,2048]{1,0:T(8,128)(2,1)}, bf16[128,2048]{1,0:T(8,128)(2,1)S(1)}, u32[]{:S(2)}, u32[]{:S(2)}) collective-permute-start(bf16[128,2048]{1,0:T(8,128)(2,1)} %bitcast.52), channel_id=1, source_target_pairs={{0,2},{2,4},{4,6},{6,0},{1,3},{3,5},{5,7},{7,1},{8,10},{10,12},{12... | collective-permute-start | bytes 1572872 | tf_op jit(solution)/shard_map/ppermute | solution.py:77
  48.5 30.0 %collective-permute-start.10 = (bf16[4,128,640]{2,1,0:T(8,128)(2,1)}, bf16[4,128,640]{2,1,0:T(8,128)(2,1)S(1)}, u32[]{:S(2)}, u32[]{:S(2)}) collective-permute-start(bf16[4,128,640]{2,1,0:T(8,128)(2,1)} %assemble_kernel.1.refs_0_), channel_id=1, source_target_pairs={{0,32},{32,64},{64,96},{96,0},{1,33},{33,65},{65,97},{97,1},{2,34}... | collective-permute-start | bytes 1966088 | tf_op jit(solution)/shard_map/ppermute | solution.py:86
  49.8 29.7 %collective-permute-start.11 = (bf16[4,128,640]{2,1,0:T(8,128)(2,1)}, bf16[4,128,640]{2,1,0:T(8,128)(2,1)S(1)}, u32[]{:S(2)}, u32[]{:S(2)}) collective-permute-start(bf16[4,128,640]{2,1,0:T(8,128)(2,1)} %assemble_kernel.1.refs_0_), channel_id=1, source_target_pairs={{0,64},{32,96},{64,0},{96,32},{1,65},{33,97},{65,1},{97,33},{2,66}... | collective-permute-start | bytes 1966088 | tf_op jit(solution)/shard_map/ppermute | solution.py:86
  52.5 27.9 %collective-permute-start.12 = (bf16[4,128,640]{2,1,0:T(8,128)(2,1)}, bf16[4,128,640]{2,1,0:T(8,128)(2,1)S(1)}, u32[]{:S(2)}, u32[]{:S(2)}) collective-permute-start(bf16[4,128,640]{2,1,0:T(8,128)(2,1)} %assemble_kernel.1.refs_0_), channel_id=1, source_target_pairs={{0,96},{32,0},{64,32},{96,64},{1,97},{33,1},{65,33},{97,65},{2,98}... | collective-permute-start | bytes 1966088 | tf_op jit(solution)/shard_map/ppermute | solution.py:86
  55.4 23.1 %collective-permute-start.18 = (bf16[128,2048]{1,0:T(8,128)(2,1)S(1)}, bf16[128,2048]{1,0:T(8,128)(2,1)S(1)}, u32[]{:S(2)}, u32[]{:S(2)}) collective-permute-start(bf16[128,2048]{1,0:T(8,128)(2,1)S(1)} %bitcast.57), channel_id=1, source_target_pairs={{0,6},{2,0},{4,2},{6,4},{1,7},{3,1},{5,3},{7,5},{8,14},{10,8},{12,... | collective-permute-start | bytes 1572872 | tf_op jit(solution)/shard_map/ppermute | solution.py:77
  83.8 291.9 %reduce-scatter.2.cloned.1.call-start = ((), (), s32[]{:S(2)}) async-start(), calls=%async_computation.5 | async-start | bytes 10027008 | tf_op jit(solution)/shard_map/reduce_scatter | solution.py:762
  131.4 14.7 %collective-permute-start.21 = (bf16[128,2048]{1,0:T(8,128)(2,1)}, bf16[128,2048]{1,0:T(8,128)(2,1)S(1)}, u32[]{:S(2)}, u32[]{:S(2)}) collective-permute-start(bf16[128,2048]{1,0:T(8,128)(2,1)} %get-tuple-element.104), channel_id=1, source_target_pairs={{0,4},{2,6},{4,0},{6,2},{1,5},{3,7},{5,1},{7,3},{8,12},{10,14},{12... | collective-permute-start | bytes 1572872 | tf_op jit(solution)/shard_map/ppermute | solution.py:738
  131.4 26.6 %collective-permute-start.22 = (bf16[128,2048]{1,0:T(8,128)(2,1)}, bf16[128,2048]{1,0:T(8,128)(2,1)S(1)}, u32[]{:S(2)}, u32[]{:S(2)}) collective-permute-start(bf16[128,2048]{1,0:T(8,128)(2,1)} %get-tuple-element.105), channel_id=1, source_target_pairs={{0,2},{2,4},{4,6},{6,0},{1,3},{3,5},{5,7},{7,1},{8,10},{10,12},{12... | collective-permute-start | bytes 1572872 | tf_op jit(solution)/shard_map/ppermute | solution.py:738
  159.7 25.5 %collective-permute-start.23 = (bf16[128,2048]{1,0:T(8,128)(2,1)S(1)}, bf16[128,2048]{1,0:T(8,128)(2,1)S(1)}, u32[]{:S(2)}, u32[]{:S(2)}) collective-permute-start(bf16[128,2048]{1,0:T(8,128)(2,1)S(1)} %multiply_convert_fusion.refs_0_), channel_id=1, source_target_pairs={{0,2},{2,4},{4,6},{6,0},{1,3},{3,5},{5,7},{7,1},{8,10},{10,12},{12... | collective-permute-start | bytes 1572872 | tf_op jit(solution)/shard_map/ppermute | solution.py:77
  159.8 26.8 %collective-permute-start.24 = (bf16[128,2048]{1,0:T(8,128)(2,1)S(1)}, bf16[128,2048]{1,0:T(8,128)(2,1)S(1)}, u32[]{:S(2)}, u32[]{:S(2)}) collective-permute-start(bf16[128,2048]{1,0:T(8,128)(2,1)S(1)} %multiply_convert_fusion.refs_0_), channel_id=1, source_target_pairs={{0,4},{2,6},{4,0},{6,2},{1,5},{3,7},{5,1},{7,3},{8,12},{10,14},{12... | collective-permute-start | bytes 1572872 | tf_op jit(solution)/shard_map/ppermute | solution.py:77
  160.7 26.0 %collective-permute-start.25 = (bf16[128,2048]{1,0:T(8,128)(2,1)S(1)}, bf16[128,2048]{1,0:T(8,128)(2,1)S(1)}, u32[]{:S(2)}, u32[]{:S(2)}) collective-permute-start(bf16[128,2048]{1,0:T(8,128)(2,1)S(1)} %multiply_convert_fusion.refs_0_), channel_id=1, source_target_pairs={{0,6},{2,0},{4,2},{6,4},{1,7},{3,1},{5,3},{7,5},{8,14},{10,8},{12,... | collective-permute-start | bytes 1572872 | tf_op jit(solution)/shard_map/ppermute | solution.py:77
  162.5 24.7 %collective-permute-start.30 = (bf16[128,2048]{1,0:T(8,128)(2,1)S(1)}, bf16[128,2048]{1,0:T(8,128)(2,1)S(1)}, u32[]{:S(2)}, u32[]{:S(2)}) collective-permute-start(bf16[128,2048]{1,0:T(8,128)(2,1)S(1)} %bitcast.58), channel_id=1, source_target_pairs={{0,1},{1,0},{2,3},{3,2},{4,5},{5,4},{6,7},{7,6},{8,9},{9,8},{10,11... | collective-permute-start | bytes 1572872 | tf_op jit(solution)/shard_map/ppermute | solution.py:73
  163.6 23.6 %collective-permute-start.26 = (bf16[128,2048]{1,0:T(8,128)(2,1)S(1)}, bf16[128,2048]{1,0:T(8,128)(2,1)S(1)}, u32[]{:S(2)}, u32[]{:S(2)}) collective-permute-start(bf16[128,2048]{1,0:T(8,128)(2,1)S(1)} %multiply_convert_fusion.refs_0_), channel_id=1, source_target_pairs={{0,1},{1,0},{2,3},{3,2},{4,5},{5,4},{6,7},{7,6},{8,9},{9,8},{10,11... | collective-permute-start | bytes 1572872 | tf_op jit(solution)/shard_map/ppermute | solution.py:73
  230.5 25.2 %collective-permute-start.32 = (bf16[128,2048]{1,0:T(8,128)(2,1)}, bf16[128,2048]{1,0:T(8,128)(2,1)S(1)}, u32[]{:S(2)}, u32[]{:S(2)}) collective-permute-start(bf16[128,2048]{1,0:T(8,128)(2,1)} %get-tuple-element.111), channel_id=1, source_target_pairs={{0,6},{2,0},{4,2},{6,4},{1,7},{3,1},{5,3},{7,5},{8,14},{10,8},{12,... | collective-permute-start | bytes 1572872 | tf_op jit(solution)/shard_map/ppermute | solution.py:738
  231.3 24.4 %collective-permute-start.33 = (bf16[128,2048]{1,0:T(8,128)(2,1)}, bf16[128,2048]{1,0:T(8,128)(2,1)S(1)}, u32[]{:S(2)}, u32[]{:S(2)}) collective-permute-start(bf16[128,2048]{1,0:T(8,128)(2,1)} %get-tuple-element.112), channel_id=1, source_target_pairs={{0,4},{2,6},{4,0},{6,2},{1,5},{3,7},{5,1},{7,3},{8,12},{10,14},{12... | collective-permute-start | bytes 1572872 | tf_op jit(solution)/shard_map/ppermute | solution.py:738
  231.3 26.8 %collective-permute-start.34 = (bf16[128,2048]{1,0:T(8,128)(2,1)}, bf16[128,2048]{1,0:T(8,128)(2,1)S(1)}, u32[]{:S(2)}, u32[]{:S(2)}) collective-permute-start(bf16[128,2048]{1,0:T(8,128)(2,1)} %get-tuple-element.113), channel_id=1, source_target_pairs={{0,2},{2,4},{4,6},{6,0},{1,3},{3,5},{5,7},{7,1},{8,10},{10,12},{12... | collective-permute-start | bytes 1572872 | tf_op jit(solution)/shard_map/ppermute | solution.py:738
  264.1 25.4 %collective-permute-start.36 = (bf16[128,2048]{1,0:T(8,128)(2,1)S(1)}, bf16[128,2048]{1,0:T(8,128)(2,1)S(1)}, u32[]{:S(2)}, u32[]{:S(2)}) collective-permute-start(bf16[128,2048]{1,0:T(8,128)(2,1)S(1)} %copy-done.37), channel_id=1, source_target_pairs={{0,2},{2,4},{4,6},{6,0},{1,3},{3,5},{5,7},{7,1},{8,10},{10,12},{12... | collective-permute-start | bytes 1572872 | tf_op jit(solution)/shard_map/ppermute | solution.py:77
  264.1 26.8 %collective-permute-start.37 = (bf16[128,2048]{1,0:T(8,128)(2,1)S(1)}, bf16[128,2048]{1,0:T(8,128)(2,1)S(1)}, u32[]{:S(2)}, u32[]{:S(2)}) collective-permute-start(bf16[128,2048]{1,0:T(8,128)(2,1)S(1)} %copy-done.37), channel_id=1, source_target_pairs={{0,4},{2,6},{4,0},{6,2},{1,5},{3,7},{5,1},{7,3},{8,12},{10,14},{12... | collective-permute-start | bytes 1572872 | tf_op jit(solution)/shard_map/ppermute | solution.py:77
  265.6 25.4 %collective-permute-start.38 = (bf16[128,2048]{1,0:T(8,128)(2,1)S(1)}, bf16[128,2048]{1,0:T(8,128)(2,1)S(1)}, u32[]{:S(2)}, u32[]{:S(2)}) collective-permute-start(bf16[128,2048]{1,0:T(8,128)(2,1)S(1)} %copy-done.37), channel_id=1, source_target_pairs={{0,6},{2,0},{4,2},{6,4},{1,7},{3,1},{5,3},{7,5},{8,14},{10,8},{12,... | collective-permute-start | bytes 1572872 | tf_op jit(solution)/shard_map/ppermute | solution.py:77
  267.9 23.6 %collective-permute-start.39 = (bf16[128,2048]{1,0:T(8,128)(2,1)S(1)}, bf16[128,2048]{1,0:T(8,128)(2,1)S(1)}, u32[]{:S(2)}, u32[]{:S(2)}) collective-permute-start(bf16[128,2048]{1,0:T(8,128)(2,1)S(1)} %copy-done.37), channel_id=1, source_target_pairs={{0,1},{1,0},{2,3},{3,2},{4,5},{5,4},{6,7},{7,6},{8,9},{9,8},{10,11... | collective-permute-start | bytes 1572872 | tf_op jit(solution)/shard_map/ppermute | solution.py:73
  319.4 20.6 %collective-permute-start.35 = (bf16[512,2048]{1,0:T(8,128)(2,1)S(1)}, bf16[512,2048]{1,0:T(8,128)(2,1)}, u32[]{:S(2)}, u32[]{:S(2)}) collective-permute-start(bf16[512,2048]{1,0:T(8,128)(2,1)S(1)} %copy-done.7), channel_id=1, source_target_pairs={{0,1},{1,0},{2,3},{3,2},{4,5},{5,4},{6,7},{7,6},{8,9},{9,8},{10,11... | collective-permute-start | bytes 6291464 | tf_op jit(solution)/shard_map/ppermute | solution.py:73
  327.7 54.7 %all-to-all-start.1 = ((bf16[16,128,640]{2,1,0:T(8,128)(2,1)}), bf16[16,128,640]{2,1,0:T(8,128)(2,1)}, u32[]{:S(2)}, u32[]{:S(2)}) async-start(bf16[16,128,640]{2,1,0:T(8,128)(2,1)} %bitcast.37), calls=%async_computation.1 | async-start | bytes 5242880 | tf_op jit(solution)/shard_map/all_to_all | solution.py:90
  338.8 14.9 %collective-permute-start.45 = (bf16[128,2048]{1,0:T(8,128)(2,1)}, bf16[128,2048]{1,0:T(8,128)(2,1)S(1)}, u32[]{:S(2)}, u32[]{:S(2)}) collective-permute-start(bf16[128,2048]{1,0:T(8,128)(2,1)} %get-tuple-element.128), channel_id=1, source_target_pairs={{0,2},{2,4},{4,6},{6,0},{1,3},{3,5},{5,7},{7,1},{8,10},{10,12},{12... | collective-permute-start | bytes 1572872 | tf_op jit(solution)/shard_map/ppermute | solution.py:738
  339.1 23.5 %collective-permute-start.49 = (bf16[128,2048]{1,0:T(8,128)(2,1)}, bf16[128,2048]{1,0:T(8,128)(2,1)}, u32[]{:S(2)}, u32[]{:S(2)}) collective-permute-start(bf16[128,2048]{1,0:T(8,128)(2,1)} %get-tuple-element.134), channel_id=1, source_target_pairs={{0,4},{2,6},{4,0},{6,2},{1,5},{3,7},{5,1},{7,3},{8,12},{10,14},{12... | collective-permute-start | bytes 1572872 | tf_op jit(solution)/shard_map/ppermute | solution.py:738
  358.3 39.9 %collective-permute-start.46 = (bf16[128,2048]{1,0:T(8,128)(2,1)}, bf16[128,2048]{1,0:T(8,128)(2,1)S(1)}, u32[]{:S(2)}, u32[]{:S(2)}) collective-permute-start(bf16[128,2048]{1,0:T(8,128)(2,1)} %get-tuple-element.130), channel_id=1, source_target_pairs={{0,6},{2,0},{4,2},{6,4},{1,7},{3,1},{5,3},{7,5},{8,14},{10,8},{12,... | collective-permute-start | bytes 1572872 | tf_op jit(solution)/shard_map/ppermute | solution.py:738
  358.3 39.9 %collective-permute-start.47 = (bf16[128,2048]{1,0:T(8,128)(2,1)}, bf16[128,2048]{1,0:T(8,128)(2,1)S(1)}, u32[]{:S(2)}, u32[]{:S(2)}) collective-permute-start(bf16[128,2048]{1,0:T(8,128)(2,1)} %get-tuple-element.131), channel_id=1, source_target_pairs={{0,4},{2,6},{4,0},{6,2},{1,5},{3,7},{5,1},{7,3},{8,12},{10,14},{12... | collective-permute-start | bytes 1572872 | tf_op jit(solution)/shard_map/ppermute | solution.py:738
  358.3 39.9 %collective-permute-start.48 = (bf16[128,2048]{1,0:T(8,128)(2,1)}, bf16[128,2048]{1,0:T(8,128)(2,1)S(1)}, u32[]{:S(2)}, u32[]{:S(2)}) collective-permute-start(bf16[128,2048]{1,0:T(8,128)(2,1)} %get-tuple-element.132), channel_id=1, source_target_pairs={{0,2},{2,4},{4,6},{6,0},{1,3},{3,5},{5,7},{7,1},{8,10},{10,12},{12... | collective-permute-start | bytes 1572872 | tf_op jit(solution)/shard_map/ppermute | solution.py:738
  386.0 17.5 %all-to-all-start.2 = ((f32[8,16,256]{2,1,0:T(8,128)}), f32[8,16,256]{2,1,0:T(8,128)S(1)}, u32[]{:S(2)}, u32[]{:S(2)}) async-start(f32[8,16,256]{2,1,0:T(8,128)} %bitcast.64), calls=%async_computation.3 | async-start | bytes 262144 | tf_op jit(solution)/shard_map/all_to_all | solution.py:90
  (84 other events, 558.8 us)
Sparse Core Ops, SparseCore 0:
  83.9 76.6 all-gather.1
  263.2 112.4 reduce-scatter.1

commit v3 on v2

--- a/solution.py
+++ b/solution.py
@@ -94,23 +94,31 @@
 HELD = [pltpu.VMEM((4, 2 * ROWS, D), BF), pltpu.SemaphoreType.DMA((8,))]
 
 
+def block_copy(halves, blocks, held, sems, k, half, source=None):
+    source = blocks[4 * half + k] if source is None else source
+    rows = pl.ds(pl.multiple_of(halves[half] * ROWS, ROWS), ROWS)
+    return pltpu.make_async_copy(source, held.at[k, rows], sems.at[4 * half + k])
+
+
+def start_blocks(halves, blocks, held, sems, at):
+    for k in at:
+        for half in range(2):
+            block_copy(halves, blocks, held, sems, k, half).start()
+
+
+def wait_blocks(halves, blocks, held, sems):
+    step = pl.program_id(0)
+    for half in range(2):
+        block_copy(halves, blocks, held, sems, step, half, blocks[0]).wait()
+    return held.at[step]
+
+
 def load_blocks(halves, blocks, held, sems):
-    step = pl.program_id(0)
-
-    def copy(i, k, half, source):
-        return pltpu.make_async_copy(
-            source, held.at[k, pl.ds(pl.multiple_of(half * ROWS, ROWS), ROWS)], sems.at[i]
-        )
-
-    @pl.when(step == 0)
+    @pl.when(pl.program_id(0) == 0)
     def _():
-        for k in range(4):
-            copy(k, k, halves[0], blocks[k]).start()
-            copy(4 + k, k, halves[1], blocks[4 + k]).start()
-
-    copy(step, step, halves[0], blocks[0]).wait()
-    copy(4 + step, step, halves[1], blocks[4]).wait()
-    return held.at[step]
+        start_blocks(halves, blocks, held, sems, range(4))
+
+    return wait_blocks(halves, blocks, held, sems)
 
 
 def by_block(width):
@@ -160,12 +168,12 @@
     )(where, *blocks, *operands, *behind, *through)
 
 
-def assemble_call(axis, pieces, behind=()):
+def assemble_call(axis, pieces, behind, through):
     order = ((lax.axis_index(axis) - jnp.arange(4)) % 4).astype(jnp.int32)
 
     def assemble_kernel(order, *refs):
         for k in range(4):
-            refs[-1][order[k]] = refs[k][...]
+            refs[-2][order[k]] = refs[k][...]
 
     shape = pieces[0].shape
     return pl.pallas_call(
@@ -173,39 +181,62 @@
         grid_spec=pltpu.PrefetchScalarGridSpec(
             num_scalar_prefetch=1,
             grid=(1,),
-            in_specs=[whole(*shape)] * 4 + [ANY] * len(behind),
-            out_specs=whole(4, *shape),
+            in_specs=[whole(*shape)] * 4 + [ANY] * (len(behind) + 1),
+            out_specs=[whole(4, *shape), ANY],
         ),
-        out_shape=shape_of((4,) + shape, pieces[0].dtype),
+        out_shape=[shape_of((4,) + shape), shape_of(through.shape)],
+        input_output_aliases={5 + len(behind): 1},
         compiler_params=params(),
         cost_estimate=cost(0, 16 * pieces[0].size),
         name="assemble_kernel",
-    )(order, *pieces, *behind)
+    )(order, *pieces, *behind, through)
 
 
 def weights_kernel(order, *refs):
     for k in range(4):
         rows = pl.ds(pl.multiple_of(order[k] * 512, 512), 512)
         piece = refs[k][...].reshape(512, AW + QW)
-        refs[4][rows] = piece[:, :AW]
-        refs[5][rows] = piece[:, AW:]
-
-
-def weights_call(pieces):
+        refs[-2][rows] = piece[:, :AW]
+        refs[-1][rows] = piece[:, AW:]
+
+
+def weights_call(pieces, behind):
     order = ((lax.axis_index("y") - jnp.arange(4)) % 4).astype(jnp.int32)
     return pl.pallas_call(
         weights_kernel,
         grid_spec=pltpu.PrefetchScalarGridSpec(
             num_scalar_prefetch=1,
             grid=(1,),
-            in_specs=[whole(*pieces[0].shape)] * 4,
+            in_specs=[whole(*pieces[0].shape)] * 4 + [ANY] * len(behind),
             out_specs=[whole(D, AW), whole(D, QW)],
         ),
         out_shape=[shape_of((D, AW)), shape_of((D, QW))],
         compiler_params=params(),
         cost_estimate=cost(0, 5 * MIB),
         name="weights_kernel",
-    )(order, *pieces)
+    )(order, *pieces, *behind)
+
+
+def small_kernel(key, value, gains, out):
+    cols = gains[...].astype(BF).astype(F32)
+    cols = jnp.concatenate([cols, jnp.zeros((6, 16), F32)], axis=0)
+    cols = jnp.concatenate([cols, jnp.zeros((8, 112), F32)], axis=1)
+    cols = jnp.concatenate([cols, jnp.zeros((120, 128), F32)], axis=0).T[:16].astype(BF)
+    for h in range(KV_HEADS):
+        at = slice(HD * h, HD * (h + 1))
+        block = jnp.concatenate([key[:, at].astype(BF), value[:, at].astype(BF), cols], axis=1)
+        out[32 * h : 32 * h + 16] = block
+        out[32 * h + 16 : 32 * h + 32] = block
+
+
+def small_call(key, value, gains):
+    return pl.pallas_call(
+        small_kernel,
+        out_shape=shape_of((ROWS, 256)),
+        compiler_params=params(),
+        cost_estimate=cost(0, 1 << 17),
+        name="small_kernel",
+    )(key, value, gains)
 
 
 def attend_weights_kernel(kvg, query, mixed, out):
@@ -266,11 +297,12 @@
 
 
 def norm_back_call(parts, x, base, kinds, through=()):
-    vmem = pl.BlockSpec(memory_space=pltpu.VMEM)
+    rows = pl.BlockSpec((ROWS // 2, D), lambda i: (i, 0))
     return pl.pallas_call(
         functools.partial(norm_back_kernel, len(through)),
-        in_specs=[vmem] * 6 + [ANY] * len(through),
-        out_specs=[vmem] * len(kinds) + [ANY] * len(through),
+        grid=(2,),
+        in_specs=[rows] * 6 + [ANY] * len(through),
+        out_specs=[rows] * len(kinds) + [ANY] * len(through),
         out_shape=[shape_of((ROWS, D), kind) for kind in kinds]
         + [shape_of(v.shape, v.dtype) for v in through],
         input_output_aliases={6 + i: len(kinds) + i for i in range(len(through))},
@@ -280,40 +312,84 @@
     )(*parts, x, base, *through)
 
 
-def first_kernel(where, *refs):
-    blocks, (w, tcos, tsin, all_out, q_out, kv_out, inv_out, held, sems) = refs[:8], refs[8:]
-    x = load_blocks((where[4], 1 - where[4]), blocks, held, sems)[...]
-    all_out[...] = x
-    y = dot(x, w[...])
-    x = x.astype(F32)
+def send_products(left, weights, held, sems, outs):
+    copies = []
+    for t in range(4):
+        at, w = weights(t)
+        held[t] = dot_cols(left, w).astype(BF)
+        half = left.shape[0] // 2
+        for i, out in enumerate(outs):
+            rows = pl.ds(i * half, half)
+            copy = pltpu.make_async_copy(held.at[t, rows], out.at[:, at], sems.at[i, t])
+            copy.start()
+            copies.append(copy)
+    for copy in copies:
+        copy.wait()
+
+
+def pick_rows(ref, order):
+    return jnp.concatenate(
+        [ref[pl.ds(pl.multiple_of(order[k] * ROWS, ROWS), ROWS)] for k in range(8)], axis=0
+    )
+
+
+SENT = [pltpu.VMEM((4, SEQ_LEN, 512), BF), pltpu.SemaphoreType.DMA((2, 4))]
+
+
+def front_kernel(order, rows, *refs):
+    pieces, (tcos, tsin, q_out, kv_out, inv_out, out, lse, *outs, held, sems) = refs[:4], refs[4:]
+    step = pl.program_id(0)
+    at = pl.ds(pl.multiple_of(step * 2 * ROWS, 2 * ROWS), 2 * ROWS)
+
+    def piece(k):
+        where = pl.ds(pl.multiple_of(order[8 + k] * 512, 512), 512)
+        return where, pieces[k][...].reshape(512, AW + QW)
+
+    y = 0.0
+    for k in range(4):
+        cols, w = piece(k)
+        y = y + dot(rows[:, cols], w[:, :AW])
+    x = rows[...].astype(F32)
     inv = lax.rsqrt(jnp.mean(x * x, axis=-1, keepdims=True) + EPS)
-    inv_out[...] = jnp.broadcast_to(inv, inv_out.shape)
+    inv_out[at] = jnp.broadcast_to(inv, (2 * ROWS, 128))
     cos, sin = tcos[...] * inv, tsin[...] * inv
     for j in range(2):
         part = y[:, j * 128 : (j + 1) * 128]
-        q_out[:, j * 128 : (j + 1) * 128] = (part * cos + swap_halves(part) * sin).astype(BF)
+        q_out[at, j * 128 : (j + 1) * 128] = (part * cos + swap_halves(part) * sin).astype(BF)
     part = y[:, 256:384]
     is_key = lax.broadcasted_iota(jnp.int32, part.shape, 1) < HD
-    kv_out[...] = jnp.where(is_key, part * cos + swap_halves(part) * sin, part * inv).astype(BF)
-
-
-def first_call(where, blocks, w, tcos, tsin, behind):
-    return blocks_call(
-        first_kernel,
-        where,
-        blocks,
-        (w, tcos, tsin),
-        [pl.BlockSpec((D, AW), lambda i, *_: (0, 0)), by_block(128), by_block(128)],
-        [by_block(D), by_block(QW), by_block(128), by_block(128)],
-        [
-            shape_of((SEQ_LEN, D)),
-            shape_of((SEQ_LEN, QW)),
-            shape_of((SEQ_LEN, 128)),
-            shape_of((SEQ_LEN, 128), F32),
-        ],
-        2 * SEQ_LEN * D * AW,
-        behind,
-    )
+    kv_out[at] = jnp.where(is_key, part * cos + swap_halves(part) * sin, part * inv).astype(BF)
+
+    @pl.when(step == 3)
+    def _():
+        attend_kernel(q_out, kv_out, out, lse)
+
+        def weights(k):
+            cols, w = piece(k)
+            return cols, w[:, AW:]
+
+        send_products(pick_rows(out, order), weights, held, sems, outs)
+
+
+def front_call(order, rows, pieces, tcos, tsin):
+    def block(width):
+        return pl.BlockSpec((2 * ROWS, width), lambda i, *_: (i, 0))
+
+    shapes = [(QW, BF), (128, BF), (128, F32), (QW, BF), (128, F32)]
+    return pl.pallas_call(
+        front_kernel,
+        grid_spec=pltpu.PrefetchScalarGridSpec(
+            num_scalar_prefetch=1,
+            grid=(4,),
+            in_specs=[block(D)] + [whole(4, ROWS, AW + QW)] * 4 + [block(128)] * 2,
+            out_specs=[whole(SEQ_LEN, w) for w, _ in shapes] + [ANY] * 2,
+            scratch_shapes=SENT,
+        ),
+        out_shape=[shape_of((SEQ_LEN, w), t) for w, t in shapes] + [shape_of((4 * ROWS, D))] * 2,
+        compiler_params=params(),
+        cost_estimate=cost(8e9, 16 * MIB, 2 * MIB),
+        name="front_kernel",
+    )(order, rows, *pieces, tcos, tsin)
 
 
 def put_halves(outs, value, cols=slice(None)):
@@ -322,60 +398,103 @@
 
 
 def middle_kernel(where, *refs):
-    blocks, grad_blocks, (w, *refs) = refs[:8], refs[8:16], refs[16:]
-    hiddens, grads, (held, sems, grad_held, grad_sems) = refs[:2], refs[2:4], refs[4:]
-    x = load_blocks((0, 1), blocks, held, sems)[...]
-    c = load_blocks((0, 1), grad_blocks, grad_held, grad_sems)[...]
+    blocks, grad_all, w, refs = refs[:8], refs[8], refs[9], refs[10:]
+    hiddens, grads, outs = refs[:2], refs[2:4], refs[4:6]
+    held, sems, grad_held, grad_sems, wide, down, w_sems, both, sent, sent_sems = refs[6:]
+    step = pl.program_id(0)
+    first = step == 0
+    grad_blocks = [
+        grad_all.at[pl.ds(pl.multiple_of(where[5 + i] * ROWS, ROWS), ROWS)] for i in range(8)
+    ]
+    loads = ((0, 1), blocks, held, sems), ((0, 1), grad_blocks, grad_held, grad_sems)
+
+    def w_copies(j):
+        return (
+            pltpu.make_async_copy(w.at[:, pl.ds(512 * j, 512)], wide.at[j], w_sems.at[0, j]),
+            pltpu.make_async_copy(
+                w.at[:, pl.ds(2 * PAD + 256 * j, 256)], down.at[j], w_sems.at[1, j]
+            ),
+        )
+
+    @pl.when(first)
+    def _():
+        for j in range(4):
+            for load in loads:
+                start_blocks(*load, (j,))
+            if j < TILES // 2:
+                for copy in w_copies(j):
+                    copy.start()
+
+    x, c = (wait_blocks(*load) for load in loads)
     for j in range(TILES // 2):
-        backs = dot(c, w[:, 2 * PAD + 256 * j : 2 * PAD + 256 * (j + 1)])
+
+        @pl.when(first)
+        def _():
+            for copy in w_copies(j):
+                copy.wait()
+
+        backs = dot(c[...], down[j])
         for i in range(2):
             t = 2 * j + i
-            y = dot(x, w[:, 256 * t : 256 * (t + 1)])
+            y = dot(x[...], wide[j, :, 256 * i : 256 * (i + 1)])
             gate, up, back = y[:, :128], y[:, 128:], backs[:, 128 * i : 128 * (i + 1)]
             sigma = jax.nn.sigmoid(gate)
             swish = gate * sigma
             put_halves(hiddens, (swish * up).astype(BF), slice(128 * t, 128 * (t + 1)))
             g = (back * up * (sigma * (1.0 + gate * (1.0 - sigma)))).astype(BF)
-            put_halves(grads, g, slice(256 * t, 256 * t + 128))
-            put_halves(grads, (back * swish).astype(BF), slice(256 * t + 128, 256 * (t + 1)))
-
-
-def middle_call(where, blocks, grad_blocks, w):
+            g = jnp.concatenate([g, (back * swish).astype(BF)], axis=1)
+            cols = slice(256 * t, 256 * (t + 1))
+            put_halves(grads, g, cols)
+            both[step, :, cols] = g[ROWS:]
+            both[4 + step, :, cols] = g[:ROWS]
+
+    @pl.when(step == 3)
+    def _():
+        left = both[...].reshape(SEQ_LEN, 2 * PAD)
+        copies = []
+        for t in range(4):
+            at = slice(512 * t, 512 * (t + 1))
+            y = 0.0
+            for j in range(TILES // 2):
+                y = y + dot_cols(left[:, 512 * j : 512 * (j + 1)], wide[j, at])
+            sent[t] = y.astype(BF)
+            for i, out in enumerate(outs):
+                copy = pltpu.make_async_copy(
+                    sent.at[t, pl.ds(i * 4 * ROWS, 4 * ROWS)],
+                    out.at[:, pl.ds(512 * t, 512)],
+                    sent_sems.at[i, t],
+                )
+                copy.start()
+                copies.append(copy)
+        for copy in copies:
+            copy.wait()
+
+
+def middle_call(where, blocks, grad_all, w):
     return blocks_call(
         middle_kernel,
         where,
         blocks,
-        (*grad_blocks, w),
-        [ANY] * 8 + [whole(D, 3 * PAD)],
-        [by_step(PAD)] * 2 + [by_step(2 * PAD)] * 2,
-        [shape_of((4 * ROWS, PAD))] * 2 + [shape_of((4 * ROWS, 2 * PAD))] * 2,
-        2 * SEQ_LEN * D * 3 * PAD,
-        scratch=HELD * 2,
-    )
-
-
-def mixed_grad_kernel(where, *refs):
-    blocks, (w, all_out, grad_out, held, sems) = refs[:8], refs[8:]
-    x = load_blocks((where[4], 1 - where[4]), blocks, held, sems)[...]
-    all_out[...] = x
-    grad_out[...] = dot(x, w[...]).astype(BF)
-
-
-def mixed_grad_call(where, blocks, w):
-    return blocks_call(
-        mixed_grad_kernel,
-        where,
-        blocks,
-        (w,),
-        [whole(D, QW)],
-        [by_block(D), by_block(QW)],
-        [shape_of((SEQ_LEN, D)), shape_of((SEQ_LEN, QW))],
-        2 * SEQ_LEN * D * QW,
-    )
-
-
-def partial_kernel(n_in, n_behind, order, *refs):
-    w, across, own = refs[n_in], refs[-2], refs[-1]
+        (grad_all, w),
+        [ANY] * 2,
+        [by_step(PAD)] * 2 + [by_step(2 * PAD)] * 2 + [ANY] * 2,
+        [shape_of((4 * ROWS, PAD))] * 2
+        + [shape_of((4 * ROWS, 2 * PAD))] * 2
+        + [shape_of((4 * ROWS, D))] * 2,
+        2 * SEQ_LEN * D * 5 * PAD,
+        scratch=HELD * 2
+        + [
+            pltpu.VMEM((TILES // 2, D, 512), BF),
+            pltpu.VMEM((TILES // 2, D, 256), BF),
+            pltpu.SemaphoreType.DMA((2, TILES // 2)),
+            pltpu.VMEM((8, ROWS, 2 * PAD), BF),
+        ]
+        + SENT,
+    )
+
+
+def partial_kernel(n_in, n_behind, n_through, order, *refs):
+    w, (across, own) = refs[n_in], refs[n_in + 1 + n_behind + n_through :][:2]
     if n_in == 1:
         a = refs[0]
         left = jnp.concatenate(
@@ -388,40 +507,62 @@
     own[...] = y[4 * ROWS :]
 
 
-def partial_call(order, a, w, col, tile, behind=()):
-    depth = a[0].shape[1]
-    return pl.pallas_call(
-        functools.partial(partial_kernel, len(a), len(behind)),
+def partial_call(order, a, w, col, tile, behind=(), through=()):
+    depth, first = a[0].shape[1], 2 + len(a) + len(behind)
+    return pl.pallas_call(
+        functools.partial(partial_kernel, len(a), len(behind), len(through)),
         grid_spec=pltpu.PrefetchScalarGridSpec(
             num_scalar_prefetch=1,
             grid=(D // tile,),
             in_specs=[whole(*v.shape) for v in a]
             + [pl.BlockSpec((tile, depth), lambda i, *_: (i, col))]
-            + [ANY] * len(behind),
-            out_specs=[pl.BlockSpec((4 * ROWS, tile), lambda i, *_: (0, i))] * 2,
+            + [ANY] * len(behind + through),
+            out_specs=[pl.BlockSpec((4 * ROWS, tile), lambda i, *_: (0, i))] * 2
+            + [ANY] * len(through),
         ),
-        out_shape=[shape_of((4 * ROWS, D))] * 2,
+        out_shape=[shape_of((4 * ROWS, D))] * 2 + [shape_of(v.shape, v.dtype) for v in through],
+        input_output_aliases={first + i: 2 + i for i in range(len(through))},
         compiler_params=params(),
         cost_estimate=cost(2 * 8 * ROWS * D * depth, 2 * depth * (D + 1024) + 4 * MIB),
         name="partial_kernel",
-    )(order, *a, w, *behind)
+    )(order, *a, w, *behind, *through)
 
 
 def add_kernel(n_behind, across, own, *refs):
-    for k, ref in enumerate(refs[n_behind:]):
-        rows = slice(k * ROWS, (k + 1) * ROWS)
-        ref[...] = (across[rows].astype(F32) + own[rows].astype(F32)).astype(BF)
+    n = own.shape[0] // ROWS
+    outs, (held, sems) = refs[n_behind : n_behind + n], refs[n_behind + n :]
+    loads, stores = [], []
+    for k in range(n):
+        rows = pl.ds(k * ROWS, ROWS)
+        loads.append(
+            [
+                pltpu.make_async_copy(ref.at[rows], held.at[i, k], sems.at[i, k])
+                for i, ref in enumerate((across, own))
+            ]
+        )
+        stores.append(pltpu.make_async_copy(held.at[2, k], outs[k], sems.at[2, k]))
+    for pair in loads:
+        for copy in pair:
+            copy.start()
+    for k in range(n):
+        for copy in loads[k]:
+            copy.wait()
+        held[2, k] = (held[0, k].astype(F32) + held[1, k].astype(F32)).astype(BF)
+        stores[k].start()
+    for copy in stores:
+        copy.wait()
 
 
 def add_call(across, own, behind=()):
-    vmem = pl.BlockSpec(memory_space=pltpu.VMEM)
+    n = own.shape[0] // ROWS
     return pl.pallas_call(
         functools.partial(add_kernel, len(behind)),
-        in_specs=[vmem] * 2 + [ANY] * len(behind),
-        out_specs=[vmem] * 4,
-        out_shape=[shape_of((ROWS, D))] * 4,
-        compiler_params=params(),
-        cost_estimate=cost(0, 6 * MIB),
+        in_specs=[ANY] * (2 + len(behind)),
+        out_specs=[ANY] * n,
+        out_shape=[shape_of((ROWS, D))] * n,
+        scratch_shapes=[pltpu.VMEM((3, n, ROWS, D), BF), pltpu.SemaphoreType.DMA((3, n))],
+        compiler_params=params(),
+        cost_estimate=cost(0, 6 * own.size),
         name="add_kernel",
     )(across, own, *behind)
 
@@ -465,16 +606,6 @@
         for h in range(4):
             spread_out = jnp.where(lane == h, log_total[ROWS * h : ROWS * (h + 1)], spread_out)
         lse[rows] = spread_out
-
-
-def attend_call(q, kv):
-    return pl.pallas_call(
-        attend_kernel,
-        out_shape=[shape_of((SEQ_LEN, QW)), shape_of((SEQ_LEN, 128), F32)],
-        compiler_params=params(),
-        cost_estimate=cost(4e9, 2 * MIB, 2 * MIB),
-        name="attend_kernel",
-    )(q, kv)
 
 
 def attend_back_kernel(
@@ -517,18 +648,51 @@
         put(rows, slice(QW, AW), held[:, rows].T, is_key)
 
 
-def attend_back_call(q, kv, lse, mixed_grad, tcos, tsin, inv):
-    return pl.pallas_call(
-        attend_back_kernel,
-        out_shape=[shape_of((SEQ_LEN, AW))] * 2,
-        scratch_shapes=[pltpu.VMEM((128, SEQ_LEN), F32)],
-        compiler_params=params(),
-        cost_estimate=cost(8e9, 4 * MIB, 2 * MIB),
-        name="attend_back_kernel",
-    )(q, kv, lse, mixed_grad, tcos, tsin, inv)
-
-
-def wgrad_kernel(counts, *refs):
+def back_kernel(where, *refs):
+    blocks, refs = refs[:8], refs[8:]
+    w_mixed, w, q, kv, lse, tcos, tsin, inv, all_out, scaled, *outs = refs[:12]
+    held, sems, mixed_grad, grad, kv_held, sent, sent_sems = refs[12:]
+    step = pl.program_id(0)
+    x = load_blocks((where[4], 1 - where[4]), blocks, held, sems)
+    all_out[...] = x[...]
+    at = pl.ds(pl.multiple_of(where[step] * 2 * ROWS, 2 * ROWS), 2 * ROWS)
+    mixed_grad[at] = dot(x[...], w_mixed[...]).astype(BF)
+
+    @pl.when(step == 3)
+    def _():
+        attend_back_kernel(q, kv, lse, mixed_grad, tcos, tsin, inv, grad, scaled, kv_held)
+        left = pick_rows(grad, [where[5 + k] for k in range(8)])
+        send_products(
+            left,
+            lambda t: (pl.ds(512 * t, 512), w[512 * t : 512 * (t + 1)]),
+            sent,
+            sent_sems,
+            outs,
+        )
+
+
+def back_call(where, blocks, *operands):
+    widths = [QW, 128, 128, 128, 128, 128]
+    return blocks_call(
+        back_kernel,
+        where,
+        blocks,
+        operands,
+        [whole(D, QW), whole(D, AW)] + [whole(SEQ_LEN, w) for w in widths],
+        [by_block(D), whole(SEQ_LEN, AW)] + [ANY] * 2,
+        [shape_of((SEQ_LEN, D)), shape_of((SEQ_LEN, AW))] + [shape_of((4 * ROWS, D))] * 2,
+        2 * SEQ_LEN * D * (QW + AW) + 8e9,
+        scratch=HELD
+        + [
+            pltpu.VMEM((SEQ_LEN, QW), BF),
+            pltpu.VMEM((SEQ_LEN, AW), BF),
+            pltpu.VMEM((128, SEQ_LEN), F32),
+        ]
+        + SENT,
+    )
+
+
+def wgrad_kernel(counts, order, *refs):
     out = refs[-1]
     at, ref = 0, 0
     for group in counts:
@@ -542,27 +706,37 @@
         at += total.shape[1]
 
 
-def wgrad_call(tile, *groups, behind=()):
+def wgrad_call(order, tile, *groups, behind=()):
     in_specs, operands, width = [], [], 0
     for group in groups:
-        for x, g in group:
-            in_specs += [pl.BlockSpec((v.shape[0], tile), lambda i: (0, i)) for v in x]
-            in_specs.append(pl.BlockSpec(g.shape, lambda i: (0, 0)))
-            operands += [*x, g]
+        for i, (x, g) in enumerate(group):
+            if isinstance(x, tuple):
+                in_specs += [
+                    pl.BlockSpec((ROWS, tile), lambda i, order, at=at: (order[at], i))
+                    for at in x[1]
+                ]
+                group[i] = ([x[0]] * len(x[1]), g)
+            else:
+                in_specs += [pl.BlockSpec((v.shape[0], tile), lambda i, *_: (0, i)) for v in x]
+            in_specs.append(whole(*g.shape))
+            operands += [*group[i][0], g]
         width += group[0][1].shape[1]
     counts = tuple(tuple(len(x) for x, _ in group) for group in groups)
     return pl.pallas_call(
         functools.partial(wgrad_kernel, counts),
-        grid=(D // tile,),
-        in_specs=in_specs + [ANY] * len(behind),
-        out_specs=pl.BlockSpec((tile, width), lambda i: (i, 0)),
+        grid_spec=pltpu.PrefetchScalarGridSpec(
+            num_scalar_prefetch=1,
+            grid=(D // tile,),
+            in_specs=in_specs + [ANY] * len(behind),
+            out_specs=pl.BlockSpec((tile, width), lambda i, *_: (i, 0)),
+        ),
         out_shape=shape_of((D, width)),
         compiler_params=params(),
         cost_estimate=cost(
             2 * SEQ_LEN * D * width, 4 * MIB * len(groups) + 2 * width * (SEQ_LEN + D)
         ),
         name="wgrad_kernel",
-    )(*operands, *behind)
+    )(order, *operands, *behind)
 
 
 WIDE_RATE = 2.0 * D ** (-0.5)
@@ -638,18 +812,12 @@
     heads = [parts[2 * h] + parts[2 * h + 1] for h in range(KV_HEADS)]
     key = jnp.concatenate([v[:, :HD] for v in heads], axis=1)
     value = jnp.concatenate([v[:, HD : 2 * HD] for v in heads], axis=1)
-    adamw(refs[0:3], refs[6:9], key, WIDE_RATE)
-    adamw(refs[3:6], refs[9:12], value, WIDE_RATE)
-    refs[12][...] = functools.reduce(jnp.add, [v[:, 128:] for v in heads])
-
-
-def adamw_step(weight, first, second, gradient, rate, decay):
-    first_new = BETA_ONE * first + (1.0 - BETA_ONE) * gradient
-    second_new = BETA_TWO * second + (1.0 - BETA_TWO) * gradient * gradient
-    first_hat = first_new / (1.0 - BETA_ONE**STEP)
-    second_hat = second_new / (1.0 - BETA_TWO**STEP)
-    weight_new = weight - rate * (first_hat / (jnp.sqrt(second_hat) + ADAM_EPS) + decay * weight)
-    return (weight_new, first_new, second_new)
+    adamw(refs[0:3], refs[9:12], key, WIDE_RATE)
+    adamw(refs[3:6], refs[12:15], value, WIDE_RATE)
+    sums = functools.reduce(jnp.add, [v[:, 128:] for v in heads])
+    sums = jnp.concatenate([sums, jnp.zeros((112, 128), F32)], axis=0).T[:2, :16]
+    sums = sums / refs[6][...].astype(BF).astype(F32)
+    adamw(refs[6:9], refs[15:18], sums, 0.3, 0.0)
 
 
 def rotary():
@@ -694,45 +862,29 @@
     z, core = lax.axis_index("z"), lax.axis_index("core")
     dp, ctx = ("y", "x"), ("z", "core")
     back = (z - jnp.arange(4)) % 4
-    where = jnp.concatenate([back, core[None]]).astype(jnp.int32)
-    order = jnp.concatenate([2 * back + 1 - core, 2 * back + core]).astype(jnp.int32)
-
-    small = jnp.concatenate(
-        [
-            w_key.astype(BF).reshape(16, 4, HD),
-            w_value.astype(BF).reshape(16, 4, HD),
-            jnp.broadcast_to(
-                jnp.pad(norm_gains.astype(BF).T, ((0, 0), (0, 126)))[:, None, :], (16, 4, 128)
-            ),
-        ],
-        axis=2,
-    ).transpose(1, 0, 2)
-    small = jnp.broadcast_to(small[:, None], (4, 2, 16, 256)).reshape(ROWS, 256)
+    y_back = (lax.axis_index("y") - jnp.arange(4)) % 4
+    order = jnp.concatenate([2 * back + 1 - core, 2 * back + core, y_back]).astype(jnp.int32)
+    where = jnp.concatenate([back, core[None], order[4:8], order[:4]]).astype(jnp.int32)
+    back_where = jnp.concatenate([back, core[None], order[:8]]).astype(jnp.int32)
+
+    small = small_call(w_key, w_value, norm_gains)
     kvg = swap_blocks(small, ctx)
     gain_one = kvg[:, 128:129].astype(F32)
 
-    token_blocks = spread_z(tokens[0])
-    grad_blocks = spread_z(cotangent[0])
+    tcos, tsin = rotary()
+    tokens_all = lax.all_gather(tokens[0], ctx, axis=0, tiled=True)
+    grad_all = lax.all_gather(cotangent[0], ctx, axis=0, tiled=True)
     w_attend = attend_weights_call(kvg, w_query, w_out)
-    near_attend = assemble_call("x", came(w_attend, "x"), token_blocks[1:])
+    w_ffn = ffn_weights_call(kvg, w_gate.T, w_up.T, w_down, (w_attend,))
+    near_attend, w_ffn = assemble_call("x", came(w_attend, "x"), (tcos, tsin), w_ffn)
     far_attend = came(near_attend, "y")
-    w_ffn = ffn_weights_call(
-        kvg, w_gate.T, w_up.T, w_down, far_attend[1:] + grad_blocks[1:]
+    query, key_value, inv_all, attended, lse, *mixed_parts = front_call(
+        order, tokens_all, far_attend, tcos, tsin
     )
     all_ffn = lax.all_gather(w_ffn, dp, axis=0, tiled=True)
-    all_attend, all_mixed = weights_call(far_attend)
-    token_blocks = token_blocks + [other_core(t) for t in token_blocks]
-
-    tcos, tsin = rotary()
-    tokens_all, query, key_value, inv_all = first_call(
-        where, token_blocks, all_attend, tcos, tsin, ()
-    )
-    grad_blocks = grad_blocks + [other_core(t) for t in grad_blocks]
-    attended, lse = attend_call(query, key_value)
-
-    def reduce_core(a, w, col, tile, behind=()):
-        across, own = partial_call(order, a, w, col, tile)
-        return add_call(other_core(across), own, behind)
+
+    def reduce_core(partials, behind=()):
+        return add_call(other_core(partials[0]), partials[1], behind)
 
     def reduce_z(parts):
         return [parts[0]] + [ring("z", 4 - k)(parts[k]) for k in (1, 2, 3)]
@@ -740,19 +892,23 @@
     def total(parts):
         return functools.reduce(jnp.add, [t.astype(F32) for t in parts])
 
-    mixed_parts = reduce_core((attended,), all_mixed, 0, 1024, grad_blocks[5:])
+    mixed_parts = reduce_core(mixed_parts)
+    all_attend, all_mixed = weights_call(far_attend, mixed_parts[:1])
     middle = tokens[0].astype(F32) + total(reduce_z(mixed_parts))
     inv_second = lax.rsqrt(jnp.mean(middle * middle, axis=-1, keepdims=True) + EPS)
     unit_second = middle * inv_second
 
     mid_blocks = spread(unit_second.astype(BF))
-    hidden0, hidden1, wide0, wide1 = middle_call(where, mid_blocks, grad_blocks, all_ffn)
-    wide_parts = reduce_core((wide1, wide0), all_ffn, 0, 512)
+    hidden0, hidden1, wide0, wide1, *wide_parts = middle_call(
+        where, mid_blocks, grad_all, all_ffn
+    )
+    wide_parts = reduce_core(wide_parts, (all_mixed,))
     mid_parts = reduce_z(wide_parts)
     ffn_wgrad = wgrad_call(
+        order,
         256,
-        ((mid_blocks[:4], wide0), (mid_blocks[4:], wide1)),
-        ((grad_blocks[:4], hidden0), (grad_blocks[4:], hidden1)),
+        [(mid_blocks[:4], wide0), (mid_blocks[4:], wide1)],
+        [((grad_all, range(4, 8)), hidden0), ((grad_all, range(4)), hidden1)],
         behind=wide_parts[:1],
     )
     down_sums = partial_call(order, (hidden1, hidden0), all_ffn, 2, 512, wide_parts[:1])
@@ -760,18 +916,18 @@
         mid_parts, middle, cotangent[0], (F32, BF), (ffn_wgrad, *down_sums)
     )
     ffn_sum = lax.psum_scatter(ffn_wgrad, dp, scatter_dimension=0, tiled=True)
-    mid_grad_all, mixed_grad = mixed_grad_call(where, spread(middle_low), all_mixed)
-    attend_grad, scaled_grad = attend_back_call(
-        query, key_value, lse, mixed_grad, tcos, tsin, inv_all
+    mid_grad_blocks = spread(middle_low)
+    mid_grad_all, scaled_grad, *in_parts = back_call(
+        back_where, mid_grad_blocks, all_mixed, all_attend, query, key_value, lse, tcos, tsin, inv_all
     )
     attend_wgrad = wgrad_call(
-        512, (([tokens_all], scaled_grad),), (([mid_grad_all], attended),)
-    )
+        order, 512, [([tokens_all], scaled_grad)], [([mid_grad_all], attended)]
+    )
+    in_parts = reduce_core(in_parts, (attend_wgrad,))
     attend_parts = swap_blocks(attend_wgrad, dp)
-    in_parts = reduce_core((attend_grad,), all_attend, 0, 1024)
     in_parts = reduce_z(in_parts)
     (input_grad,) = norm_back_call(in_parts, tokens[0], middle_grad, (BF,))
-    down_parts = add_call(other_core(down_sums[0]), down_sums[1], in_parts[1::2])
+    down_parts = add_call(other_core(down_sums[0]), down_sums[1], in_parts[1:2])
     output = middle + total(reduce_z(down_parts))
 
     *wide_new, gain_two_sum = step_call(
@@ -792,22 +948,24 @@
         [shape_of((ROWS, 256), F32)],
     )
     tail = swap_blocks(tail, ctx).reshape(8, 16, 256)
-    *kv_new, gains_sum = step_call(
+    last_new = step_call(
         last_step_kernel,
         (tail,),
-        ((w_key, key_first, key_second), (w_value, value_first, value_second)),
-        [shape_of((16, 128), F32)],
-    )
-    gains_sum = gains_sum[:, :2].T / norm_gains.astype(BF).astype(F32)
-    gains_new = adamw_step(norm_gains, gains_first, gains_second, gains_sum, 0.3, 0.0)
+        (
+            (w_key, key_first, key_second),
+            (w_value, value_first, value_second),
+            (norm_gains, gains_first, gains_second),
+        ),
+        [],
+    )
     return (
         output.astype(BF)[None],
         input_grad[None],
         *query_new[:3],
-        *kv_new,
+        *last_new[:6],
         *query_new[3:],
         *wide_new,
-        *gains_new,
+        *last_new[6:],
     )
 
 

time: 422 us -> 371 us (0.88)
  waiting for transfers between devices: 154 us -> 126 us
  Pallas kernels: 151 us -> 140 us
  local copies, waits for them, and re-layouts: 15.4 us -> 9.78 us
    ppermute x12 -> x6, waiting for transfers between devices: 67 us -> 30.7 us  [spread_z(): return [v, ring('z', 1)(v), ring('z', 2)(v), ring('z', 3)(v)]]
    pallas_call x14 -> x11, Pallas kernels: 95.2 us -> 70.1 us  [the longest x2 25.7 us: wgrad_call(): pl.pallas_call(functools.partial(wgrad_kernel, counts), grid_spec=pltpu.P...]
    pallas_call x3 -> x2, Pallas kernels: 34 us -> 48.7 us  [blocks_call(): pl.pallas_call(body, grid_spec=pltpu.PrefetchScalarGridSpec(num_scalar_pr...]
    ppermute x6, waiting for transfers between devices: 13.8 us -> 27.5 us  [came(): return [v] + [ring(axis, k)(v) for k in (1, 2, 3)]]
    all_to_all x3, starting transfers between devices: 24.8 us -> 16.1 us  [swap_blocks(): return lax.all_to_all(v, axes, split_axis=0, concat_axis=0, tiled=True)]
    ppermute x20 -> x12, starting transfers between devices: 12.7 us -> 21 us  [other_core(): return lax.ppermute(v, 'core', [(0, 1), (1, 0)])]
    ppermute x12 -> x6, starting transfers between devices: 13.8 us -> 7.03 us  [spread_z(): return [v, ring('z', 1)(v), ring('z', 2)(v), ring('z', 3)(v)]]
    ppermute x20 -> x12, waiting for transfers between devices: 14.2 us -> 7.97 us  [other_core(): return lax.ppermute(v, 'core', [(0, 1), (1, 0)])]
  transfers between devices with their start and end apart: 55 -> 43, of which waited for: 30 -> 22; matrix products, arithmetic and copies ran while one was open for 2% -> 2% of each run, Pallas kernels for 26% -> 29%
where the time goes in v3:
time: 371 us; the launch traced here: 365 us
  Pallas kernels  140 us (38%)
  waiting for transfers between devices  126 us (34%)
  starting transfers between devices  66.4 us (18%)
  between operations  14.4 us (4%)
  local copies, waits for them, and re-layouts  9.78 us (3%)
  other arithmetic  8.96 us (2%)
    pallas_call x2, Pallas kernels, blocks_call(): pl.pallas_call(body, grid_spec=pltpu.PrefetchScalarGridSpec(num_scalar_pr...  48.7 us
    ppermute x12, waiting for transfers between devices, reduce_z(): return [parts[0]] + [ring('z', 4 - k)(parts[k]) for k in (1, 2, 3)]  44.9 us
    ppermute x6, waiting for transfers between devices, spread_z(): return [v, ring('z', 1)(v), ring('z', 2)(v), ring('z', 3)(v)]  30.7 us
    ppermute x6, waiting for transfers between devices, came(): return [v] + [ring(axis, k)(v) for k in (1, 2, 3)]  27.5 us
    pallas_call x2, Pallas kernels, wgrad_call(): pl.pallas_call(functools.partial(wgrad_kernel, counts), grid_spec=pltpu.P...  25.7 us
    ppermute x12, starting transfers between devices, other_core(): return lax.ppermute(v, 'core', [(0, 1), (1, 0)])  21 us
    all_to_all x3, starting transfers between devices, swap_blocks(): return lax.all_to_all(v, axes, split_axis=0, concat_axis=0, tiled=True)  16.1 us
    pallas_call x1, Pallas kernels, front_call(): pl.pallas_call(front_kernel, grid_spec=pltpu.PrefetchScalarGridSpec(num_s...  16.1 us
  transfers between devices with their start and end apart: 43, of which 22 were waited for; matrix products, arithmetic and copies ran while one was open for 2% of the time, Pallas kernels for 29%

profile of v3, /device:TPU:1, one launch (start us, length us, event | category | flops | bytes accessed | tf_op | source)
XLA Modules:
  0.0 365.3 jit_solution(13556740577457754882)
XLA Ops:
  10.1 6.8 %all-to-all-start = ((bf16[8,16,256]{2,1,0:T(8,128)(2,1)}), bf16[8,16,256]{2,1,0:T(8,128)(2,1)S(1)}, u32[]{:S(2)}, u32[]{:S(2)}) async-start(bf16[8,16,256]{2,1,0:T(8,128)(2,1)} %bitcast.54), calls=%async_computation | async-start | bytes 131072 | tf_op jit(solution)/shard_map/all_to_all | solution.py:90
  18.9 2.9 all-to-all-done
  44.5 10.4 %collective-permute-done.3.refs_1_ = bf16[4,128,640]{2,1,0:T(8,128)(2,1)S(1)} collective-permute-done((bf16[4,128,640]{2,1,0:T(8,128)(2,1)}, bf16[4,128,640]{2,1,0:T(8,128)(2,1)S(1)}, u32[]{:S(2)}, u32[]{:S(2)}) %collective-permute-start.3) | collective-permute-done | bytes 655392 | tf_op jit(solution)/shard_map/ppermute | solution.py:86
  54.9 15.2 %collective-permute-done.4.refs_2_ = bf16[4,128,640]{2,1,0:T(8,128)(2,1)S(1)} collective-permute-done((bf16[4,128,640]{2,1,0:T(8,128)(2,1)}, bf16[4,128,640]{2,1,0:T(8,128)(2,1)S(1)}, u32[]{:S(2)}, u32[]{:S(2)}) %collective-permute-start.4) | collective-permute-done | bytes 655392 | tf_op jit(solution)/shard_map/ppermute | solution.py:86
  71.5 16.1 %front_kernel.1 = (bf16[1024,256]{1,0:T(8,128)(2,1)}, bf16[1024,128]{1,0:T(8,128)(2,1)}, f32[1024,128]{1,0:T(8,128)}, bf16[1024,256]{1,0:T(8,128)(2,1)}, f32[102...) custom-call(s32[12]{0:T(128)} %pad_add_fusion.order, bf16[1024,2048]{1,0:T(8,128)(2,1)} %bitcast.38, ...), custom_call_target="tpu_custom_call" | custom-call | flops 8000000000 | bytes 16777216 | tf_op jit(solution)/shard_map/front_kernel/pallas_call | solution.py:379
  89.8 4.0 %collective-permute-done.6.across = bf16[512,2048]{1,0:T(8,128)(2,1)S(1)} collective-permute-done((bf16[512,2048]{1,0:T(8,128)(2,1)}, bf16[512,2048]{1,0:T(8,128)(2,1)S(1)}, u32[]{:S(2)}, u32[]{:S(2)}) %collective-permute-start.6) | collective-permute-done | bytes 2097184 | tf_op jit(solution)/shard_map/ppermute | solution.py:73
  95.1 3.2 add_kernel.4
  100.5 11.4 %collective-permute-done.7 = bf16[128,2048]{1,0:T(8,128)(2,1)S(1)} collective-permute-done((bf16[128,2048]{1,0:T(8,128)(2,1)}, bf16[128,2048]{1,0:T(8,128)(2,1)S(1)}, u32[]{:S(2)}, u32[]{:S(2)}) %collective-permute-start.7) | collective-permute-done | bytes 524320 | tf_op jit(solution)/shard_map/ppermute | solution.py:890
  113.8 12.3 %collective-permute-done.9 = bf16[128,2048]{1,0:T(8,128)(2,1)S(1)} collective-permute-done((bf16[128,2048]{1,0:T(8,128)(2,1)}, bf16[128,2048]{1,0:T(8,128)(2,1)S(1)}, u32[]{:S(2)}, u32[]{:S(2)}) %collective-permute-start.9) | collective-permute-done | bytes 524320 | tf_op jit(solution)/shard_map/ppermute | solution.py:890
  132.4 21.1 %collective-permute-done.10.refs_1_ = bf16[128,2048]{1,0:T(8,128)(2,1)S(1)} collective-permute-done((bf16[128,2048]{1,0:T(8,128)(2,1)S(1)}, bf16[128,2048]{1,0:T(8,128)(2,1)S(1)}, u32[]{:S(2)}, u32[]{:S(2)}) %collective-permute-start.10) | collective-permute-done | bytes 524320 | tf_op jit(solution)/shard_map/ppermute | solution.py:77
  157.9 27.7 %middle_kernel.1 = (bf16[512,768]{1,0:T(8,128)(2,1)}, bf16[512,768]{1,0:T(8,128)(2,1)}, bf16[512,1536]{1,0:T(8,128)(2,1)}, bf16[512,1536]{1,0:T(8,128)(2,1)}, bf...) custom-call(s32[13]{0:T(128)} %get-tuple-element.172.where, bf16[128,2048]{1,0:T(8,128)(2,1)} %copy-done.3, ...), custom_call_target="tpu_custom_call" | custom-call | flops 16106127360 | bytes 26738688 | tf_op jit(solution)/shard_map/middle_kernel/pallas_call | solution.py:154
  186.0 4.1 %weights_kernel.1 = (bf16[2048,384]{1,0:T(8,128)(2,1)}, bf16[2048,256]{1,0:T(8,128)(2,1)}) custom-call(s32[4]{0:T(128)} %copy-done.26, bf16[4,128,640]{2,1,0:T(8,128)(2,1)} %get-tuple-element.96.refs_0_, bf16[4,128,640]{2,1,0:T(8,128)(2,1)} %copy-done.10, bf16[4,128,640]{2,1,0:T(8,128)(2,1)} %copy-done.11, bf16[4,128,640]{2,1,0:T(8,128)(2,1)} %copy-done.12, ...), custom_call_target="tpu_custom_call" | custom-call | bytes 5242880 | tf_op jit(solution)/shard_map/weights_kernel/pallas_call | solution.py:205
  191.4 3.1 add_kernel.5
  197.6 17.0 %wgrad_kernel.2.refs_6_ = bf16[2048,2304]{1,0:T(8,128)(2,1)} custom-call(s32[12]{0:T(128)} %pad_add_fusion.order, bf16[128,2048]{1,0:T(8,128)(2,1)} %copy-done.3, bf16[128,2048]{1,0:T(8,128)(2,1)} %copy-done.13, bf16[128,2048]{1,0:T(8,128)(2,1)} %copy-done.14, bf16[128,2048]{1,0:T(8,128)(2,1)} %copy-done.15, bf16[512,1536]{1,0:T(8,128)(2,1)} %get-tuple-element.111.refs_4_, ...), custom_call_target="tpu_custom_call" | custom-call | flops 9663676416 | bytes 22544384 | tf_op jit(solution)/shard_map/wgrad_kernel/pallas_call | solution.py:725
  214.6 7.7 %partial_kernel.1 = (bf16[512,2048]{1,0:T(8,128)(2,1)}, bf16[512,2048]{1,0:T(8,128)(2,1)}) custom-call(s32[12]{0:T(128)} %pad_add_fusion.order, bf16[512,768]{1,0:T(8,128)(2,1)} %get-tuple-element.114.refs_19_.refs_0_, bf16[512,768]{1,0:T(8,128)(2,1)} %get-tuple-element.113.refs_14_.refs_1_, bf16[2048,2304]{1,0:T(8,128)(2,1)} %all-gather.6.cloned.1.call-done.refs_9_.refs_2_, ...), custom_call_target="tpu_custom_call" | custom-call | flops 3221225472 | bytes 8912896 | tf_op jit(solution)/shard_map/partial_kernel/pallas_call | solution.py:512
  224.1 3.3 norm_back_kernel.2
  234.1 9.6 %collective-permute-done.22.refs_1_ = bf16[128,2048]{1,0:T(8,128)(2,1)S(1)} collective-permute-done((bf16[128,2048]{1,0:T(8,128)(2,1)S(1)}, bf16[128,2048]{1,0:T(8,128)(2,1)S(1)}, u32[]{:S(2)}, u32[]{:S(2)}) %collective-permute-start.22) | collective-permute-done | bytes 524320 | tf_op jit(solution)/shard_map/ppermute | solution.py:77
  243.7 11.7 %collective-permute-start.26 = (bf16[128,2048]{1,0:T(8,128)(2,1)S(1)}, bf16[128,2048]{1,0:T(8,128)(2,1)S(1)}, u32[]{:S(2)}, u32[]{:S(2)}) collective-permute-start(bf16[128,2048]{1,0:T(8,128)(2,1)S(1)} %collective-permute-done.22.refs_1_), channel_id=1, source_target_pairs={{0,1},{1,0},{2,3},{3,2},{4,5},{5,4},{6,7},{7,6},{8,9},{9,8},{10,11... | collective-permute-start | bytes 1572872 | tf_op jit(solution)/shard_map/ppermute | solution.py:73
  259.2 21.0 %back_kernel.1 = (bf16[1024,2048]{1,0:T(8,128)(2,1)}, bf16[1024,384]{1,0:T(8,128)(2,1)}, bf16[512,2048]{1,0:T(8,128)(2,1)}, bf16[512,2048]{1,0:T(8,128)(2,1)}) custom-call(s32[13]{0:T(128)} %get-tuple-element.171.where, bf16[128,2048]{1,0:T(8,128)(2,1)} %get-tuple-element.119.refs_0_, bf16[128,2048]{1,0:T(8,128)(2,1)} %copy-done.28, ...), custom_call_target="tpu_custom_call" | custom-call | flops 10684354560 | bytes 18874368 | tf_op jit(solution)/shard_map/back_kernel/pallas_call | solution.py:154
  281.0 8.6 %wgrad_kernel.3.refs_0_ = bf16[2048,640]{1,0:T(8,128)(2,1)} custom-call(s32[12]{0:T(128)} %pad_add_fusion.order, bf16[1024,2048]{1,0:T(8,128)(2,1)} %bitcast.39, bf16[1024,384]{1,0:T(8,128)(2,1)} %get-tuple-element.127.refs_1_, bf16[1024,2048]{1,0:T(8,128)(2,1)} %get-tuple-element.128.refs_2_, bf16[1024,256]{1,0:T(8,128)(2,1)} %get-tuple-element.129.refs_3_), custom_call_target="tpu_custom_call" | custom-call | flops 2684354560 | bytes 12320768 | tf_op jit(solution)/shard_map/wgrad_kernel/pallas_call | solution.py:725
  289.7 4.5 %all-to-all-start.1 = ((bf16[16,128,640]{2,1,0:T(8,128)(2,1)}), bf16[16,128,640]{2,1,0:T(8,128)(2,1)}, u32[]{:S(2)}, u32[]{:S(2)}) async-start(bf16[16,128,640]{2,1,0:T(8,128)(2,1)} %bitcast.36), calls=%async_computation.1 | async-start | bytes 5242880 | tf_op jit(solution)/shard_map/all_to_all | solution.py:90
  294.1 3.2 add_kernel.6
  300.2 10.8 %collective-permute-done.30.refs_0_.refs_1_ = bf16[128,2048]{1,0:T(8,128)(2,1)S(1)} collective-permute-done((bf16[128,2048]{1,0:T(8,128)(2,1)}, bf16[128,2048]{1,0:T(8,128)(2,1)S(1)}, u32[]{:S(2)}, u32[]{:S(2)}) %collective-permute-start.30) | collective-permute-done | bytes 524320 | tf_op jit(solution)/shard_map/ppermute | solution.py:890
  311.9 3.2 add_kernel.7
  315.1 3.4 collective-permute-start.31
  319.9 7.4 %collective-permute-done.35.refs_3_ = bf16[128,2048]{1,0:T(8,128)(2,1)S(1)} collective-permute-done((bf16[128,2048]{1,0:T(8,128)(2,1)}, bf16[128,2048]{1,0:T(8,128)(2,1)S(1)}, u32[]{:S(2)}, u32[]{:S(2)}) %collective-permute-start.35) | collective-permute-done | bytes 524320 | tf_op jit(solution)/shard_map/ppermute | solution.py:890
  328.1 3.1 norm_back_kernel.3
  331.2 6.2 %reduce-scatter.2.cloned.1.call-done.sums = bf16[128,2304]{1,0:T(8,128)(2,1)} async-done(((bf16[2048,2304]{1,0:T(8,128)(2,1)}), bf16[128,2304]{1,0:T(8,128)(2,1)}) %reduce-scatter.2.cloned.1.call-update) | async-done | bytes 589840 | tf_op jit(solution)/shard_map/reduce_scatter | solution.py:918
  337.4 5.0 %wide_step_kernel.1 = (f32[704,128]{1,0:T(8,128)}, f32[704,128]{1,0:T(8,128)}, f32[704,128]{1,0:T(8,128)}, f32[704,128]{1,0:T(8,128)}, f32[704,128]{1,0:T(8,128)...) custom-call(bf16[128,2304]{1,0:T(8,128)(2,1)} %reduce-scatter.2.clon, ...), custom_call_target="tpu_custom_call" | custom-call | bytes 6488064 | tf_op jit(solution)/shard_map/wide_step_kernel/pallas_call | solution.py:760
  342.4 3.6 query_step_kernel.1
  346.0 4.9 %all-to-all-start.2 = ((f32[8,16,256]{2,1,0:T(8,128)}), f32[8,16,256]{2,1,0:T(8,128)S(1)}, u32[]{:S(2)}, u32[]{:S(2)}) async-start(f32[8,16,256]{2,1,0:T(8,128)} %bitcast.55), calls=%async_computation.3 | async-start | bytes 262144 | tf_op jit(solution)/shard_map/all_to_all | solution.py:90
  352.1 4.1 %all-to-all-done.2.parts = f32[8,16,256]{2,1,0:T(8,128)S(1)} async-done(((f32[8,16,256]{2,1,0:T(8,128)}), f32[8,16,256]{2,1,0:T(8,128)S(1)}, u32[]{:S(2)}, u32[]{:S(2)}) %all-to-all-start.2) | async-done | bytes 131104 | tf_op jit(solution)/shard_map/all_to_all | solution.py:90
  (163 shorter events, 74.3 us)
Async XLA Ops:
  7.2 63.5 %all-gather.8.cloned.1.call-start = ((), (), s32[]{:S(2)}) async-start(), calls=%async_computation.6 | async-start | bytes 4718592 | tf_op jit(solution)/shard_map/all_gather | solution.py:875
  7.9 148.3 %all-gather.10.cloned.1.call-start = ((), (), s32[]{:S(2)}) async-start(), calls=%async_computation.7 | async-start | bytes 4718592 | tf_op jit(solution)/shard_map/all_gather | solution.py:876
  10.1 11.7 %all-to-all-start = ((bf16[8,16,256]{2,1,0:T(8,128)(2,1)}), bf16[8,16,256]{2,1,0:T(8,128)(2,1)S(1)}, u32[]{:S(2)}, u32[]{:S(2)}) async-start(bf16[8,16,256]{2,1,0:T(8,128)(2,1)} %bitcast.54), calls=%async_computation | async-start | bytes 131072 | tf_op jit(solution)/shard_map/all_to_all | solution.py:90
  17.0 140.9 %all-gather.6.cloned.1.call-start = ((), (), s32[]{:S(2)}) async-start(), calls=%async_computation.4 | async-start | bytes 10027008 | tf_op jit(solution)/shard_map/all_gather | solution.py:884
  38.6 298.7 %reduce-scatter.2.cloned.1.call-start = ((), (), s32[]{:S(2)}) async-start(), calls=%async_computation.5 | async-start | bytes 10027008 | tf_op jit(solution)/shard_map/reduce_scatter | solution.py:918
  38.7 16.3 %collective-permute-start.3 = (bf16[4,128,640]{2,1,0:T(8,128)(2,1)}, bf16[4,128,640]{2,1,0:T(8,128)(2,1)S(1)}, u32[]{:S(2)}, u32[]{:S(2)}) collective-permute-start(bf16[4,128,640]{2,1,0:T(8,128)(2,1)} %get-tuple-element.96.refs_0_), channel_id=1, source_target_pairs={{0,32},{32,64},{64,96},{96,0},{1,33},{33,65},{65,97},{97,1},{2,34}... | collective-permute-start | bytes 1966088 | tf_op jit(solution)/shard_map/ppermute | solution.py:86
  40.0 30.1 %collective-permute-start.4 = (bf16[4,128,640]{2,1,0:T(8,128)(2,1)}, bf16[4,128,640]{2,1,0:T(8,128)(2,1)S(1)}, u32[]{:S(2)}, u32[]{:S(2)}) collective-permute-start(bf16[4,128,640]{2,1,0:T(8,128)(2,1)} %get-tuple-element.96.refs_0_), channel_id=1, source_target_pairs={{0,64},{32,96},{64,0},{96,32},{1,65},{33,97},{65,1},{97,33},{2,66}... | collective-permute-start | bytes 1966088 | tf_op jit(solution)/shard_map/ppermute | solution.py:86
  42.7 28.0 %collective-permute-start.5 = (bf16[4,128,640]{2,1,0:T(8,128)(2,1)}, bf16[4,128,640]{2,1,0:T(8,128)(2,1)S(1)}, u32[]{:S(2)}, u32[]{:S(2)}) collective-permute-start(bf16[4,128,640]{2,1,0:T(8,128)(2,1)} %get-tuple-element.96.refs_0_), channel_id=1, source_target_pairs={{0,96},{32,0},{64,32},{96,64},{1,97},{33,1},{65,33},{97,65},{2,98}... | collective-permute-start | bytes 1966088 | tf_op jit(solution)/shard_map/ppermute | solution.py:86
  98.4 13.4 %collective-permute-start.7 = (bf16[128,2048]{1,0:T(8,128)(2,1)}, bf16[128,2048]{1,0:T(8,128)(2,1)S(1)}, u32[]{:S(2)}, u32[]{:S(2)}) collective-permute-start(bf16[128,2048]{1,0:T(8,128)(2,1)} %get-tuple-element.100), channel_id=1, source_target_pairs={{0,6},{2,0},{4,2},{6,4},{1,7},{3,1},{5,3},{7,5},{8,14},{10,8},{12,... | collective-permute-start | bytes 1572872 | tf_op jit(solution)/shard_map/ppermute | solution.py:890
  99.2 14.6 %collective-permute-start.8 = (bf16[128,2048]{1,0:T(8,128)(2,1)}, bf16[128,2048]{1,0:T(8,128)(2,1)S(1)}, u32[]{:S(2)}, u32[]{:S(2)}) collective-permute-start(bf16[128,2048]{1,0:T(8,128)(2,1)} %get-tuple-element.101), channel_id=1, source_target_pairs={{0,4},{2,6},{4,0},{6,2},{1,5},{3,7},{5,1},{7,3},{8,12},{10,14},{12... | collective-permute-start | bytes 1572872 | tf_op jit(solution)/shard_map/ppermute | solution.py:890
  100.4 25.6 %collective-permute-start.9 = (bf16[128,2048]{1,0:T(8,128)(2,1)}, bf16[128,2048]{1,0:T(8,128)(2,1)S(1)}, u32[]{:S(2)}, u32[]{:S(2)}) collective-permute-start(bf16[128,2048]{1,0:T(8,128)(2,1)} %get-tuple-element.102), channel_id=1, source_target_pairs={{0,2},{2,4},{4,6},{6,0},{1,3},{3,5},{5,7},{7,1},{8,10},{10,12},{12... | collective-permute-start | bytes 1572872 | tf_op jit(solution)/shard_map/ppermute | solution.py:890
  127.8 25.7 %collective-permute-start.10 = (bf16[128,2048]{1,0:T(8,128)(2,1)S(1)}, bf16[128,2048]{1,0:T(8,128)(2,1)S(1)}, u32[]{:S(2)}, u32[]{:S(2)}) collective-permute-start(bf16[128,2048]{1,0:T(8,128)(2,1)S(1)} %multiply_convert_fusion.refs_0_), channel_id=1, source_target_pairs={{0,2},{2,4},{4,6},{6,0},{1,3},{3,5},{5,7},{7,1},{8,10},{10,12},{12... | collective-permute-start | bytes 1572872 | tf_op jit(solution)/shard_map/ppermute | solution.py:77
  127.9 26.8 %collective-permute-start.11 = (bf16[128,2048]{1,0:T(8,128)(2,1)S(1)}, bf16[128,2048]{1,0:T(8,128)(2,1)S(1)}, u32[]{:S(2)}, u32[]{:S(2)}) collective-permute-start(bf16[128,2048]{1,0:T(8,128)(2,1)S(1)} %multiply_convert_fusion.refs_0_), channel_id=1, source_target_pairs={{0,4},{2,6},{4,0},{6,2},{1,5},{3,7},{5,1},{7,3},{8,12},{10,14},{12... | collective-permute-start | bytes 1572872 | tf_op jit(solution)/shard_map/ppermute | solution.py:77
  129.2 25.6 %collective-permute-start.12 = (bf16[128,2048]{1,0:T(8,128)(2,1)S(1)}, bf16[128,2048]{1,0:T(8,128)(2,1)S(1)}, u32[]{:S(2)}, u32[]{:S(2)}) collective-permute-start(bf16[128,2048]{1,0:T(8,128)(2,1)S(1)} %multiply_convert_fusion.refs_0_), channel_id=1, source_target_pairs={{0,6},{2,0},{4,2},{6,4},{1,7},{3,1},{5,3},{7,5},{8,14},{10,8},{12,... | collective-permute-start | bytes 1572872 | tf_op jit(solution)/shard_map/ppermute | solution.py:77
  131.2 25.1 %collective-permute-start.13 = (bf16[128,2048]{1,0:T(8,128)(2,1)S(1)}, bf16[128,2048]{1,0:T(8,128)(2,1)}, u32[]{:S(2)}, u32[]{:S(2)}) collective-permute-start(bf16[128,2048]{1,0:T(8,128)(2,1)S(1)} %multiply_convert_fusion.refs_0_), channel_id=1, source_target_pairs={{0,1},{1,0},{2,3},{3,2},{4,5},{5,4},{6,7},{7,6},{8,9},{9,8},{10,11... | collective-permute-start | bytes 1572872 | tf_op jit(solution)/shard_map/ppermute | solution.py:73
  194.6 27.7 %collective-permute-start.18 = (bf16[128,2048]{1,0:T(8,128)(2,1)}, bf16[128,2048]{1,0:T(8,128)(2,1)S(1)}, u32[]{:S(2)}, u32[]{:S(2)}) collective-permute-start(bf16[128,2048]{1,0:T(8,128)(2,1)} %get-tuple-element.108), channel_id=1, source_target_pairs={{0,6},{2,0},{4,2},{6,4},{1,7},{3,1},{5,3},{7,5},{8,14},{10,8},{12,... | collective-permute-start | bytes 1572872 | tf_op jit(solution)/shard_map/ppermute | solution.py:890
  196.5 25.8 %collective-permute-start.19 = (bf16[128,2048]{1,0:T(8,128)(2,1)}, bf16[128,2048]{1,0:T(8,128)(2,1)S(1)}, u32[]{:S(2)}, u32[]{:S(2)}) collective-permute-start(bf16[128,2048]{1,0:T(8,128)(2,1)} %get-tuple-element.109), channel_id=1, source_target_pairs={{0,4},{2,6},{4,0},{6,2},{1,5},{3,7},{5,1},{7,3},{8,12},{10,14},{12... | collective-permute-start | bytes 1572872 | tf_op jit(solution)/shard_map/ppermute | solution.py:890
  196.9 26.4 %collective-permute-start.20 = (bf16[128,2048]{1,0:T(8,128)(2,1)}, bf16[128,2048]{1,0:T(8,128)(2,1)S(1)}, u32[]{:S(2)}, u32[]{:S(2)}) collective-permute-start(bf16[128,2048]{1,0:T(8,128)(2,1)} %get-tuple-element.110), channel_id=1, source_target_pairs={{0,2},{2,4},{4,6},{6,0},{1,3},{3,5},{5,7},{7,1},{8,10},{10,12},{12... | collective-permute-start | bytes 1572872 | tf_op jit(solution)/shard_map/ppermute | solution.py:890
  228.5 15.2 %collective-permute-start.22 = (bf16[128,2048]{1,0:T(8,128)(2,1)S(1)}, bf16[128,2048]{1,0:T(8,128)(2,1)S(1)}, u32[]{:S(2)}, u32[]{:S(2)}) collective-permute-start(bf16[128,2048]{1,0:T(8,128)(2,1)S(1)} %copy-done.27), channel_id=1, source_target_pairs={{0,2},{2,4},{4,6},{6,0},{1,3},{3,5},{5,7},{7,1},{8,10},{10,12},{12... | collective-permute-start | bytes 1572872 | tf_op jit(solution)/shard_map/ppermute | solution.py:77
  229.5 25.9 %collective-permute-start.23 = (bf16[128,2048]{1,0:T(8,128)(2,1)S(1)}, bf16[128,2048]{1,0:T(8,128)(2,1)S(1)}, u32[]{:S(2)}, u32[]{:S(2)}) collective-permute-start(bf16[128,2048]{1,0:T(8,128)(2,1)S(1)} %copy-done.27), channel_id=1, source_target_pairs={{0,4},{2,6},{4,0},{6,2},{1,5},{3,7},{5,1},{7,3},{8,12},{10,14},{12... | collective-permute-start | bytes 1572872 | tf_op jit(solution)/shard_map/ppermute | solution.py:77
  231.2 24.3 %collective-permute-start.24 = (bf16[128,2048]{1,0:T(8,128)(2,1)S(1)}, bf16[128,2048]{1,0:T(8,128)(2,1)S(1)}, u32[]{:S(2)}, u32[]{:S(2)}) collective-permute-start(bf16[128,2048]{1,0:T(8,128)(2,1)S(1)} %copy-done.27), channel_id=1, source_target_pairs={{0,6},{2,0},{4,2},{6,4},{1,7},{3,1},{5,3},{7,5},{8,14},{10,8},{12,... | collective-permute-start | bytes 1572872 | tf_op jit(solution)/shard_map/ppermute | solution.py:77
  232.1 23.9 %collective-permute-start.25 = (bf16[128,2048]{1,0:T(8,128)(2,1)S(1)}, bf16[128,2048]{1,0:T(8,128)(2,1)S(1)}, u32[]{:S(2)}, u32[]{:S(2)}) collective-permute-start(bf16[128,2048]{1,0:T(8,128)(2,1)S(1)} %copy-done.27), channel_id=1, source_target_pairs={{0,1},{1,0},{2,3},{3,2},{4,5},{5,4},{6,7},{7,6},{8,9},{9,8},{10,11... | collective-permute-start | bytes 1572872 | tf_op jit(solution)/shard_map/ppermute | solution.py:73
  243.7 13.3 %collective-permute-start.26 = (bf16[128,2048]{1,0:T(8,128)(2,1)S(1)}, bf16[128,2048]{1,0:T(8,128)(2,1)S(1)}, u32[]{:S(2)}, u32[]{:S(2)}) collective-permute-start(bf16[128,2048]{1,0:T(8,128)(2,1)S(1)} %collective-permute-done.22.refs_1_), channel_id=1, source_target_pairs={{0,1},{1,0},{2,3},{3,2},{4,5},{5,4},{6,7},{7,6},{8,9},{9,8},{10,11... | collective-permute-start | bytes 1572872 | tf_op jit(solution)/shard_map/ppermute | solution.py:73
  280.2 13.9 %collective-permute-start.29 = (bf16[512,2048]{1,0:T(8,128)(2,1)}, bf16[512,2048]{1,0:T(8,128)(2,1)}, u32[]{:S(2)}, u32[]{:S(2)}) collective-permute-start(bf16[512,2048]{1,0:T(8,128)(2,1)} %get-tuple-element.125), channel_id=1, source_target_pairs={{0,1},{1,0},{2,3},{3,2},{4,5},{5,4},{6,7},{7,6},{8,9},{9,8},{10,11... | collective-permute-start | bytes 6291464 | tf_op jit(solution)/shard_map/ppermute | solution.py:73
  280.3 19.9 %collective-permute-start.21 = (bf16[512,2048]{1,0:T(8,128)(2,1)S(1)}, bf16[512,2048]{1,0:T(8,128)(2,1)}, u32[]{:S(2)}, u32[]{:S(2)}) collective-permute-start(bf16[512,2048]{1,0:T(8,128)(2,1)S(1)} %copy-done.4), channel_id=1, source_target_pairs={{0,1},{1,0},{2,3},{3,2},{4,5},{5,4},{6,7},{7,6},{8,9},{9,8},{10,11... | collective-permute-start | bytes 6291464 | tf_op jit(solution)/shard_map/ppermute | solution.py:73
  289.7 52.7 %all-to-all-start.1 = ((bf16[16,128,640]{2,1,0:T(8,128)(2,1)}), bf16[16,128,640]{2,1,0:T(8,128)(2,1)}, u32[]{:S(2)}, u32[]{:S(2)}) async-start(bf16[16,128,640]{2,1,0:T(8,128)(2,1)} %bitcast.36), calls=%async_computation.1 | async-start | bytes 5242880 | tf_op jit(solution)/shard_map/all_to_all | solution.py:90
  297.4 13.7 %collective-permute-start.30 = (bf16[128,2048]{1,0:T(8,128)(2,1)}, bf16[128,2048]{1,0:T(8,128)(2,1)S(1)}, u32[]{:S(2)}, u32[]{:S(2)}) collective-permute-start(bf16[128,2048]{1,0:T(8,128)(2,1)} %get-tuple-element.130), channel_id=1, source_target_pairs={{0,6},{2,0},{4,2},{6,4},{1,7},{3,1},{5,3},{7,5},{8,14},{10,8},{12,... | collective-permute-start | bytes 1572872 | tf_op jit(solution)/shard_map/ppermute | solution.py:890
  299.3 20.6 %collective-permute-start.34 = (bf16[128,2048]{1,0:T(8,128)(2,1)}, bf16[128,2048]{1,0:T(8,128)(2,1)S(1)}, u32[]{:S(2)}, u32[]{:S(2)}) collective-permute-start(bf16[128,2048]{1,0:T(8,128)(2,1)} %get-tuple-element.136), channel_id=1, source_target_pairs={{0,4},{2,6},{4,0},{6,2},{1,5},{3,7},{5,1},{7,3},{8,12},{10,14},{12... | collective-permute-start | bytes 1572872 | tf_op jit(solution)/shard_map/ppermute | solution.py:890
  300.2 27.0 %collective-permute-start.35 = (bf16[128,2048]{1,0:T(8,128)(2,1)}, bf16[128,2048]{1,0:T(8,128)(2,1)S(1)}, u32[]{:S(2)}, u32[]{:S(2)}) collective-permute-start(bf16[128,2048]{1,0:T(8,128)(2,1)} %get-tuple-element.137), channel_id=1, source_target_pairs={{0,2},{2,4},{4,6},{6,0},{1,3},{3,5},{5,7},{7,1},{8,10},{10,12},{12... | collective-permute-start | bytes 1572872 | tf_op jit(solution)/shard_map/ppermute | solution.py:890
  315.1 35.7 %collective-permute-start.31 = (bf16[128,2048]{1,0:T(8,128)(2,1)}, bf16[128,2048]{1,0:T(8,128)(2,1)S(1)}, u32[]{:S(2)}, u32[]{:S(2)}) collective-permute-start(bf16[128,2048]{1,0:T(8,128)(2,1)} %get-tuple-element.132), channel_id=1, source_target_pairs={{0,6},{2,0},{4,2},{6,4},{1,7},{3,1},{5,3},{7,5},{8,14},{10,8},{12,... | collective-permute-start | bytes 1572872 | tf_op jit(solution)/shard_map/ppermute | solution.py:890
  318.5 32.3 %collective-permute-start.32 = (bf16[128,2048]{1,0:T(8,128)(2,1)}, bf16[128,2048]{1,0:T(8,128)(2,1)S(1)}, u32[]{:S(2)}, u32[]{:S(2)}) collective-permute-start(bf16[128,2048]{1,0:T(8,128)(2,1)} %get-tuple-element.133), channel_id=1, source_target_pairs={{0,4},{2,6},{4,0},{6,2},{1,5},{3,7},{5,1},{7,3},{8,12},{10,14},{12... | collective-permute-start | bytes 1572872 | tf_op jit(solution)/shard_map/ppermute | solution.py:890
  318.6 32.3 %collective-permute-start.33 = (bf16[128,2048]{1,0:T(8,128)(2,1)}, bf16[128,2048]{1,0:T(8,128)(2,1)S(1)}, u32[]{:S(2)}, u32[]{:S(2)}) collective-permute-start(bf16[128,2048]{1,0:T(8,128)(2,1)} %get-tuple-element.134), channel_id=1, source_target_pairs={{0,2},{2,4},{4,6},{6,0},{1,3},{3,5},{5,7},{7,1},{8,10},{10,12},{12... | collective-permute-start | bytes 1572872 | tf_op jit(solution)/shard_map/ppermute | solution.py:890
  (46 other events, 343.0 us)
Sparse Core Ops, SparseCore 0:
  9.8 35.9 all-gather.7
  47.5 32.1 all-gather.9
  81.8 74.9 all-gather.5
  227.6 109.7 reduce-scatter.1
